TPU v7x, 32 devices: a whole 2x2x4 slice. The times are simulated.
32 devices in a mesh: gx: 16 (over z, y, core), gy: 2 (over x).
Axes of the slice: x: 2, y: 2, z: 4, core: 2. Of those that a mesh axis runs over, the one named last changes fastest.
Arguments:
- child_state: float32 [5, 32, 256, 256], P(None, None, 'gx', 'gy'), may hold values from -6 to 6
- cotangent: float32 [5, 32, 256, 256], P(None, None, 'gx', 'gy'), may hold values from -6 to 6
- diffusivity: float32 [32, 256, 256], P(None, 'gx', 'gy'), may hold values from 0.01 to 0.16
- field_mix: float32 [5, 5], replicated, may hold values from -2.5 to 2.5
- parent_we: float32 [2, 5, 128, 256], P(None, None, 'gx', 'gy'), may hold values from -6 to 6
- parent_sn: float32 [2, 5, 128, 256], P(None, None, 'gy', 'gx'), may hold values from -6 to 6
- terrain_we: int32 [2, 256], P(None, 'gy'), may hold values from 0 to 96, as said below
- terrain_sn: int32 [2, 256], P(None, 'gx'), may hold values from 0 to 96, as said below
- relax_width: int32 [1], replicated, may hold values from 4 to 15
Outputs:
- child_final: float32 [5, 32, 256, 256], P(None, None, 'gx', 'gy')
- grad_state: float32 [5, 32, 256, 256], P(None, None, 'gx', 'gy')
- grad_we: float32 [2, 5, 128, 256], P(None, None, 'gx', 'gy')
- grad_sn: float32 [2, 5, 128, 256], P(None, None, 'gy', 'gx')
Inputs may be any that keep to these rules, and one draw needn't show every extreme that they name: `terrain_we`: on each edge some column has the largest value 128 - 32. `terrain_sn`: on each edge some column has the largest value 128 - 32.
All inputs are finite; a program needn't handle non-finite values.
Results may differ from a plain program's by a relative error of at most 0.000084.
Values sent between devices are 32-bit elements; how exact they have to be, the bound alone decides.
No kernel may reach another device: no remote copies, remote signals or barrier semaphores. Data moves between devices by JAX's collectives and lax.ppermute only.
A program may use at most 128 MiB of HBM per device.

v0:
```python
import functools

import jax
import jax.numpy as jnp
from jax import lax
from jax.experimental import pallas as pl
from jax.experimental.pallas import tpu as pltpu
from jax.sharding import PartitionSpec as P

near = 4.0 / 3.0
far = -1.0 / 12.0
coupling = 0.25
highest = lax.Precision.HIGHEST
f32 = jnp.float32
places = {
    "v": pl.BlockSpec(memory_space=pltpu.VMEM),
    "s": pl.BlockSpec(memory_space=pltpu.SMEM),
    "h": pl.BlockSpec(memory_space=pltpu.HBM),
    "a": pl.BlockSpec(memory_space=pl.ANY),
}
widest_zone = 15


class Geometry:
    def __init__(self, child, nx, ny):
        self.F, self.K, self.X, self.Y = child
        self.nx, self.ny = nx, ny
        self.tiles = self.K // 8
        assert self.K % 8 == 0 and self.Y == 128 and 4 * self.X <= 64
        assert self.X > widest_zone and self.Y > widest_zone
        assert self.X == 16
        assert nx >= 4 and nx & (nx - 1) == 0 and ny % 2 == 0
        assert 4 * self.F <= 128
        self.pair = ny == 2
        self.tall = self.K + self.X + 8


def lanes():
    return lax.broadcasted_iota(jnp.int32, (8, 128), 1)


def turn(values, shift):
    return pltpu.roll(values, shift % 128, values.ndim - 1)


def ramp(position, length, width):
    distance = jnp.minimum(position, length - 1 - position)
    inside = (position >= 0) & (position < length)
    top = jnp.where(inside, jnp.maximum(width - distance, 0), 0)
    bottom = jnp.full((8, 128), width + 1, jnp.int32)
    return jnp.broadcast_to(top, (8, 128)).astype(f32) / bottom.astype(f32)


def ramp_y(g, width):
    return ramp(lax.axis_index("gy") * g.Y + lanes(), g.ny * g.Y, width)


def ramp_x(g, width, x):
    return ramp(lax.axis_index("gx") * g.X + x, g.nx * g.X, width)


def fill_ramp_x(g, width, ref):
    for x in range(g.X):
        ref[x] = ramp_x(g, width, x)


def lap_masks():
    lane = lanes()
    zero = jnp.zeros((8, 128), f32)
    return (
        (1, jnp.where(lane > 0, near, zero)),
        (-1, jnp.where(lane < 127, near, zero)),
        (2, jnp.where(lane > 1, far, zero)),
        (-2, jnp.where(lane < 126, far, zero)),
    )


def lap_inside(cells, x):
    beside = {
        1: [turn(cells[x], 1), turn(cells[x], -1)],
        2: [turn(cells[x], 2), turn(cells[x], -2)],
    }
    for step in (1, 2):
        beside[step] += [cells[x + i] for i in (-step, step) if 0 <= x + i < len(cells)]
    total = near * functools.reduce(jnp.add, beside[1]) - 5.0 * cells[x]
    return total + far * functools.reduce(jnp.add, beside[2])


def pack_lanes(x, base, values, packed):
    lane = lanes()
    start = base + 4 * x
    return jnp.where((lane >= start) & (lane < start + 4), turn(values, start + 2), packed)


def packed_message(packed):
    spot = lanes() % 4
    zero = jnp.zeros((8, 128), f32)
    low = far * turn(packed, -2) + jnp.where(spot == 1, near * turn(packed, -1), zero)
    high = far * turn(packed, 2) + jnp.where(spot == 2, near * turn(packed, 1), zero)
    return jnp.where(spot < 2, low, high)


def valid_lanes(g):
    at = lax.axis_index("gy")
    spot = lanes() % 4
    low = (at < g.ny - 1).astype(f32)
    high = (at > 0).astype(f32)
    return jnp.where(spot < 2, low, high)


def border():
    lane = lanes()
    return jnp.where((lane < 2) | (lane >= 126), 1.0, 0.0).astype(f32)


def unpack_lanes(x, base, packed, edge):
    return edge * turn(packed, -(base + 4 * x + 2))


def strided(ref, g, f, tile, x):
    start = (f * g.K + tile * 8) * g.X + x
    return ref.at[pl.ds(start, 8, stride=g.X), :]


def mix_table(mix, transposed):
    count = mix.shape[0]
    return [
        [
            (mix[h, f] if transposed else mix[f, h]) * coupling + (1.0 if f == h else 0.0)
            for h in range(count)
        ]
        for f in range(count)
    ]


def mixed(table, f, values):
    total = table[f][0] * values[0]
    for h in range(1, len(values)):
        total = total + table[f][h] * values[h]
    return total


def column_of(row):
    count = row.shape[1]
    wide = jnp.broadcast_to(row.astype(f32), (count, count))
    a = lax.broadcasted_iota(jnp.int32, (count, count), 0)
    b = lax.broadcasted_iota(jnp.int32, (count, count), 1)
    picked = jnp.sum(jnp.where(a == b, wide, 0.0), axis=1, keepdims=True)
    return jnp.broadcast_to(picked, (count, 128)).astype(jnp.int32)


def shift_levels(values, shift, sign):
    step = 1
    while step < 128:
        values = jnp.where((shift & step) != 0, turn(values, sign * step), values)
        step *= 2
    return values


def level_copies(g, pairs, sems, tile):
    levels = pl.ds(pl.multiple_of(tile * 8, 8), 8)
    copies = []
    for i, (source, target) in enumerate(pairs):
        at = (levels,) if len(source.shape) == 3 else (slice(None), levels)
        copies.append(pltpu.make_async_copy(source.at[at], target.at[at], sems.at[i, tile]))
    return copies


def rows_of(tile):
    return pl.ds(pl.multiple_of(tile * 8, 8), 8)


def odd_column():
    return lax.axis_index("gx") % 2 == 1


def send_ends(g, s, source, rows, ma, mb):
    odd = odd_column()
    for f in range(g.F):
        for j in range(2):
            low, high = source(f, j), source(f, g.X - 2 + j)
            ma[s, j, f, rows, :] = jnp.where(odd, low, high)
            mb[s, j, f, rows, :] = jnp.where(odd, high, low)


class Beyond:
    def __init__(self, g, s, fa, fb, fy, own):
        self.g, self.s, self.fa, self.fb, self.fy, self.own = g, s, fa, fb, fy, own
        self.edge = border()
        self.valid = valid_lanes(g)
        here = lax.axis_index("gx")
        self.odd = here % 2 == 1
        self.first, self.last = here == 0, here == g.nx - 1

    def left(self, j, f, rows):
        at = (self.s, j, f, rows, slice(None))
        value = jnp.where(self.odd, self.fa[at], self.fb[at])
        return jnp.where(self.first, jnp.zeros_like(value), value)

    def right(self, j, f, rows):
        at = (self.s, j, f, rows, slice(None))
        value = jnp.where(self.odd, self.fb[at], self.fa[at])
        return jnp.where(self.last, jnp.zeros_like(value), value)

    def lanes_of(self, f, rows):
        return self.fy[f, rows, :] * self.valid - self.own[f, rows, :]

    def add(self, f, x, rows, packed):
        s, last = self.s, self.g.X - 1
        total = unpack_lanes(x, 64 * s, packed, self.edge)
        if x == 0:
            total = total + near * self.left(1, f, rows) + far * self.left(0, f, rows)
        if x == 1:
            total = total + far * self.left(1, f, rows)
        if x == last - 1:
            total = total + far * self.right(0, f, rows)
        if x == last:
            total = total + near * self.right(0, f, rows) + far * self.right(1, f, rows)
        return total


def lane_sums(vectors):
    lane = lanes()
    step = 1
    while len(vectors) > 1:
        low = (lane & step) == 0
        merged = []
        for a, b in zip(vectors[::2], vectors[1::2]):
            merged.append(jnp.where(low, a, b) + turn(jnp.where(low, b, a), step))
        vectors = merged
        step *= 2
    total = vectors[0]
    while step < 128:
        total = total + turn(total, step)
        step *= 2
    return total


def pack_kernel(
    g, relax, child_far, cot_far, diff_far, sn_far, parent_far, terrain_far,
    ut, at, dt, qt, ma, mb, my, rx, child, cot, diff, sn, parent, terrain, sems, side_sems,
):
    width = relax[0]
    pairs = ((diff_far, diff), (child_far, child), (cot_far, cot))
    for tile in range(g.tiles):
        for copy in level_copies(g, pairs, sems, tile):
            copy.start()
    side_copies = [
        pltpu.make_async_copy(source, target, side_sems.at[i])
        for i, (source, target) in enumerate(
            ((sn_far, sn), (parent_far, parent), (terrain_far, terrain))
        )
    ]
    for copy in side_copies:
        copy.start()
    fill_ramp_x(g, width, rx)
    open_y = 1.0 - ramp_y(g, width)
    child2 = child.reshape(g.F * g.K * g.X, g.Y)
    cot2 = cot.reshape(g.F * g.K * g.X, g.Y)
    diff2 = diff.reshape(g.K * g.X, g.Y)

    def tile_step(tile, carry):
        for copy in level_copies(g, pairs, sems, tile):
            copy.wait()
        rows = rows_of(tile)
        packed = [jnp.zeros((8, 128), f32) for _ in range(g.F)]
        for x in range(g.X):
            d = strided(diff2, g, 0, tile, x)[...]
            dt[x, rows, :] = d
            open_xy = open_y * (1.0 - rx[x])
            for f in range(g.F):
                u = strided(child2, g, f, tile, x)[...]
                a = strided(cot2, g, f, tile, x)[...]
                q = d * (open_xy * a)
                ut[f, x, rows, :] = u
                at[f, x, rows, :] = a
                qt[f, x, rows, :] = q
                packed[f] = pack_lanes(x, 0, u, packed[f])
                packed[f] = pack_lanes(x, 64, q, packed[f])
        for f in range(g.F):
            my[f, rows, :] = packed_message(packed[f])
        for s, source in enumerate((ut, qt)):
            send_ends(g, s, lambda f, x: source[f, x, rows, :], rows, ma, mb)
        return carry

    lax.fori_loop(0, g.tiles, tile_step, 0)
    for copy in side_copies:
        copy.wait()
    for f in range(g.F):
        my[f, g.K :, :] = jnp.zeros((g.X + 8, 128), f32)
    if g.pair:
        other = 1 - lax.axis_index("gy")
        for f in range(g.F):
            my[f, g.K : g.K + g.X, : sn.shape[3]] = sn[other, f]
    span = parent.shape[2]
    lane = lax.broadcasted_iota(jnp.int32, (span, 128), 1)
    for f in range(g.F):
        total = jnp.zeros((span, 128), f32)
        for e in range(2):
            heights = jnp.broadcast_to(terrain[e : e + 1, :].astype(f32), (span, 128))
            for spot, values in ((e, parent[e, f]), (2 + e, heights)):
                here = (lane >= 4 * spot) & (lane < 4 * spot + 4)
                total = jnp.where(here, turn(values, 4 * spot + 2), total)
        my[f, g.K + g.X : g.K + g.X + span, :] = total


def adjoint_inside_kernel(g, scaled, relax, mix, ps, qs, gate, out, rx):
    width = relax[0]
    table = mix_table(mix, True)
    if scaled:
        fill_ramp_x(g, width, rx)
        open_y = 1.0 - ramp_y(g, width)

    def tile_step(tile, carry):
        rows = rows_of(tile)
        for x in range(g.X):
            p = [ps[f, x, rows, :] for f in range(g.F)]
            if scaled:
                open_xy = open_y * (1.0 - rx[x])
                p = [open_xy * value for value in p]
            for f in range(g.F):
                near_cells = Column(qs, f, rows, g.X)
                out[f, x, rows, :] = mixed(table, f, p) + lap_inside(near_cells, x)
        return carry

    lax.fori_loop(0, g.tiles, tile_step, 0)


class Column:
    def __init__(self, ref, f, rows, count):
        self.ref, self.f, self.rows, self.count = ref, f, rows, count

    def __len__(self):
        return self.count

    def __getitem__(self, x):
        return self.ref[self.f, x, self.rows, :]


def forward_inside_kernel(g, mix, ut, dt, gate, out):
    table = mix_table(mix, False)

    def tile_step(tile, carry):
        rows = rows_of(tile)
        for x in range(g.X):
            u = [ut[f, x, rows, :] for f in range(g.F)]
            d = dt[x, rows, :]
            for f in range(g.F):
                lap = lap_inside(Column(ut, f, rows, g.X), x)
                out[f, x, rows, :] = mixed(table, f, u) + d * lap
        return carry

    lax.fori_loop(0, g.tiles, tile_step, 0)


def adjoint_first_kernel(
    g, relax, inside, at, dt, fa, fb, fy, own, gate, p1, q1, ma, mb, my, dwe, dsn, rx
):
    width = relax[0]
    fill_ramp_x(g, width, rx)
    slope_y = ramp_y(g, width)
    open_y = 1.0 - slope_y
    beyond = Beyond(g, 1, fa, fb, fy, own)

    def tile_step(tile, carry):
        rows = rows_of(tile)
        for f in range(g.F):
            halo = beyond.lanes_of(f, rows)
            packed = jnp.zeros((8, 128), f32)
            share = jnp.zeros((8, 128), f32)
            pushes = []
            for x in range(g.X):
                slope_x = rx[x]
                open_xy = open_y * (1.0 - slope_x)
                middle = inside[f, x, rows, :] + beyond.add(f, x, rows, halo)
                carried = at[f, x, rows, :] + middle
                share = share + slope_x * carried
                pushes.append(slope_y * carried)
                pulled = open_xy * middle
                q = dt[x, rows, :] * pulled
                p1[f, x, rows, :] = pulled
                q1[f, x, rows, :] = q
                packed = pack_lanes(x, 64, q, packed)
            my[f, rows, :] = packed_message(packed)
            dsn[f, rows, :] = lane_sums(pushes)
            dwe[f, rows, :] = open_y * share
        send_ends(g, 1, lambda f, x: q1[f, x, rows, :], rows, ma, mb)
        return carry

    lax.fori_loop(0, g.tiles, tile_step, 0)
    for f in range(g.F):
        my[f, g.K :, :] = jnp.zeros((g.X + 8, 128), f32)


def forward_first_kernel(
    g, relax, inside, dt, fa, fb, fy, own, sides, gate, ma_in, mb_in, my_in, u1, ma, mb, my, rx
):
    width = relax[0]
    fill_ramp_x(g, width, rx)
    open_y = 1.0 - ramp_y(g, width)
    beyond = Beyond(g, 0, fa, fb, fy, own)
    lane = lanes()

    def tile_step(tile, carry):
        rows = rows_of(tile)
        for f in range(g.F):
            halo = beyond.lanes_of(f, rows)
            packed = jnp.zeros((8, 128), f32)
            for x in range(g.X):
                open_xy = open_y * (1.0 - rx[x])
                stepped = inside[f, x, rows, :] + dt[x, rows, :] * beyond.add(f, x, rows, halo)
                done = open_xy * stepped + sides[f, x, rows, :]
                u1[f, x, rows, :] = done
                packed = pack_lanes(x, 0, done, packed)
            my[f, rows, :] = jnp.where(lane < 64, packed_message(packed), my_in[f, rows, :])
        send_ends(g, 0, lambda f, x: u1[f, x, rows, :], rows, ma, mb)
        return carry

    lax.fori_loop(0, g.tiles, tile_step, 0)


def adjoint_last_kernel(g, inside, fa, fb, fy, own, gsn_own, gate, out, gsn):
    out2 = out.reshape(g.F * g.K * g.X, g.Y)
    beyond = Beyond(g, 1, fa, fb, fy, own)

    def tile_step(tile, carry):
        rows = rows_of(tile)
        for f in range(g.F):
            halo = beyond.lanes_of(f, rows)
            for x in range(g.X):
                value = inside[f, x, rows, :] + beyond.add(f, x, rows, halo)
                strided(out2, g, f, tile, x)[...] = value
        return carry

    lax.fori_loop(0, g.tiles, tile_step, 0)
    if g.pair:
        here = lax.axis_index("gy")
        span = gsn.shape[3]
        for f in range(g.F):
            gsn[here, f] = gsn_own[f, :, :span]
            gsn[1 - here, f] = fy[f, g.K : g.K + g.X, :span]
    else:
        gsn[...] = jnp.zeros(gsn.shape, f32)


def forward_last_kernel(
    g, relax, mix, inside, dt, fa, fb, fy, own, sides, kept, swapped, out, rx, lx
):
    width = relax[0]
    for x in range(-2, g.X + 2):
        rx[x + 2] = ramp_x(g, width, x)
    for x in range(g.X):
        lap_x = near * (rx[x + 1] + rx[x + 3]) + far * (rx[x] + rx[x + 4]) - 5.0 * rx[x + 2]
        lx[x] = lap_x
    open_y = 1.0 - ramp_y(g, width)
    masks = lap_masks()
    table = mix_table(mix, False)
    beyond = Beyond(g, 0, fa, fb, fy, own)
    out2 = out.reshape(g.F * g.K * g.X, g.Y)

    def tile_step(tile, carry):
        rows = rows_of(tile)
        bound = [
            open_y * (kept[g.F + f, rows, :] + swapped[g.F + f, rows, :]) for f in range(g.F)
        ]
        past = packed_message(kept[2 * g.F, rows, :] + swapped[2 * g.F, rows, :]) * beyond.valid
        for f in range(g.F):
            lap_y = unpack_lanes(f, 0, past, beyond.edge)
            for shift, mask in masks:
                lap_y = lap_y + mask * turn(bound[f], shift)
            mixed_bound = mixed(table, f, bound)
            halo = beyond.lanes_of(f, rows)
            for x in range(g.X):
                slope_x = rx[x + 2]
                open_xy = open_y * (1.0 - slope_x)
                lap = beyond.add(f, x, rows, halo) + slope_x * lap_y + lx[x] * bound[f]
                stepped = inside[f, x, rows, :] + slope_x * mixed_bound + dt[x, rows, :] * lap
                done = open_xy * stepped + slope_x * bound[f] + sides[f, x, rows, :]
                strided(out2, g, f, tile, x)[...] = done
        return carry

    lax.fori_loop(0, g.tiles, tile_step, 0)


def side_sums_kernel(g, dsn, tsn, my_in, gsn, my, wide):
    here = lax.axis_index("gy")
    shift = column_of(jnp.where(here == 0, tsn[0:1, :], tsn[1:2, :]))
    wide[...] = jnp.zeros(wide.shape, f32)
    for f in range(g.F):
        wide[f, : g.K, :] = dsn[f]
        whole = shift_levels(wide[f].T[: g.X], shift, 1)
        moved = turn(whole, 64)
        gsn[f] = jnp.where(here == 0, whole, moved)
        my[f, g.K : g.K + g.X, :] = jnp.where(here == 0, moved, whole)


def side_bounds_kernel(g, sn, fsn, tsn, gate, bsn, wide):
    here = lax.axis_index("gy")
    shift = column_of(jnp.where(here == 0, tsn[0:1, :], tsn[1:2, :]))
    span = sn.shape[3]
    wide[...] = jnp.zeros(wide.shape, f32)
    for f in range(g.F):
        wide[f, : g.X, :span] = sn[here, f]
        mine = wide[f, : g.X, :]
        theirs = fsn[f, g.K : g.K + g.X, :]
        whole = jnp.where(here == 0, mine, theirs) + turn(
            jnp.where(here == 0, theirs, mine), 64
        )
        wide[f, : g.X, :] = shift_levels(whole, shift, -1)
        bsn[f] = wide[f].T[: g.K]


def side_spread_kernel(g, relax, bsn, out):
    slope_y = ramp_y(g, relax[0])

    def tile_step(tile, carry):
        rows = rows_of(tile)
        for f in range(g.F):
            bounds = bsn[f, rows, :]
            for x in range(g.X):
                out[f, x, rows, :] = slope_y * jnp.broadcast_to(bounds[:, x : x + 1], (8, 128))
        return carry

    lax.fori_loop(0, g.tiles, tile_step, 0)


def fold_rows(values, base, first, count):
    level = lax.broadcasted_iota(jnp.int32, (count, 128), 0) + base - first
    total = jnp.zeros((count, 128), f32)
    for j in range(values.shape[0]):
        row = jnp.broadcast_to(values[j : j + 1, :], (count, 128))
        total = jnp.where(level == j, row, total)
    return total


def fold_kernel(g, parent, terrain, fy, keep, send):
    here = lax.axis_index("gx")
    odd = here >= g.nx // 2
    span = parent.shape[2]
    first = here * span
    lane = lax.broadcasted_iota(jnp.int32, (span, 128), 1)
    top = g.K + g.X
    parts = []
    for e in range(2):
        part = [fold_rows(parent[e, f], terrain[e : e + 1, :], first, g.K) for f in range(g.F)]
        values = jnp.zeros((span, 128), f32)
        heights = jnp.zeros((span, 128), f32)
        for f in range(g.F):
            spots = (lane >= 4 * f) & (lane < 4 * f + 4)
            rows = fy[f, top : top + span, :]
            values = jnp.where(spots, turn(rows, 4 * f - 4 * e), values)
            heights = jnp.where(spots, turn(rows, 4 * f - 8 - 4 * e), heights)
        part.append(fold_rows(values, heights[0:1, :].astype(jnp.int32), first, g.K))
        parts.append(part)
    for i in range(g.F + 1):
        keep[i] = jnp.where(odd, parts[1][i], parts[0][i])
        send[i] = jnp.where(odd, parts[0][i], parts[1][i])


def join_kernel(g, sums, bounds, more_bounds, out):
    for f in range(g.F):
        out[f] = sums[f]
    for f in range(g.F + 1):
        out[g.F + f] = bounds[f] + more_bounds[f]


def split_kernel(g, state, moved, out, sums):
    for f in range(2 * g.F + 1):
        total = state[f] + moved[f]
        out[f] = total
        if f < g.F:
            sums[f] = total


def finish_kernel(g, state, moved, out):
    for f in range(g.F):
        out[f] = state[f] + moved[f]
    for f in range(g.F, 2 * g.F + 1):
        out[f] = state[f]


def spread_kernel(g, kept, swapped, terrain, out):
    here = lax.axis_index("gx")
    odd = here % 2
    span = out.shape[2]
    for e in range(2):
        place = lax.broadcasted_iota(jnp.int32, (span, 128), 0) + here * span - terrain[e : e + 1, :]
        keep = [place == k for k in range(g.K)]
        for f in range(g.F):
            a, b = kept[f], swapped[f]
            chosen = jnp.where(odd == e, a, b)
            total = jnp.zeros((span, 128), f32)
            for k in range(g.K):
                row = jnp.broadcast_to(chosen[k : k + 1, :], (span, 128))
                total = jnp.where(keep[k], row, total)
            out[e, f] = total


def call(kernel, outs, scratch, ins, time, aliases=None):
    out_shape = [jax.ShapeDtypeStruct(s, f32) for s in outs]
    size = 4 * sum(functools.reduce(lambda a, b: a * b, s) for s in outs)
    return pl.pallas_call(
        kernel,
        out_shape=out_shape,
        in_specs=[places[where] for where, _ in ins],
        out_specs=[places["v"]] * len(outs),
        scratch_shapes=[pltpu.VMEM(s, f32) if isinstance(s, tuple) else s for s in scratch],
        input_output_aliases=aliases or {},
        compiler_params=pltpu.CompilerParams(vmem_limit_bytes=24 * 1024 * 1024),
        cost_estimate=pl.CostEstimate(flops=int(time * 1.1e9), bytes_accessed=2 * size, transcendentals=0),
    )(*[pltpu.with_memory_space_constraint(v, pltpu.HBM) if w == "h" else v for w, v in ins])


def body(
    child_state,
    cotangent,
    diffusivity,
    field_mix,
    parent_we,
    parent_sn,
    terrain_we,
    terrain_sn,
    relax_width,
):
    nx, ny = lax.axis_size("gx"), lax.axis_size("gy")
    g = Geometry(child_state.shape, nx, ny)
    F, K, X, Y = child_state.shape
    evens = [(i, i ^ 1) for i in range(nx)]
    odds = [(i, (((i + 1) ^ 1) - 1) % nx) for i in range(nx)]
    block = (F, X, K, 128)
    row_shape = (2, 2, F, K, 128)
    lane_shape = (F, g.tall, 128)
    edge_shape = (F, K, 128)
    ramps = (X, 8, 128)

    def bind(kernel, *args):
        return functools.partial(kernel, g, *args)

    def swapped(values, distance):
        return lax.ppermute(values, "gx", [(i, i ^ distance) for i in range(nx)])

    def to_y(message):
        if g.pair:
            return lax.ppermute(message, "gy", [(0, 1), (1, 0)])
        up = lax.ppermute(message, "gy", [(i, i + 1) for i in range(ny - 1)])
        down = lax.ppermute(message, "gy", [(i + 1, i) for i in range(ny - 1)])
        low = (jnp.arange(128, dtype=jnp.int32) % 4 < 2)[None, None, :]
        rows = (jnp.arange(g.tall, dtype=jnp.int32) < K)[None, :, None]
        return jnp.where(low == rows, down, up)

    sn_turned = jnp.swapaxes(parent_sn, 2, 3)
    ut, at, dt, qt, ma, mb, my = call(
        bind(pack_kernel),
        [block, block, (X, K, 128), block, row_shape, row_shape, lane_shape],
        [
            ramps,
            child_state.shape,
            child_state.shape,
            diffusivity.shape,
            sn_turned.shape,
            parent_we.shape,
            pltpu.VMEM(terrain_we.shape, jnp.int32),
            pltpu.SemaphoreType.DMA((3, g.tiles)),
            pltpu.SemaphoreType.DMA((3,)),
        ],
        [
            ("s", relax_width),
            ("h", child_state),
            ("h", cotangent),
            ("h", diffusivity),
            ("h", sn_turned),
            ("h", parent_we),
            ("h", terrain_we),
        ],
        3,
    )
    own = my
    fy = to_y(my)
    fa = lax.ppermute(ma, "gx", evens)
    fb = lax.ppermute(mb, "gx", odds)

    (inside_a,) = call(
        bind(adjoint_inside_kernel, True),
        [block],
        [ramps],
        [("s", relax_width), ("s", field_mix), ("v", at), ("v", qt), ("a", dt)],
        2.5,
    )
    (inside_u,) = call(
        bind(forward_inside_kernel),
        [block],
        [],
        [("s", field_mix), ("v", ut), ("v", dt), ("a", inside_a)],
        2.5,
    )
    keep, send = call(
        bind(fold_kernel),
        [(F + 1, K, 128)] * 2,
        [],
        [("v", parent_we), ("v", terrain_we), ("v", fy)],
        0.3,
    )
    first_bounds = swapped(send, nx // 2)
    p1, q1, ma, mb, my, dwe, dsn = call(
        bind(adjoint_first_kernel),
        [block, block, row_shape, row_shape, lane_shape, edge_shape, edge_shape],
        [ramps],
        [
            ("s", relax_width),
            ("v", inside_a),
            ("v", at),
            ("v", dt),
            ("v", fa),
            ("v", fb),
            ("v", fy),
            ("v", own),
            ("a", keep),
        ],
        3,
    )
    if g.pair:
        (bsn,) = call(
            bind(side_bounds_kernel),
            [edge_shape],
            [(F, 128, 128)],
            [("v", sn_turned), ("v", fy), ("v", terrain_sn), ("a", dwe)],
            0.7,
        )
    else:
        bsn = bound_sn_general(g, parent_sn, terrain_sn)
    (sides,) = call(
        bind(side_spread_kernel), [block], [], [("s", relax_width), ("v", bsn)], 0.7
    )
    state_shape = (2 * F + 1, K, 128)
    (state,) = call(
        bind(join_kernel),
        [state_shape],
        [],
        [("v", dwe), ("v", keep), ("v", first_bounds)],
        0.1,
    )
    gates = []
    distance = 2
    while distance < nx // 4:
        state = state + swapped(state, distance)
        gates.append(state)
        distance *= 2
    moved = swapped(state, distance) if distance < nx // 2 else jnp.zeros_like(state)
    state, sums = call(
        bind(split_kernel), [state_shape, edge_shape], [], [("v", state), ("v", moved)], 0.1
    )
    gates.append(state)
    (state,) = call(
        bind(finish_kernel), [state_shape], [], [("v", state), ("v", swapped(sums, nx // 2))], 0.1
    )
    other = swapped(state, 1)

    if g.pair:
        gsn_own, my = call(
            bind(side_sums_kernel),
            [(F, X, 128), lane_shape],
            [(F, 128, 128)],
            [("v", dsn), ("v", terrain_sn), ("v", my)],
            0.6,
            {2: 1},
        )
    else:
        gsn_own = dsn
    u1, ma, mb, my = call(
        bind(forward_first_kernel),
        [block, row_shape, row_shape, lane_shape],
        [ramps],
        [
            ("s", relax_width),
            ("v", inside_u),
            ("v", dt),
            ("v", fa),
            ("v", fb),
            ("v", fy),
            ("v", own),
            ("v", sides),
            ("a", gates[0]),
            ("v", ma),
            ("v", mb),
            ("v", my),
        ],
        2.5,
        {9: 1, 10: 2, 11: 3},
    )
    own = my
    fy = to_y(my)
    fa = lax.ppermute(ma, "gx", evens)
    fb = lax.ppermute(mb, "gx", odds)

    (inside_a,) = call(
        bind(adjoint_inside_kernel, False),
        [block],
        [ramps],
        [("s", relax_width), ("s", field_mix), ("v", p1), ("v", q1), ("a", gates[-1])],
        2.5,
    )
    (inside_u,) = call(
        bind(forward_inside_kernel),
        [block],
        [],
        [("s", field_mix), ("v", u1), ("v", dt), ("a", u1)],
        2.5,
    )
    grad_state, grad_sn = call(
        bind(adjoint_last_kernel),
        [child_state.shape, sn_turned.shape],
        [],
        [("v", inside_a), ("v", fa), ("v", fb), ("v", fy), ("v", own), ("v", gsn_own), ("a", state)],
        2.5,
    )
    (child_final,) = call(
        bind(forward_last_kernel),
        [child_state.shape],
        [(X + 4, 8, 128), ramps],
        [
            ("s", relax_width),
            ("s", field_mix),
            ("v", inside_u),
            ("v", dt),
            ("v", fa),
            ("v", fb),
            ("v", fy),
            ("v", own),
            ("v", sides),
            ("v", state),
            ("v", other),
        ],
        3,
    )
    (grad_we,) = call(
        bind(spread_kernel),
        [parent_we.shape],
        [],
        [("v", state), ("v", other), ("v", terrain_we)],
        0.7,
    )
    if g.pair:
        grad_sn = jnp.swapaxes(grad_sn, 2, 3)
    else:
        grad_sn = grad_sn_general(g, gsn_own, terrain_sn, parent_sn.shape[2])
    return (child_final, grad_state, grad_we, grad_sn)


def level_weights(g, terrain, span):
    first = lax.axis_index("gy") * span
    base = terrain[:, None, :] + jnp.arange(g.K, dtype=jnp.int32)[None, :, None]
    parent = first + jnp.arange(span, dtype=jnp.int32)
    return (parent[None, None, :, None] == base[:, :, None, :]).astype(f32)


def bound_sn_general(g, parent_sn, terrain_sn):
    weights = level_weights(g, terrain_sn, parent_sn.shape[2])
    bound = jnp.einsum("eflc,eklc->efkc", parent_sn, weights, precision=highest)
    bound = lax.psum(bound, "gy")
    mine = jnp.where(lax.axis_index("gy") < g.ny // 2, bound[0], bound[1])
    return jnp.pad(mine, ((0, 0), (0, 0), (0, 128 - g.X)))


def grad_sn_general(g, sums, terrain_sn, span):
    sums = sums[:, :, : g.X]
    south = lax.axis_index("gy") < g.ny // 2
    zero = jnp.zeros_like(sums)
    both = jnp.stack([jnp.where(south, sums, zero), jnp.where(south, zero, sums)])
    both = lax.psum(both, "gy")
    weights = level_weights(g, terrain_sn, span)
    return jnp.einsum("efkc,eklc->eflc", both, weights, precision=highest)


def solution(mesh):
    return jax.shard_map(
        body,
        mesh=mesh,
        in_specs=(
            P(None, None, "gx", "gy"),
            P(None, None, "gx", "gy"),
            P(None, "gx", "gy"),
            P(),
            P(None, None, "gx", "gy"),
            P(None, None, "gy", "gx"),
            P(None, "gy"),
            P(None, "gx"),
            P(),
        ),
        out_specs=(
            P(None, None, "gx", "gy"),
            P(None, None, "gx", "gy"),
            P(None, None, "gx", "gy"),
            P(None, None, "gy", "gx"),
        ),
        check_vma=False,
    )
```

profile of v0, /device:TPU:0, one launch (start us, length us, event | category | flops | bytes accessed | tf_op | source)
XLA Modules:
  0.0 49.2 jit_solution(2706407900523768318)
XLA Ops:
  1.3 3.1 %shard_map.120 = (f32[5,16,32,128]{3,2,1,0:T(8,128)S(1)}, f32[5,16,32,128]{3,2,1,0:T(8,128)S(1)}, f32[16,32,128]{2,1,0:T(8,128)S(1)}, f32[5,16,32,128]{3,2,1,0:T...) custom-call(s32[1]{0:T(128)S(6)} %copy.21.relax, ...), custom_call_target="tpu_custom_call" | custom-call | flops 3300000000 | bytes 9986048 | tf_op jit(solution)/shard_map/pallas_call | solution.py:602
  4.4 3.0 %collective-permute-start.2 = (f32[5,56,128]{2,1,0:T(8,128)S(1)}, f32[5,56,128]{2,1,0:T(8,128)S(1)}, u32[]{:S(2)}, u32[]{:S(2)}) collective-permute-start(f32[5,56,128]{2,1,0:T(8,128)S(1)} %get-tuple-element.36.own), channel_id=1, source_target_pairs={{0,1},{1,0},{2,3},{3,2},{4,5},{5,4},{6,7},{7,6},{8,9},{9,8},{10,11... | collective-permute-start | bytes 430088 | tf_op jit(solution)/shard_map/ppermute | solution.py:644
  7.4 0.0 collective-permute-start
  7.4 4.7 %collective-permute-start.1 = (f32[2,2,5,32,128]{4,3,2,1,0:T(8,128)S(1)}, f32[2,2,5,32,128]{4,3,2,1,0:T(8,128)S(1)}, u32[]{:S(2)}, u32[]{:S(2)}) collective-permute-start(f32[2,2,5,32,128]{4,3,2,1,0:T(8,128)S(1)} %get-tuple-element.35), channel_id=1, source_target_pairs={{0,30},{2,4},{4,2},{6,8},{8,6},{10,12},{12,10},{14,16},{16,14},{18... | collective-permute-start | bytes 983048 | tf_op jit(solution)/shard_map/ppermute | solution.py:680
  12.1 2.3 %shard_map.121.gate.inside = f32[5,16,32,128]{3,2,1,0:T(8,128)S(1)} custom-call(s32[1]{0:T(128)S(6)} %copy.21.relax, f32[5,5]{1,0:T(8,128)S(1)} %copy-done.2, f32[5,16,32,128]{3,2,1,0:T(8,128)S(1)} %get-tuple-element.32.ps.at, f32[5,16,32,128]{3,2,1,0:T(8,128)S(1)} %get-tuple-element.33.qs, f32[16,32,128]{2,1,0:T(8,128)S(1)} %get-tuple-element.31.gate.dt), custom_call_target="tpu_custom_call" | custom-call | flops 2750000128 | bytes 2621440 | tf_op jit(solution)/shard_map/pallas_call | solution.py:602
  14.4 0.0 copy-start.1
  14.5 0.0 copy-start.4
  14.5 2.3 %shard_map.122.inside = f32[5,16,32,128]{3,2,1,0:T(8,128)S(1)} custom-call(f32[5,5]{1,0:T(8,128)S(1)} %copy-done.2, f32[5,16,32,128]{3,2,1,0:T(8,128)S(1)} %get-tuple-element.30.ut, f32[16,32,128]{2,1,0:T(8,128)S(1)} %get-tuple-element.31.gate.dt, f32[5,16,32,128]{3,2,1,0:T(8,128)S(1)} %shard_map.121.gate.inside), custom_call_target="tpu_custom_call" | custom-call | flops 2750000128 | bytes 2621440 | tf_op jit(solution)/shard_map/pallas_call | solution.py:602
  16.8 0.1 shard_map.123
  16.9 0.1 collective-permute-start.3
  17.0 0.0 copy-start.3
  17.0 3.0 %shard_map.124 = (f32[5,16,32,128]{3,2,1,0:T(8,128)S(1)}, f32[5,16,32,128]{3,2,1,0:T(8,128)S(1)}, f32[2,2,5,32,128]{4,3,2,1,0:T(8,128)S(1)}, f32[2,2,5,32,128]{4...) custom-call(s32[1]{0:T(128)S(6)} %copy.21.relax, ...), custom_call_target="tpu_custom_call" | custom-call | flops 3300000000 | bytes 7168000 | tf_op jit(solution)/shard_map/pallas_call | solution.py:602
  20.0 2.5 %collective-permute-done.3.more_bounds = f32[6,32,128]{2,1,0:T(8,128)S(1)} collective-permute-done((f32[6,32,128]{2,1,0:T(8,128)S(1)}, f32[6,32,128]{2,1,0:T(8,128)S(1)}, u32[]{:S(2)}, u32[]{:S(2)}) %collective-permute-start.3) | collective-permute-done | bytes 98336 | tf_op jit(solution)/shard_map/ppermute | solution.py:640
  22.5 0.0 copy-start
  22.5 0.6 %collective-permute-start.4 = (f32[11,32,128]{2,1,0:T(8,128)S(1)}, f32[11,32,128]{2,1,0:T(8,128)S(1)}, u32[]{:S(2)}, u32[]{:S(2)}) collective-permute-start(f32[11,32,128]{2,1,0:T(8,128)S(1)} %shard_map.127), channel_id=1, source_target_pairs={{0,4},{2,6},{4,0},{6,2},{8,12},{10,14},{12,8},{14,10},{16,20},{18,... | collective-permute-start | bytes 540680 | tf_op jit(solution)/shard_map/ppermute | solution.py:640
  23.2 0.6 %shard_map.128 = (f32[5,16,128]{2,1,0:T(8,128)S(1)}, f32[5,56,128]{2,1,0:T(8,128)S(1)}) custom-call(f32[5,32,128]{2,1,0:T(8,128)S(1)} %get-tuple-element.42.dsn, s32[2,16]{1,0:T(2,128)S(1)} %copy-done.3, f32[5,56,128]{2,1,0:T(8,128)S(1)} %get-tuple-element.43.my_in), custom_call_target="tpu_custom_call", output_to_operand_aliasing={{1}: (2, {})} | custom-call | flops 660000000 | bytes 368640 | tf_op jit(solution)/shard_map/pallas_call | solution.py:602
  23.8 0.7 %shard_map.125.bsn = f32[5,32,128]{2,1,0:T(8,128)S(1)} custom-call(f32[2,5,16,64]{3,2,1,0:T(8,128)S(1)} %bitcast.3, f32[5,56,128]{2,1,0:T(8,128)S(1)} %collective-permute-done.2.fy.fsn, s32[2,16]{1,0:T(2,128)S(1)} %copy-done.3, f32[5,32,128]{2,1,0:T(8,128)S(1)} %get-tuple-element.38.gate.sums), custom_call_target="tpu_custom_call" | custom-call | flops 770000000 | bytes 163840 | tf_op jit(solution)/shard_map/pallas_call | solution.py:602
  24.5 0.9 %shard_map.126.sides = f32[5,16,32,128]{3,2,1,0:T(8,128)S(1)} custom-call(s32[1]{0:T(128)S(6)} %copy.21.relax, f32[5,32,128]{2,1,0:T(8,128)S(1)} %shard_map.125.bsn), custom_call_target="tpu_custom_call" | custom-call | flops 770000000 | bytes 2621440 | tf_op jit(solution)/shard_map/pallas_call | solution.py:602
  25.4 2.7 %collective-permute-done.4 = f32[11,32,128]{2,1,0:T(8,128)S(1)} collective-permute-done((f32[11,32,128]{2,1,0:T(8,128)S(1)}, f32[11,32,128]{2,1,0:T(8,128)S(1)}, u32[]{:S(2)}, u32[]{:S(2)}) %collective-permute-start.4) | collective-permute-done | bytes 180256 | tf_op jit(solution)/shard_map/ppermute | solution.py:640
  28.1 1.1 %collective-permute-start.8 = (f32[11,32,128]{2,1,0:T(8,128)S(1)}, f32[11,32,128]{2,1,0:T(8,128)S(1)}, u32[]{:S(2)}, u32[]{:S(2)}) collective-permute-start(f32[11,32,128]{2,1,0:T(8,128)S(1)} %add.3.gate.state), channel_id=1, source_target_pairs={{0,8},{2,10},{4,12},{6,14},{8,0},{10,2},{12,4},{14,6},{16,24},{18,... | collective-permute-start | bytes 540680 | tf_op jit(solution)/shard_map/ppermute | solution.py:640
  29.2 1.6 %shard_map.129 = (f32[5,16,32,128]{3,2,1,0:T(8,128)S(1)}, f32[2,2,5,32,128]{4,3,2,1,0:T(8,128)S(1)}, f32[2,2,5,32,128]{4,3,2,1,0:T(8,128)S(1)}, f32[5,56,128]{2,1,0:T(8,128)S(1)}) custom-call(s32[1]{0:T(128)S(6)} %copy.21.relax, f32[5,16,32,128]{3,2,1,0:T(8,128)S(1)} %shard_map.122.inside, ...), custom_call_target="tpu_custom_call", output_to_operand_aliasing={{1}: (9, {}), {2}: (10, {}), {3}: (11, {})} | custom-call | flops 2750000128 | bytes 4218880 | tf_op jit(solution)/shard_map/pallas_call | solution.py:602
  30.8 0.1 collective-permute-start.5
  30.9 2.5 %collective-permute-start.6 = (f32[2,2,5,32,128]{4,3,2,1,0:T(8,128)S(1)}, f32[2,2,5,32,128]{4,3,2,1,0:T(8,128)S(1)}, u32[]{:S(2)}, u32[]{:S(2)}) collective-permute-start(f32[2,2,5,32,128]{4,3,2,1,0:T(8,128)S(1)} %get-tuple-element.47), channel_id=1, source_target_pairs={{0,30},{2,4},{4,2},{6,8},{8,6},{10,12},{12,10},{14,16},{16,14},{18... | collective-permute-start | bytes 983048 | tf_op jit(solution)/shard_map/ppermute | solution.py:793
  33.5 2.3 %shard_map.130.inside = f32[5,16,32,128]{3,2,1,0:T(8,128)S(1)} custom-call(f32[5,5]{1,0:T(8,128)S(1)} %copy-done.2, f32[5,16,32,128]{3,2,1,0:T(8,128)S(1)} %get-tuple-element.45.ut.gate, f32[16,32,128]{2,1,0:T(8,128)S(1)} %get-tuple-element.31.gate.dt, f32[5,16,32,128]{3,2,1,0:T(8,128)S(1)} %get-tuple-element.45.ut.gate), custom_call_target="tpu_custom_call" | custom-call | flops 2750000128 | bytes 2621440 | tf_op jit(solution)/shard_map/pallas_call | solution.py:602
  35.7 0.6 %collective-permute-start.7 = (f32[5,56,128]{2,1,0:T(8,128)S(1)}, f32[5,56,128]{2,1,0:T(8,128)S(1)}, u32[]{:S(2)}, u32[]{:S(2)}) collective-permute-start(f32[5,56,128]{2,1,0:T(8,128)S(1)} %get-tuple-element.48.own), channel_id=1, source_target_pairs={{0,1},{1,0},{2,3},{3,2},{4,5},{5,4},{6,7},{7,6},{8,9},{9,8},{10,11... | collective-permute-start | bytes 430088 | tf_op jit(solution)/shard_map/ppermute | solution.py:644
  36.4 0.9 %collective-permute-start.9 = (f32[5,32,128]{2,1,0:T(8,128)S(1)}, f32[5,32,128]{2,1,0:T(8,128)S(1)}, u32[]{:S(2)}, u32[]{:S(2)}) collective-permute-start(f32[5,32,128]{2,1,0:T(8,128)S(1)} %get-tuple-element.50), channel_id=1, source_target_pairs={{0,16},{2,18},{4,20},{6,22},{8,24},{10,26},{12,28},{14,30},{16,0},... | collective-permute-start | bytes 245768 | tf_op jit(solution)/shard_map/ppermute | solution.py:640
  37.2 2.3 %shard_map.134.inside = f32[5,16,32,128]{3,2,1,0:T(8,128)S(1)} custom-call(s32[1]{0:T(128)S(6)} %copy.21.relax, f32[5,5]{1,0:T(8,128)S(1)} %copy-done.2, f32[5,16,32,128]{3,2,1,0:T(8,128)S(1)} %get-tuple-element.51.ps, f32[5,16,32,128]{3,2,1,0:T(8,128)S(1)} %get-tuple-element.52.qs, f32[11,32,128]{2,1,0:T(8,128)S(1)} %get-tuple-element.49.state.gate), custom_call_target="tpu_custom_call" | custom-call | flops 2750000128 | bytes 2621440 | tf_op jit(solution)/shard_map/pallas_call | solution.py:602
  39.5 3.7 %collective-permute-done.9.moved = f32[5,32,128]{2,1,0:T(8,128)S(1)} collective-permute-done((f32[5,32,128]{2,1,0:T(8,128)S(1)}, f32[5,32,128]{2,1,0:T(8,128)S(1)}, u32[]{:S(2)}, u32[]{:S(2)}) %collective-permute-start.9) | collective-permute-done | bytes 81952 | tf_op jit(solution)/shard_map/ppermute | solution.py:640
  43.2 0.1 collective-permute-start.10
  43.3 1.8 %shard_map.135 = (f32[5,32,16,128]{3,2,1,0:T(8,128)}, f32[2,5,16,64]{3,2,1,0:T(8,128)}) custom-call(f32[5,16,32,128]{3,2,1,0:T(8,128)S(1)} %shard_map.134.inside, f32[2,2,5,32,128]{4,3,2,1,0:T(8,128)S(1)} %collective-permute-done.5.fa, f32[2,2,5,32,128]{4,3,2,1,0:T(8,128)S(1)} %collective-permute-done.6.fb, f32[5,56,128]{2,1,0:T(8,128)S(1)} %collective-permute-done.7.fy, ...), custom_call_target="tpu_custom_call" | custom-call | flops 2750000128 | bytes 2703360 | tf_op jit(solution)/shard_map/pallas_call | solution.py:602
  45.2 0.8 %shard_map.136 = f32[2,5,8,128]{3,2,1,0:T(8,128)} custom-call(f32[11,32,128]{2,1,0:T(8,128)S(1)} %shard_map.132.kept.gate, f32[11,32,128]{2,1,0:T(8,128)S(1)} %collective-permute-done.10.swapped, s32[2,128]{1,0:T(2,128)S(1)} %copy-done.4), custom_call_target="tpu_custom_call" | custom-call | flops 770000000 | bytes 81920 | tf_op jit(solution)/shard_map/pallas_call | solution.py:602
  45.9 3.3 %shard_map.133 = f32[5,32,16,128]{3,2,1,0:T(8,128)} custom-call(s32[1]{0:T(128)S(6)} %copy.21.relax, f32[5,5]{1,0:T(8,128)S(1)} %copy-done.2, f32[5,16,32,128]{3,2,1,0:T(8,128)S(1)} %shard_map.130.inside, f32[16,32,128]{2,1,0:T(8,128)S(1)} %get-tuple-element.31.gate.dt, f32[2,2,5,32,128]{4,3,2,1,0:T(8,128)S(1)} %collective-permute-done.5.fa, ...), custom_call_target="tpu_custom_call" | custom-call | flops 3300000000 | bytes 2621440 | tf_op jit(solution)/shard_map/pallas_call | solution.py:602
  (18 shorter events, 0.1 us)
Async XLA Ops:
  1.3 10.8 %copy-start.2 = (f32[5,5]{1,0:T(8,128)S(1)}, f32[5,5]{1,0:T(8,128)}, u32[]{:S(2)}) copy-start(f32[5,5]{1,0:T(8,128)} %mix.9) | copy-start | bytes 304
  4.4 12.3 %collective-permute-start.2 = (f32[5,56,128]{2,1,0:T(8,128)S(1)}, f32[5,56,128]{2,1,0:T(8,128)S(1)}, u32[]{:S(2)}, u32[]{:S(2)}) collective-permute-start(f32[5,56,128]{2,1,0:T(8,128)S(1)} %get-tuple-element.36.own), channel_id=1, source_target_pairs={{0,1},{1,0},{2,3},{3,2},{4,5},{5,4},{6,7},{7,6},{8,9},{9,8},{10,11... | collective-permute-start | bytes 430088 | tf_op jit(solution)/shard_map/ppermute | solution.py:644
  7.4 9.6 %collective-permute-start = (f32[2,2,5,32,128]{4,3,2,1,0:T(8,128)S(1)}, f32[2,2,5,32,128]{4,3,2,1,0:T(8,128)S(1)}, u32[]{:S(2)}, u32[]{:S(2)}) collective-permute-start(f32[2,2,5,32,128]{4,3,2,1,0:T(8,128)S(1)} %get-tuple-element.34), channel_id=1, source_target_pairs={{0,2},{2,0},{4,6},{6,4},{8,10},{10,8},{12,14},{14,12},{16,18},{18,... | collective-permute-start | bytes 983048 | tf_op jit(solution)/shard_map/ppermute | solution.py:679
  7.4 9.6 %collective-permute-start.1 = (f32[2,2,5,32,128]{4,3,2,1,0:T(8,128)S(1)}, f32[2,2,5,32,128]{4,3,2,1,0:T(8,128)S(1)}, u32[]{:S(2)}, u32[]{:S(2)}) collective-permute-start(f32[2,2,5,32,128]{4,3,2,1,0:T(8,128)S(1)} %get-tuple-element.35), channel_id=1, source_target_pairs={{0,30},{2,4},{4,2},{6,8},{8,6},{10,12},{12,10},{14,16},{16,14},{18... | collective-permute-start | bytes 983048 | tf_op jit(solution)/shard_map/ppermute | solution.py:680
  14.4 2.3 %copy-start.1 = (f32[2,5,8,128]{3,2,1,0:T(8,128)S(1)}, f32[2,5,8,128]{3,2,1,0:T(8,128)}, u32[]{:S(2)}) copy-start(f32[2,5,8,128]{3,2,1,0:T(8,128)} %parent.1) | copy-start | bytes 122884
  14.5 2.3 %copy-start.4 = (s32[2,128]{1,0:T(2,128)S(1)}, s32[2,128]{1,0:T(2,128)}, u32[]{:S(2)}) copy-start(s32[2,128]{1,0:T(2,128)} %terrain.3) | copy-start | bytes 3076
  16.9 5.6 %collective-permute-start.3 = (f32[6,32,128]{2,1,0:T(8,128)S(1)}, f32[6,32,128]{2,1,0:T(8,128)S(1)}, u32[]{:S(2)}, u32[]{:S(2)}) collective-permute-start(f32[6,32,128]{2,1,0:T(8,128)S(1)} %get-tuple-element.39), channel_id=1, source_target_pairs={{0,16},{2,18},{4,20},{6,22},{8,24},{10,26},{12,28},{14,30},{16,0},... | collective-permute-start | bytes 294920 | tf_op jit(solution)/shard_map/ppermute | solution.py:640
  17.0 6.2 %copy-start.3 = (s32[2,16]{1,0:T(2,128)S(1)}, s32[2,16]{1,0:T(2,128)}, u32[]{:S(2)}) copy-start(s32[2,16]{1,0:T(2,128)} %tsn.3) | copy-start | bytes 388
  22.5 1.3 %copy-start = (f32[2,5,64,16]{2,3,1,0:T(8,128)S(1)}, f32[2,5,64,16]{2,3,1,0:T(8,128)}, u32[]{:S(2)}) copy-start(f32[2,5,64,16]{2,3,1,0:T(8,128)} %param.14) | copy-start | bytes 122884
  22.5 5.6 %collective-permute-start.4 = (f32[11,32,128]{2,1,0:T(8,128)S(1)}, f32[11,32,128]{2,1,0:T(8,128)S(1)}, u32[]{:S(2)}, u32[]{:S(2)}) collective-permute-start(f32[11,32,128]{2,1,0:T(8,128)S(1)} %shard_map.127), channel_id=1, source_target_pairs={{0,4},{2,6},{4,0},{6,2},{8,12},{10,14},{12,8},{14,10},{16,20},{18,... | collective-permute-start | bytes 540680 | tf_op jit(solution)/shard_map/ppermute | solution.py:640
  28.1 8.2 %collective-permute-start.8 = (f32[11,32,128]{2,1,0:T(8,128)S(1)}, f32[11,32,128]{2,1,0:T(8,128)S(1)}, u32[]{:S(2)}, u32[]{:S(2)}) collective-permute-start(f32[11,32,128]{2,1,0:T(8,128)S(1)} %add.3.gate.state), channel_id=1, source_target_pairs={{0,8},{2,10},{4,12},{6,14},{8,0},{10,2},{12,4},{14,6},{16,24},{18,... | collective-permute-start | bytes 540680 | tf_op jit(solution)/shard_map/ppermute | solution.py:640
  30.8 12.5 %collective-permute-start.5 = (f32[2,2,5,32,128]{4,3,2,1,0:T(8,128)S(1)}, f32[2,2,5,32,128]{4,3,2,1,0:T(8,128)S(1)}, u32[]{:S(2)}, u32[]{:S(2)}) collective-permute-start(f32[2,2,5,32,128]{4,3,2,1,0:T(8,128)S(1)} %get-tuple-element.46), channel_id=1, source_target_pairs={{0,2},{2,0},{4,6},{6,4},{8,10},{10,8},{12,14},{14,12},{16,18},{18,... | collective-permute-start | bytes 983048 | tf_op jit(solution)/shard_map/ppermute | solution.py:792
  30.9 12.4 %collective-permute-start.6 = (f32[2,2,5,32,128]{4,3,2,1,0:T(8,128)S(1)}, f32[2,2,5,32,128]{4,3,2,1,0:T(8,128)S(1)}, u32[]{:S(2)}, u32[]{:S(2)}) collective-permute-start(f32[2,2,5,32,128]{4,3,2,1,0:T(8,128)S(1)} %get-tuple-element.47), channel_id=1, source_target_pairs={{0,30},{2,4},{4,2},{6,8},{8,6},{10,12},{12,10},{14,16},{16,14},{18... | collective-permute-start | bytes 983048 | tf_op jit(solution)/shard_map/ppermute | solution.py:793
  35.7 7.6 %collective-permute-start.7 = (f32[5,56,128]{2,1,0:T(8,128)S(1)}, f32[5,56,128]{2,1,0:T(8,128)S(1)}, u32[]{:S(2)}, u32[]{:S(2)}) collective-permute-start(f32[5,56,128]{2,1,0:T(8,128)S(1)} %get-tuple-element.48.own), channel_id=1, source_target_pairs={{0,1},{1,0},{2,3},{3,2},{4,5},{5,4},{6,7},{7,6},{8,9},{9,8},{10,11... | collective-permute-start | bytes 430088 | tf_op jit(solution)/shard_map/ppermute | solution.py:644
  36.4 6.8 %collective-permute-start.9 = (f32[5,32,128]{2,1,0:T(8,128)S(1)}, f32[5,32,128]{2,1,0:T(8,128)S(1)}, u32[]{:S(2)}, u32[]{:S(2)}) collective-permute-start(f32[5,32,128]{2,1,0:T(8,128)S(1)} %get-tuple-element.50), channel_id=1, source_target_pairs={{0,16},{2,18},{4,20},{6,22},{8,24},{10,26},{12,28},{14,30},{16,0},... | collective-permute-start | bytes 245768 | tf_op jit(solution)/shard_map/ppermute | solution.py:640
  43.2 1.9 %collective-permute-start.10 = (f32[11,32,128]{2,1,0:T(8,128)S(1)}, f32[11,32,128]{2,1,0:T(8,128)S(1)}, u32[]{:S(2)}, u32[]{:S(2)}) collective-permute-start(f32[11,32,128]{2,1,0:T(8,128)S(1)} %shard_map.132.kept.gate), channel_id=1, source_target_pairs={{0,2},{2,0},{4,6},{6,4},{8,10},{10,8},{12,14},{14,12},{16,18},{18,... | collective-permute-start | bytes 540680 | tf_op jit(solution)/shard_map/ppermute | solution.py:640
where the time goes:
time: 49.4 us; the launch traced here: 49.2 us
  Pallas kernels  25.1 us (51%)
  starting transfers between devices  13.6 us (28%)
  waiting for transfers between devices  8.92 us (18%)
  between operations  1.48 us (3%)
    pallas_call x17, Pallas kernels, call(): pl.pallas_call(kernel, out_shape=out_shape, in_specs=[places[where] for w...  25.1 us
    ppermute x5, waiting for transfers between devices, swapped(): return lax.ppermute(values, 'gx', [(i, i ^ distance) for i in range(nx)])  8.91 us
    ppermute x2, starting transfers between devices, body(): fb = lax.ppermute(mb, 'gx', odds)  7.22 us
    ppermute x2, starting transfers between devices, to_y(): return lax.ppermute(message, 'gy', [(0, 1), (1, 0)])  3.6 us
    ppermute x5, starting transfers between devices, swapped(): return lax.ppermute(values, 'gx', [(i, i ^ distance) for i in range(nx)])  2.71 us
  transfers between devices with their start and end apart: 11, of which 3 were waited for; matrix products, arithmetic and copies ran while one was open for 0% of the time, Pallas kernels for 36%

commit v1 on v0

--- a/solution.py
+++ b/solution.py
@@ -29,8 +29,8 @@
         assert self.K % 8 == 0 and self.Y == 128 and 4 * self.X <= 64
         assert self.X > widest_zone and self.Y > widest_zone
         assert self.X == 16
-        assert nx >= 4 and nx & (nx - 1) == 0 and ny % 2 == 0
-        assert 4 * self.F <= 128
+        assert nx >= 16 and nx & (nx - 1) == 0 and ny % 2 == 0
+        assert 4 * self.F <= 128 and 128 % self.K == 0
         self.pair = ny == 2
         self.tall = self.K + self.X + 8
 
@@ -75,15 +75,28 @@
     )
 
 
-def lap_inside(cells, x):
-    beside = {
-        1: [turn(cells[x], 1), turn(cells[x], -1)],
-        2: [turn(cells[x], 2), turn(cells[x], -2)],
-    }
-    for step in (1, 2):
-        beside[step] += [cells[x + i] for i in (-step, step) if 0 <= x + i < len(cells)]
-    total = near * functools.reduce(jnp.add, beside[1]) - 5.0 * cells[x]
-    return total + far * functools.reduce(jnp.add, beside[2])
+def fill_band(band):
+    shape = (2 * 128, 128)
+    row = lax.broadcasted_iota(jnp.int32, shape, 0) % 128
+    gap = jnp.abs(row - lax.broadcasted_iota(jnp.int32, shape, 1))
+    entry = jnp.where(gap == 0, -60.0, jnp.where(gap == 1, 16.0, jnp.where(gap == 2, -1.0, 0.0)))
+    band[...] = entry.astype(jnp.bfloat16)
+
+
+def along_lanes(values, band):
+    high = values.astype(jnp.bfloat16)
+    low = (values - high.astype(f32)).astype(jnp.bfloat16)
+    return jnp.dot(
+        jnp.concatenate([high, low], axis=1), band[...], preferred_element_type=f32
+    )
+
+
+def lap_inside(cells, lane_part, x):
+    count = len(cells)
+    ones = [cells[x + i] for i in (-1, 1) if 0 <= x + i < count]
+    twos = [cells[x + i] for i in (-2, 2) if 0 <= x + i < count]
+    total = lane_part + 16.0 * functools.reduce(jnp.add, ones) - functools.reduce(jnp.add, twos)
+    return total * (1.0 / 12.0)
 
 
 def pack_lanes(x, base, values, packed):
@@ -184,8 +197,8 @@
 
 
 class Beyond:
-    def __init__(self, g, s, fa, fb, fy, own):
-        self.g, self.s, self.fa, self.fb, self.fy, self.own = g, s, fa, fb, fy, own
+    def __init__(self, g, s, fa, fb, fy):
+        self.g, self.s, self.fa, self.fb, self.fy = g, s, fa, fb, fy
         self.edge = border()
         self.valid = valid_lanes(g)
         here = lax.axis_index("gx")
@@ -203,7 +216,7 @@
         return jnp.where(self.last, jnp.zeros_like(value), value)
 
     def lanes_of(self, f, rows):
-        return self.fy[f, rows, :] * self.valid - self.own[f, rows, :]
+        return self.fy[f, rows, :] * self.valid
 
     def add(self, f, x, rows, packed):
         s, last = self.s, self.g.X - 1
@@ -304,49 +317,58 @@
         my[f, g.K + g.X : g.K + g.X + span, :] = total
 
 
-def adjoint_inside_kernel(g, scaled, relax, mix, ps, qs, gate, out, rx):
+class Column:
+    def __init__(self, ref, f, rows, count):
+        self.ref, self.f, self.rows, self.count = ref, f, rows, count
+
+    def __len__(self):
+        return self.count
+
+    def __getitem__(self, x):
+        return self.ref[self.f, x, self.rows, :]
+
+
+def lane_parts(g, source, rows, band, parts):
+    for f in range(g.F):
+        parts[f] = along_lanes(source[f, :, rows, :].reshape(8 * g.X, 128), band)
+
+
+def adjoint_inside_kernel(g, scaled, relax, mix, ps, qs, out, rx, band, parts):
     width = relax[0]
     table = mix_table(mix, True)
+    fill_band(band)
     if scaled:
         fill_ramp_x(g, width, rx)
         open_y = 1.0 - ramp_y(g, width)
 
     def tile_step(tile, carry):
         rows = rows_of(tile)
+        lane_parts(g, qs, rows, band, parts)
         for x in range(g.X):
             p = [ps[f, x, rows, :] for f in range(g.F)]
             if scaled:
                 open_xy = open_y * (1.0 - rx[x])
                 p = [open_xy * value for value in p]
             for f in range(g.F):
-                near_cells = Column(qs, f, rows, g.X)
-                out[f, x, rows, :] = mixed(table, f, p) + lap_inside(near_cells, x)
+                lap = lap_inside(Column(qs, f, rows, g.X), parts[f, 8 * x : 8 * x + 8, :], x)
+                out[f, x, rows, :] = mixed(table, f, p) + lap
         return carry
 
     lax.fori_loop(0, g.tiles, tile_step, 0)
 
 
-class Column:
-    def __init__(self, ref, f, rows, count):
-        self.ref, self.f, self.rows, self.count = ref, f, rows, count
-
-    def __len__(self):
-        return self.count
-
-    def __getitem__(self, x):
-        return self.ref[self.f, x, self.rows, :]
-
-
-def forward_inside_kernel(g, mix, ut, dt, gate, out):
+def forward_inside_kernel(g, mix, ut, dt, out, band, parts):
     table = mix_table(mix, False)
+    fill_band(band)
 
     def tile_step(tile, carry):
         rows = rows_of(tile)
+        lane_parts(g, ut, rows, band, parts)
         for x in range(g.X):
             u = [ut[f, x, rows, :] for f in range(g.F)]
             d = dt[x, rows, :]
             for f in range(g.F):
-                lap = lap_inside(Column(ut, f, rows, g.X), x)
+                lap = lap_inside(Column(ut, f, rows, g.X), parts[f, 8 * x : 8 * x + 8, :], x)
                 out[f, x, rows, :] = mixed(table, f, u) + d * lap
         return carry
 
@@ -354,13 +376,13 @@
 
 
 def adjoint_first_kernel(
-    g, relax, inside, at, dt, fa, fb, fy, own, gate, p1, q1, ma, mb, my, dwe, dsn, rx
+    g, relax, inside, at, dt, fa, fb, fy, p1, q1, ma, mb, my, dwe, dsn, rx
 ):
     width = relax[0]
     fill_ramp_x(g, width, rx)
     slope_y = ramp_y(g, width)
     open_y = 1.0 - slope_y
-    beyond = Beyond(g, 1, fa, fb, fy, own)
+    beyond = Beyond(g, 1, fa, fb, fy)
 
     def tile_step(tile, carry):
         rows = rows_of(tile)
@@ -393,12 +415,12 @@
 
 
 def forward_first_kernel(
-    g, relax, inside, dt, fa, fb, fy, own, sides, gate, ma_in, mb_in, my_in, u1, ma, mb, my, rx
+    g, relax, inside, dt, fa, fb, fy, sides, ma_in, mb_in, my_in, u1, ma, mb, my, rx
 ):
     width = relax[0]
     fill_ramp_x(g, width, rx)
     open_y = 1.0 - ramp_y(g, width)
-    beyond = Beyond(g, 0, fa, fb, fy, own)
+    beyond = Beyond(g, 0, fa, fb, fy)
     lane = lanes()
 
     def tile_step(tile, carry):
@@ -419,9 +441,9 @@
     lax.fori_loop(0, g.tiles, tile_step, 0)
 
 
-def adjoint_last_kernel(g, inside, fa, fb, fy, own, gsn_own, gate, out, gsn):
+def adjoint_last_kernel(g, inside, fa, fb, fy, gsn_own, out, gsn):
     out2 = out.reshape(g.F * g.K * g.X, g.Y)
-    beyond = Beyond(g, 1, fa, fb, fy, own)
+    beyond = Beyond(g, 1, fa, fb, fy)
 
     def tile_step(tile, carry):
         rows = rows_of(tile)
@@ -444,7 +466,7 @@
 
 
 def forward_last_kernel(
-    g, relax, mix, inside, dt, fa, fb, fy, own, sides, kept, swapped, out, rx, lx
+    g, relax, mix, inside, dt, fa, fb, fy, sides, kept, swapped, out, rx, lx
 ):
     width = relax[0]
     for x in range(-2, g.X + 2):
@@ -455,15 +477,15 @@
     open_y = 1.0 - ramp_y(g, width)
     masks = lap_masks()
     table = mix_table(mix, False)
-    beyond = Beyond(g, 0, fa, fb, fy, own)
+    beyond = Beyond(g, 0, fa, fb, fy)
     out2 = out.reshape(g.F * g.K * g.X, g.Y)
 
     def tile_step(tile, carry):
         rows = rows_of(tile)
         bound = [
-            open_y * (kept[g.F + f, rows, :] + swapped[g.F + f, rows, :]) for f in range(g.F)
+            open_y * (kept[f, rows, :] + swapped[f, rows, :]) for f in range(g.F)
         ]
-        past = packed_message(kept[2 * g.F, rows, :] + swapped[2 * g.F, rows, :]) * beyond.valid
+        past = packed_message(kept[g.F, rows, :] + swapped[g.F, rows, :]) * beyond.valid
         for f in range(g.F):
             lap_y = unpack_lanes(f, 0, past, beyond.edge)
             for shift, mask in masks:
@@ -485,16 +507,22 @@
 def side_sums_kernel(g, dsn, tsn, my_in, gsn, my, wide):
     here = lax.axis_index("gy")
     shift = column_of(jnp.where(here == 0, tsn[0:1, :], tsn[1:2, :]))
-    wide[...] = jnp.zeros(wide.shape, f32)
-    for f in range(g.F):
-        wide[f, : g.K, :] = dsn[f]
-        whole = shift_levels(wide[f].T[: g.X], shift, 1)
-        moved = turn(whole, 64)
-        gsn[f] = jnp.where(here == 0, whole, moved)
-        my[f, g.K : g.K + g.X, :] = jnp.where(here == 0, moved, whole)
-
-
-def side_bounds_kernel(g, sn, fsn, tsn, gate, bsn, wide):
+    lane = lax.broadcasted_iota(jnp.int32, (g.X, 128), 1)
+    batch = 128 // g.K
+    for first in range(0, g.F, batch):
+        some = range(first, min(first + batch, g.F))
+        for f in some:
+            wide[(f - first) * g.K : (f - first + 1) * g.K, :] = dsn[f]
+        turned = wide[...].T[: g.X]
+        for f in some:
+            levels = jnp.where(lane < g.K, turn(turned, -(f - first) * g.K), 0.0)
+            whole = shift_levels(levels, shift, 1)
+            moved = turn(whole, 64)
+            gsn[f] = jnp.where(here == 0, whole, moved)
+            my[f, g.K : g.K + g.X, :] = jnp.where(here == 0, moved, whole)
+
+
+def side_bounds_kernel(g, sn, fsn, tsn, bsn, wide):
     here = lax.axis_index("gy")
     shift = column_of(jnp.where(here == 0, tsn[0:1, :], tsn[1:2, :]))
     span = sn.shape[3]
@@ -557,50 +585,47 @@
         send[i] = jnp.where(odd, parts[0][i], parts[1][i])
 
 
-def join_kernel(g, sums, bounds, more_bounds, out):
-    for f in range(g.F):
-        out[f] = sums[f]
-    for f in range(g.F + 1):
-        out[g.F + f] = bounds[f] + more_bounds[f]
-
-
-def split_kernel(g, state, moved, out, sums):
-    for f in range(2 * g.F + 1):
-        total = state[f] + moved[f]
-        out[f] = total
-        if f < g.F:
-            sums[f] = total
-
-
-def finish_kernel(g, state, moved, out):
-    for f in range(g.F):
-        out[f] = state[f] + moved[f]
-    for f in range(g.F, 2 * g.F + 1):
-        out[f] = state[f]
+def add_kernel(g, first, second, out):
+    out[...] = first[...] + second[...]
 
 
 def spread_kernel(g, kept, swapped, terrain, out):
     here = lax.axis_index("gx")
     odd = here % 2
     span = out.shape[2]
+    row = lax.broadcasted_iota(jnp.int32, (8, 128), 0)
+    zero = jnp.zeros((8, 128), f32)
     for e in range(2):
-        place = lax.broadcasted_iota(jnp.int32, (span, 128), 0) + here * span - terrain[e : e + 1, :]
-        keep = [place == k for k in range(g.K)]
+        start = jnp.broadcast_to(here * span - terrain[e : e + 1, :], (8, 128)) + 8
+        inside = (start > 0) & (start < g.K + 8)
+        tile, rest = start >> 3, start & 7
         for f in range(g.F):
-            a, b = kept[f], swapped[f]
-            chosen = jnp.where(odd == e, a, b)
-            total = jnp.zeros((span, 128), f32)
-            for k in range(g.K):
-                row = jnp.broadcast_to(chosen[k : k + 1, :], (span, 128))
-                total = jnp.where(keep[k], row, total)
-            out[e, f] = total
-
-
-def call(kernel, outs, scratch, ins, time, aliases=None):
+            chosen = jnp.where(odd == e, kept[f], swapped[f])
+            tiles = [zero] + [chosen[8 * i : 8 * i + 8] for i in range(g.tiles)] + [zero]
+            low, high = zero, zero
+            for i in range(g.tiles + 1):
+                low = jnp.where(tile == i, tiles[i], low)
+                high = jnp.where(tile == i, tiles[i + 1], high)
+            for step in (4, 2, 1):
+                moves = (rest & step) != 0
+                up_low = pltpu.roll(low, 8 - step, 0)
+                up_high = pltpu.roll(high, 8 - step, 0)
+                low = jnp.where(moves, jnp.where(row < 8 - step, up_low, up_high), low)
+                high = jnp.where(moves, up_high, high)
+            out[e, f] = jnp.where(inside, low, zero)[:span]
+
+
+def call(kernel, outs, scratch, ins, time, aliases=None, after=()):
+    count = len(ins)
+    ins = ins + [("a", value) for value in after]
+
+    def run(*refs):
+        kernel(*refs[:count], *refs[len(ins) :])
+
     out_shape = [jax.ShapeDtypeStruct(s, f32) for s in outs]
     size = 4 * sum(functools.reduce(lambda a, b: a * b, s) for s in outs)
     return pl.pallas_call(
-        kernel,
+        run,
         out_shape=out_shape,
         in_specs=[places[where] for where, _ in ins],
         out_specs=[places["v"]] * len(outs),
@@ -632,6 +657,8 @@
     lane_shape = (F, g.tall, 128)
     edge_shape = (F, K, 128)
     ramps = (X, 8, 128)
+    band = pltpu.VMEM((256, 128), jnp.bfloat16)
+    parts = (F, 8 * X, 128)
 
     def bind(kernel, *args):
         return functools.partial(kernel, g, *args)
@@ -647,6 +674,12 @@
         low = (jnp.arange(128, dtype=jnp.int32) % 4 < 2)[None, None, :]
         rows = (jnp.arange(g.tall, dtype=jnp.int32) < K)[None, :, None]
         return jnp.where(low == rows, down, up)
+
+    def add(first, second, after):
+        (total,) = call(
+            bind(add_kernel), [first.shape], [], [("v", first), ("v", second)], 0.1, after=after
+        )
+        return total
 
     sn_turned = jnp.swapaxes(parent_sn, 2, 3)
     ut, at, dt, qt, ma, mb, my = call(
@@ -674,24 +707,24 @@
         ],
         3,
     )
-    own = my
+    fb = lax.ppermute(mb, "gx", odds)
+    fa = lax.ppermute(ma, "gx", evens)
     fy = to_y(my)
-    fa = lax.ppermute(ma, "gx", evens)
-    fb = lax.ppermute(mb, "gx", odds)
 
     (inside_a,) = call(
         bind(adjoint_inside_kernel, True),
         [block],
-        [ramps],
-        [("s", relax_width), ("s", field_mix), ("v", at), ("v", qt), ("a", dt)],
+        [ramps, band, parts],
+        [("s", relax_width), ("s", field_mix), ("v", at), ("v", qt)],
         2.5,
     )
     (inside_u,) = call(
         bind(forward_inside_kernel),
         [block],
-        [],
-        [("s", field_mix), ("v", ut), ("v", dt), ("a", inside_a)],
+        [band, parts],
+        [("s", field_mix), ("v", ut), ("v", dt)],
         2.5,
+        after=[inside_a],
     )
     keep, send = call(
         bind(fold_kernel),
@@ -701,6 +734,21 @@
         0.3,
     )
     first_bounds = swapped(send, nx // 2)
+
+    if g.pair:
+        (bsn,) = call(
+            bind(side_bounds_kernel),
+            [edge_shape],
+            [(F, 128, 128)],
+            [("v", sn_turned), ("v", fy), ("v", terrain_sn)],
+            0.7,
+        )
+    else:
+        bsn = bound_sn_general(g, parent_sn, terrain_sn)
+    (sides,) = call(
+        bind(side_spread_kernel), [block], [], [("s", relax_width), ("v", bsn)], 0.7
+    )
+
     p1, q1, ma, mb, my, dwe, dsn = call(
         bind(adjoint_first_kernel),
         [block, block, row_shape, row_shape, lane_shape, edge_shape, edge_shape],
@@ -713,59 +761,13 @@
             ("v", fa),
             ("v", fb),
             ("v", fy),
-            ("v", own),
-            ("a", keep),
         ],
         3,
-    )
-    if g.pair:
-        (bsn,) = call(
-            bind(side_bounds_kernel),
-            [edge_shape],
-            [(F, 128, 128)],
-            [("v", sn_turned), ("v", fy), ("v", terrain_sn), ("a", dwe)],
-            0.7,
-        )
-    else:
-        bsn = bound_sn_general(g, parent_sn, terrain_sn)
-    (sides,) = call(
-        bind(side_spread_kernel), [block], [], [("s", relax_width), ("v", bsn)], 0.7
-    )
-    state_shape = (2 * F + 1, K, 128)
-    (state,) = call(
-        bind(join_kernel),
-        [state_shape],
-        [],
-        [("v", dwe), ("v", keep), ("v", first_bounds)],
-        0.1,
-    )
-    gates = []
-    distance = 2
-    while distance < nx // 4:
-        state = state + swapped(state, distance)
-        gates.append(state)
-        distance *= 2
-    moved = swapped(state, distance) if distance < nx // 2 else jnp.zeros_like(state)
-    state, sums = call(
-        bind(split_kernel), [state_shape, edge_shape], [], [("v", state), ("v", moved)], 0.1
-    )
-    gates.append(state)
-    (state,) = call(
-        bind(finish_kernel), [state_shape], [], [("v", state), ("v", swapped(sums, nx // 2))], 0.1
-    )
-    other = swapped(state, 1)
-
-    if g.pair:
-        gsn_own, my = call(
-            bind(side_sums_kernel),
-            [(F, X, 128), lane_shape],
-            [(F, 128, 128)],
-            [("v", dsn), ("v", terrain_sn), ("v", my)],
-            0.6,
-            {2: 1},
-        )
-    else:
-        gsn_own = dsn
+        after=[keep, sides],
+    )
+    first_sums = swapped(dwe, 2)
+    bounds = add(keep, first_bounds, [dwe])
+    second_bounds = swapped(bounds, 2)
     u1, ma, mb, my = call(
         bind(forward_first_kernel),
         [block, row_shape, row_shape, lane_shape],
@@ -777,42 +779,72 @@
             ("v", fa),
             ("v", fb),
             ("v", fy),
-            ("v", own),
             ("v", sides),
-            ("a", gates[0]),
             ("v", ma),
             ("v", mb),
             ("v", my),
         ],
         2.5,
-        {9: 1, 10: 2, 11: 3},
-    )
-    own = my
+        {7: 1, 8: 2, 9: 3},
+        after=[bounds],
+    )
+    if g.pair:
+        gsn_own, my = call(
+            bind(side_sums_kernel),
+            [(F, X, 128), lane_shape],
+            [(128, 128)],
+            [("v", dsn), ("v", terrain_sn), ("v", my)],
+            0.6,
+            {2: 1},
+        )
+    else:
+        gsn_own = dsn
+    fb = lax.ppermute(mb, "gx", odds)
+    fa = lax.ppermute(ma, "gx", evens)
     fy = to_y(my)
-    fa = lax.ppermute(ma, "gx", evens)
-    fb = lax.ppermute(mb, "gx", odds)
-
+
+    sums = add(dwe, first_sums, [gsn_own])
+    second_sums = swapped(sums, 4)
+    bounds = add(bounds, second_bounds, [gsn_own])
+    third_bounds = swapped(bounds, 4)
     (inside_a,) = call(
         bind(adjoint_inside_kernel, False),
         [block],
-        [ramps],
-        [("s", relax_width), ("s", field_mix), ("v", p1), ("v", q1), ("a", gates[-1])],
+        [ramps, band, parts],
+        [("s", relax_width), ("s", field_mix), ("v", p1), ("v", q1)],
         2.5,
-    )
+        after=[sums, bounds],
+    )
+    sums = add(sums, second_sums, [inside_a])
+    third_sums = swapped(sums, 8)
     (inside_u,) = call(
         bind(forward_inside_kernel),
         [block],
-        [],
-        [("s", field_mix), ("v", u1), ("v", dt), ("a", u1)],
+        [band, parts],
+        [("s", field_mix), ("v", u1), ("v", dt)],
         2.5,
-    )
+        after=[sums],
+    )
+    bounds = add(bounds, third_bounds, [inside_u])
+    distance = 8
+    while distance < nx // 2:
+        bounds = bounds + swapped(bounds, distance)
+        distance *= 2
+    other_bounds = swapped(bounds, 1)
     grad_state, grad_sn = call(
         bind(adjoint_last_kernel),
         [child_state.shape, sn_turned.shape],
         [],
-        [("v", inside_a), ("v", fa), ("v", fb), ("v", fy), ("v", own), ("v", gsn_own), ("a", state)],
+        [("v", inside_a), ("v", fa), ("v", fb), ("v", fy), ("v", gsn_own)],
         2.5,
-    )
+        after=[bounds],
+    )
+    sums = add(sums, third_sums, [grad_state])
+    distance = 16
+    while distance < nx:
+        sums = sums + swapped(sums, distance)
+        distance *= 2
+    other_sums = swapped(sums, 1)
     (child_final,) = call(
         bind(forward_last_kernel),
         [child_state.shape],
@@ -825,10 +857,9 @@
             ("v", fa),
             ("v", fb),
             ("v", fy),
-            ("v", own),
             ("v", sides),
-            ("v", state),
-            ("v", other),
+            ("v", bounds),
+            ("v", other_bounds),
         ],
         3,
     )
@@ -836,7 +867,7 @@
         bind(spread_kernel),
         [parent_we.shape],
         [],
-        [("v", state), ("v", other), ("v", terrain_we)],
+        [("v", sums), ("v", other_sums), ("v", terrain_we)],
         0.7,
     )
     if g.pair:

time: 49.4 us -> 49.6 us (level)
  starting transfers between devices: 13.6 us -> 19.7 us
  waiting for transfers between devices: 8.92 us -> 3.27 us
  Pallas kernels: 25.1 us -> 23.6 us
  local copies, waits for them, and re-layouts: 0.03 us -> 1.35 us
    ppermute x5 -> x8, waiting for transfers between devices: 8.91 us -> 3.26 us  [swapped(): return lax.ppermute(values, 'gx', [(i, i ^ distance) for i in range(nx)])]
    ppermute x5 -> x8, starting transfers between devices: 2.71 us -> 7.57 us  [swapped(): return lax.ppermute(values, 'gx', [(i, i ^ distance) for i in range(nx)])]
    pallas_call x17 -> x20, Pallas kernels: 25.1 us -> 23.6 us  [call(): pl.pallas_call(run, out_shape=out_shape, in_specs=[places[where] for wher...]
    unnamed x10 -> x12, local copies, waits for them, and re-layouts: 0.03 us -> 1.35 us
    ppermute x2, starting transfers between devices: 7.22 us -> 8.53 us  [body(): fb = lax.ppermute(mb, 'gx', odds)]
  transfers between devices with their start and end apart: 11 -> 14, of which waited for: 3 -> 1; matrix products, arithmetic and copies ran while one was open for 0% -> 0% of each run, Pallas kernels for 36% -> 40%
where the time goes in v1:
time: 49.6 us; the launch traced here: 49.4 us
  Pallas kernels  23.6 us (48%)
  starting transfers between devices  19.7 us (40%)
  waiting for transfers between devices  3.27 us (7%)
  between operations  1.53 us (3%)
  local copies, waits for them, and re-layouts  1.35 us (3%)
    pallas_call x20, Pallas kernels, call(): pl.pallas_call(run, out_shape=out_shape, in_specs=[places[where] for wher...  23.6 us
    ppermute x2, starting transfers between devices, body(): fb = lax.ppermute(mb, 'gx', odds)  8.53 us
    ppermute x8, starting transfers between devices, swapped(): return lax.ppermute(values, 'gx', [(i, i ^ distance) for i in range(nx)])  7.57 us
    ppermute x2, starting transfers between devices, to_y(): return lax.ppermute(message, 'gy', [(0, 1), (1, 0)])  3.6 us
    ppermute x8, waiting for transfers between devices, swapped(): return lax.ppermute(values, 'gx', [(i, i ^ distance) for i in range(nx)])  3.26 us
    unnamed x12, local copies, waits for them, and re-layouts  1.35 us
  transfers between devices with their start and end apart: 14, of which 1 were waited for; matrix products, arithmetic and copies ran while one was open for 0% of the time, Pallas kernels for 40%

profile of v1, /device:TPU:0, one launch (start us, length us, event | category | flops | bytes accessed | tf_op | source)
XLA Modules:
  0.0 49.4 jit_solution(945882817497234074)
XLA Ops:
  1.3 3.1 %shard_map.120 = (f32[5,16,32,128]{3,2,1,0:T(8,128)S(1)}, f32[5,16,32,128]{3,2,1,0:T(8,128)S(1)}, f32[16,32,128]{2,1,0:T(8,128)S(1)}, f32[5,16,32,128]{3,2,1,0:T...) custom-call(s32[1]{0:T(128)S(6)} %copy.21.refs_0_, ...), custom_call_target="tpu_custom_call" | custom-call | flops 3300000000 | bytes 9986048 | tf_op jit(solution)/shard_map/pallas_call | solution.py:627
  4.4 3.0 %collective-permute-start.2 = (f32[5,56,128]{2,1,0:T(8,128)S(1)}, f32[5,56,128]{2,1,0:T(8,128)S(1)}, u32[]{:S(2)}, u32[]{:S(2)}) collective-permute-start(f32[5,56,128]{2,1,0:T(8,128)S(1)} %get-tuple-element.34), channel_id=1, source_target_pairs={{0,1},{1,0},{2,3},{3,2},{4,5},{5,4},{6,7},{7,6},{8,9},{9,8},{10,11... | collective-permute-start | bytes 430088 | tf_op jit(solution)/shard_map/ppermute | solution.py:671
  7.4 4.7 %collective-permute-start.1 = (f32[2,2,5,32,128]{4,3,2,1,0:T(8,128)S(1)}, f32[2,2,5,32,128]{4,3,2,1,0:T(8,128)S(1)}, u32[]{:S(2)}, u32[]{:S(2)}) collective-permute-start(f32[2,2,5,32,128]{4,3,2,1,0:T(8,128)S(1)} %get-tuple-element.33), channel_id=1, source_target_pairs={{0,30},{2,4},{4,2},{6,8},{8,6},{10,12},{12,10},{14,16},{16,14},{18... | collective-permute-start | bytes 983048 | tf_op jit(solution)/shard_map/ppermute | solution.py:710
  12.1 1.9 %shard_map.121.refs_3_.refs_1_ = f32[5,16,32,128]{3,2,1,0:T(8,128)S(1)} custom-call(s32[1]{0:T(128)S(6)} %copy.21.refs_0_, f32[5,5]{1,0:T(8,128)S(1)} %copy-done.3, f32[5,16,32,128]{3,2,1,0:T(8,128)S(1)} %get-tuple-element.30.refs_2_, f32[5,16,32,128]{3,2,1,0:T(8,128)S(1)} %get-tuple-element.31.refs_3_), custom_call_target="tpu_custom_call" | custom-call | flops 2750000128 | bytes 2621440 | tf_op jit(solution)/shard_map/pallas_call | solution.py:627
  14.0 0.0 copy-start.2
  14.0 0.0 copy-start.5
  14.1 0.0 copy-start.1
  14.1 0.0 copy-start.4
  14.1 1.9 %shard_map.122.refs_1_ = f32[5,16,32,128]{3,2,1,0:T(8,128)S(1)} custom-call(f32[5,5]{1,0:T(8,128)S(1)} %copy-done.3, f32[5,16,32,128]{3,2,1,0:T(8,128)S(1)} %get-tuple-element.28.refs_1_, f32[16,32,128]{2,1,0:T(8,128)S(1)} %get-tuple-element.29.refs_2_.refs_3_, f32[5,16,32,128]{3,2,1,0:T(8,128)S(1)} %shard_map.121.refs_3_.refs_1_), custom_call_target="tpu_custom_call" | custom-call | flops 2750000128 | bytes 2621440 | tf_op jit(solution)/shard_map/pallas_call | solution.py:627
  16.0 0.1 shard_map.125
  16.1 0.1 collective-permute-start.3
  16.2 0.7 %shard_map.123.refs_1_ = f32[5,32,128]{2,1,0:T(8,128)S(1)} custom-call(f32[2,5,16,64]{3,2,1,0:T(8,128)S(1)} %bitcast.3, f32[5,56,128]{2,1,0:T(8,128)S(1)} %collective-permute-done.2.refs_1_.refs_2_.refs_6_.refs_5_, s32[2,16]{1,0:T(2,128)S(1)} %copy-done.4), custom_call_target="tpu_custom_call" | custom-call | flops 770000000 | bytes 163840 | tf_op jit(solution)/shard_map/pallas_call | solution.py:627
  16.9 0.9 %shard_map.124.refs_8_.refs_6_.refs_7_ = f32[5,16,32,128]{3,2,1,0:T(8,128)S(1)} custom-call(s32[1]{0:T(128)S(6)} %copy.21.refs_0_, f32[5,32,128]{2,1,0:T(8,128)S(1)} %shard_map.123.refs_1_), custom_call_target="tpu_custom_call" | custom-call | flops 770000000 | bytes 2621440 | tf_op jit(solution)/shard_map/pallas_call | solution.py:627
  17.8 3.0 %shard_map.126 = (f32[5,16,32,128]{3,2,1,0:T(8,128)S(1)}, f32[5,16,32,128]{3,2,1,0:T(8,128)S(1)}, f32[2,2,5,32,128]{4,3,2,1,0:T(8,128)S(1)}, f32[2,2,5,32,128]{4...) custom-call(s32[1]{0:T(128)S(6)} %copy.21.refs_0_, ...), custom_call_target="tpu_custom_call" | custom-call | flops 3300000000 | bytes 7168000 | tf_op jit(solution)/shard_map/pallas_call | solution.py:627
  20.8 1.2 %collective-permute-start.4 = (f32[5,32,128]{2,1,0:T(8,128)S(1)}, f32[5,32,128]{2,1,0:T(8,128)S(1)}, u32[]{:S(2)}, u32[]{:S(2)}) collective-permute-start(f32[5,32,128]{2,1,0:T(8,128)S(1)} %get-tuple-element.40.refs_2_.refs_0_), channel_id=1, source_target_pairs={{0,4},{2,6},{4,0},{6,2},{8,12},{10,14},{12,8},{14,10},{16,20},{18,... | collective-permute-start | bytes 245768 | tf_op jit(solution)/shard_map/ppermute | solution.py:667
  22.1 0.9 %collective-permute-start.6 = (f32[6,32,128]{2,1,0:T(8,128)S(1)}, f32[6,32,128]{2,1,0:T(8,128)S(1)}, u32[]{:S(2)}, u32[]{:S(2)}) collective-permute-start(f32[6,32,128]{2,1,0:T(8,128)S(1)} %shard_map.127.refs_10_.refs_0_), channel_id=1, source_target_pairs={{0,4},{2,6},{4,0},{6,2},{8,12},{10,14},{12,8},{14,10},{16,20},{18,... | collective-permute-start | bytes 294920 | tf_op jit(solution)/shard_map/ppermute | solution.py:667
  23.0 1.7 %shard_map.128 = (f32[5,16,32,128]{3,2,1,0:T(8,128)S(1)}, f32[2,2,5,32,128]{4,3,2,1,0:T(8,128)S(1)}, f32[2,2,5,32,128]{4,3,2,1,0:T(8,128)S(1)}, f32[5,56,128]{2,1,0:T(8,128)S(1)}) custom-call(s32[1]{0:T(128)S(6)} %copy.21.refs_0_, f32[5,16,32,128]{3,2,1,0:T(8,128)S(1)} %shard_map.122.refs_1_, ...), custom_call_target="tpu_custom_call", output_to_operand_aliasing={{1}: (7, {}), {2}: (8, {}), {3}: (9, {})} | custom-call | flops 2750000128 | bytes 4218880 | tf_op jit(solution)/shard_map/pallas_call | solution.py:627
  24.7 0.7 %shard_map.129 = (f32[5,16,128]{2,1,0:T(8,128)S(1)}, f32[5,56,128]{2,1,0:T(8,128)S(1)}) custom-call(f32[5,32,128]{2,1,0:T(8,128)S(1)} %get-tuple-element.42.refs_0_, s32[2,16]{1,0:T(2,128)S(1)} %copy-done.4, f32[5,56,128]{2,1,0:T(8,128)S(1)} %get-tuple-element.43.refs_2_), custom_call_target="tpu_custom_call", output_to_operand_aliasing={{1}: (2, {})} | custom-call | flops 660000000 | bytes 368640 | tf_op jit(solution)/shard_map/pallas_call | solution.py:627
  25.4 0.6 %collective-permute-start.9 = (f32[5,56,128]{2,1,0:T(8,128)S(1)}, f32[5,56,128]{2,1,0:T(8,128)S(1)}, u32[]{:S(2)}, u32[]{:S(2)}) collective-permute-start(f32[5,56,128]{2,1,0:T(8,128)S(1)} %get-tuple-element.49), channel_id=1, source_target_pairs={{0,1},{1,0},{2,3},{3,2},{4,5},{5,4},{6,7},{7,6},{8,9},{9,8},{10,11... | collective-permute-start | bytes 430088 | tf_op jit(solution)/shard_map/ppermute | solution.py:671
  26.0 3.9 %collective-permute-start.8 = (f32[2,2,5,32,128]{4,3,2,1,0:T(8,128)S(1)}, f32[2,2,5,32,128]{4,3,2,1,0:T(8,128)S(1)}, u32[]{:S(2)}, u32[]{:S(2)}) collective-permute-start(f32[2,2,5,32,128]{4,3,2,1,0:T(8,128)S(1)} %get-tuple-element.48), channel_id=1, source_target_pairs={{0,30},{2,4},{4,2},{6,8},{8,6},{10,12},{12,10},{14,16},{16,14},{18... | collective-permute-start | bytes 983048 | tf_op jit(solution)/shard_map/ppermute | solution.py:802
  29.8 0.1 collective-permute-start.5
  30.0 2.1 %collective-permute-start.10 = (f32[6,32,128]{2,1,0:T(8,128)S(1)}, f32[6,32,128]{2,1,0:T(8,128)S(1)}, u32[]{:S(2)}, u32[]{:S(2)}) collective-permute-start(f32[6,32,128]{2,1,0:T(8,128)S(1)} %shard_map.131.refs_5_.refs_0_), channel_id=1, source_target_pairs={{0,8},{2,10},{4,12},{6,14},{8,0},{10,2},{12,4},{14,6},{16,24},{18,... | collective-permute-start | bytes 294920 | tf_op jit(solution)/shard_map/ppermute | solution.py:667
  32.0 1.9 %shard_map.132.refs_2_.refs_0_ = f32[5,16,32,128]{3,2,1,0:T(8,128)S(1)} custom-call(s32[1]{0:T(128)S(6)} %copy.21.refs_0_, f32[5,5]{1,0:T(8,128)S(1)} %copy-done.3, f32[5,16,32,128]{3,2,1,0:T(8,128)S(1)} %get-tuple-element.45.refs_2_, f32[5,16,32,128]{3,2,1,0:T(8,128)S(1)} %get-tuple-element.46.refs_3_, f32[5,32,128]{2,1,0:T(8,128)S(1)} %shard_map.130.refs_4_.refs_0_, ...), custom_call_target="tpu_custom_call" | custom-call | flops 2750000128 | bytes 2621440 | tf_op jit(solution)/shard_map/pallas_call | solution.py:627
  33.9 3.2 %collective-permute-done.5.refs_1_ = f32[5,32,128]{2,1,0:T(8,128)S(1)} collective-permute-done((f32[5,32,128]{2,1,0:T(8,128)S(1)}, f32[5,32,128]{2,1,0:T(8,128)S(1)}, u32[]{:S(2)}, u32[]{:S(2)}) %collective-permute-start.5) | collective-permute-done | bytes 81952 | tf_op jit(solution)/shard_map/ppermute | solution.py:667
  37.2 2.6 %collective-permute-start.12 = (f32[5,32,128]{2,1,0:T(8,128)S(1)}, f32[5,32,128]{2,1,0:T(8,128)S(1)}, u32[]{:S(2)}, u32[]{:S(2)}) collective-permute-start(f32[5,32,128]{2,1,0:T(8,128)S(1)} %shard_map.133.refs_3_.refs_0_), channel_id=1, source_target_pairs={{0,16},{2,18},{4,20},{6,22},{8,24},{10,26},{12,28},{14,30},{16,0},... | collective-permute-start | bytes 245768 | tf_op jit(solution)/shard_map/ppermute | solution.py:667
  39.8 1.9 %shard_map.134.refs_2_ = f32[5,16,32,128]{3,2,1,0:T(8,128)S(1)} custom-call(f32[5,5]{1,0:T(8,128)S(1)} %copy-done.3, f32[5,16,32,128]{3,2,1,0:T(8,128)S(1)} %get-tuple-element.41.refs_1_, f32[16,32,128]{2,1,0:T(8,128)S(1)} %get-tuple-element.29.refs_2_.refs_3_, f32[5,32,128]{2,1,0:T(8,128)S(1)} %shard_map.133.refs_3_.refs_0_), custom_call_target="tpu_custom_call" | custom-call | flops 2750000128 | bytes 2621440 | tf_op jit(solution)/shard_map/pallas_call | solution.py:627
  41.7 0.1 collective-permute-start.11
  41.8 1.8 %shard_map.137 = (f32[5,32,16,128]{3,2,1,0:T(8,128)}, f32[2,5,16,64]{3,2,1,0:T(8,128)}) custom-call(f32[5,16,32,128]{3,2,1,0:T(8,128)S(1)} %shard_map.132.refs_2_.refs_0_, f32[2,2,5,32,128]{4,3,2,1,0:T(8,128)S(1)} %collective-permute-done.7.refs_4_.refs_1_, f32[2,2,5,32,128]{4,3,2,1,0:T(8,128)S(1)} %collective-permute-done.8.refs_5_.refs_2_, ...), custom_call_target="tpu_custom_call" | custom-call | flops 2750000128 | bytes 2703360 | tf_op jit(solution)/shard_map/pallas_call | solution.py:627
  43.6 1.3 %copy-done = f32[5,32,16,128]{3,2,1,0:T(8,128)S(1)} copy-done((f32[5,32,16,128]{3,2,1,0:T(8,128)S(1)}, f32[5,32,16,128]{3,2,1,0:T(8,128)}, u32[]{:S(2)}) %copy-start) | copy-done | bytes 1310744
  44.9 0.5 %collective-permute-start.13 = (f32[5,32,128]{2,1,0:T(8,128)S(1)}, f32[5,32,128]{2,1,0:T(8,128)S(1)}, u32[]{:S(2)}, u32[]{:S(2)}) collective-permute-start(f32[5,32,128]{2,1,0:T(8,128)S(1)} %shard_map.138.refs_0_), channel_id=1, source_target_pairs={{0,2},{2,0},{4,6},{6,4},{8,10},{10,8},{12,14},{14,12},{16,18},{18,... | collective-permute-start | bytes 245768 | tf_op jit(solution)/shard_map/ppermute | solution.py:667
  45.5 3.3 %shard_map.136 = f32[5,32,16,128]{3,2,1,0:T(8,128)} custom-call(s32[1]{0:T(128)S(6)} %copy.21.refs_0_, f32[5,5]{1,0:T(8,128)S(1)} %copy-done.3, f32[5,16,32,128]{3,2,1,0:T(8,128)S(1)} %shard_map.134.refs_2_, f32[16,32,128]{2,1,0:T(8,128)S(1)} %get-tuple-element.29.refs_2_.refs_3_, f32[2,2,5,32,128]{4,3,2,1,0:T(8,128)S(1)} %collective-permute-done.7.refs_4_.refs_1_, ...), custom_call_target="tpu_custom_call" | custom-call | flops 3300000000 | bytes 2621440 | tf_op jit(solution)/shard_map/pallas_call | solution.py:627
  48.8 0.7 %shard_map.139 = f32[2,5,8,128]{3,2,1,0:T(8,128)} custom-call(f32[5,32,128]{2,1,0:T(8,128)S(1)} %shard_map.138.refs_0_, f32[5,32,128]{2,1,0:T(8,128)S(1)} %collective-permute-done.13.refs_1_, s32[2,128]{1,0:T(2,128)S(1)} %copy-done.5), custom_call_target="tpu_custom_call" | custom-call | flops 770000000 | bytes 81920 | tf_op jit(solution)/shard_map/pallas_call | solution.py:627
  (28 shorter events, 0.1 us)
Async XLA Ops:
  1.3 10.8 %copy-start.3 = (f32[5,5]{1,0:T(8,128)S(1)}, f32[5,5]{1,0:T(8,128)}, u32[]{:S(2)}) copy-start(f32[5,5]{1,0:T(8,128)} %refs_1_.11) | copy-start | bytes 304
  4.4 11.5 %collective-permute-start.2 = (f32[5,56,128]{2,1,0:T(8,128)S(1)}, f32[5,56,128]{2,1,0:T(8,128)S(1)}, u32[]{:S(2)}, u32[]{:S(2)}) collective-permute-start(f32[5,56,128]{2,1,0:T(8,128)S(1)} %get-tuple-element.34), channel_id=1, source_target_pairs={{0,1},{1,0},{2,3},{3,2},{4,5},{5,4},{6,7},{7,6},{8,9},{9,8},{10,11... | collective-permute-start | bytes 430088 | tf_op jit(solution)/shard_map/ppermute | solution.py:671
  7.4 10.3 %collective-permute-start = (f32[2,2,5,32,128]{4,3,2,1,0:T(8,128)S(1)}, f32[2,2,5,32,128]{4,3,2,1,0:T(8,128)S(1)}, u32[]{:S(2)}, u32[]{:S(2)}) collective-permute-start(f32[2,2,5,32,128]{4,3,2,1,0:T(8,128)S(1)} %get-tuple-element.32), channel_id=1, source_target_pairs={{0,2},{2,0},{4,6},{6,4},{8,10},{10,8},{12,14},{14,12},{16,18},{18,... | collective-permute-start | bytes 983048 | tf_op jit(solution)/shard_map/ppermute | solution.py:711
  7.4 10.3 %collective-permute-start.1 = (f32[2,2,5,32,128]{4,3,2,1,0:T(8,128)S(1)}, f32[2,2,5,32,128]{4,3,2,1,0:T(8,128)S(1)}, u32[]{:S(2)}, u32[]{:S(2)}) collective-permute-start(f32[2,2,5,32,128]{4,3,2,1,0:T(8,128)S(1)} %get-tuple-element.33), channel_id=1, source_target_pairs={{0,30},{2,4},{4,2},{6,8},{8,6},{10,12},{12,10},{14,16},{16,14},{18... | collective-permute-start | bytes 983048 | tf_op jit(solution)/shard_map/ppermute | solution.py:710
  14.0 1.9 %copy-start.2 = (f32[2,5,8,128]{3,2,1,0:T(8,128)S(1)}, f32[2,5,8,128]{3,2,1,0:T(8,128)}, u32[]{:S(2)}) copy-start(f32[2,5,8,128]{3,2,1,0:T(8,128)} %refs_0_.11) | copy-start | bytes 122884
  14.0 1.9 %copy-start.5 = (s32[2,128]{1,0:T(2,128)S(1)}, s32[2,128]{1,0:T(2,128)}, u32[]{:S(2)}) copy-start(s32[2,128]{1,0:T(2,128)} %refs_2_.5) | copy-start | bytes 3076
  14.1 2.1 %copy-start.1 = (f32[2,5,64,16]{2,3,1,0:T(8,128)S(1)}, f32[2,5,64,16]{2,3,1,0:T(8,128)}, u32[]{:S(2)}) copy-start(f32[2,5,64,16]{2,3,1,0:T(8,128)} %param.14) | copy-start | bytes 122884
  14.1 2.1 %copy-start.4 = (s32[2,16]{1,0:T(2,128)S(1)}, s32[2,16]{1,0:T(2,128)}, u32[]{:S(2)}) copy-start(s32[2,16]{1,0:T(2,128)} %refs_1_.9) | copy-start | bytes 388
  16.1 5.9 %collective-permute-start.3 = (f32[6,32,128]{2,1,0:T(8,128)S(1)}, f32[6,32,128]{2,1,0:T(8,128)S(1)}, u32[]{:S(2)}, u32[]{:S(2)}) collective-permute-start(f32[6,32,128]{2,1,0:T(8,128)S(1)} %get-tuple-element.39), channel_id=1, source_target_pairs={{0,16},{2,18},{4,20},{6,22},{8,24},{10,26},{12,28},{14,30},{16,0},... | collective-permute-start | bytes 294920 | tf_op jit(solution)/shard_map/ppermute | solution.py:667
  20.8 9.0 %collective-permute-start.4 = (f32[5,32,128]{2,1,0:T(8,128)S(1)}, f32[5,32,128]{2,1,0:T(8,128)S(1)}, u32[]{:S(2)}, u32[]{:S(2)}) collective-permute-start(f32[5,32,128]{2,1,0:T(8,128)S(1)} %get-tuple-element.40.refs_2_.refs_0_), channel_id=1, source_target_pairs={{0,4},{2,6},{4,0},{6,2},{8,12},{10,14},{12,8},{14,10},{16,20},{18,... | collective-permute-start | bytes 245768 | tf_op jit(solution)/shard_map/ppermute | solution.py:667
  22.1 7.9 %collective-permute-start.6 = (f32[6,32,128]{2,1,0:T(8,128)S(1)}, f32[6,32,128]{2,1,0:T(8,128)S(1)}, u32[]{:S(2)}, u32[]{:S(2)}) collective-permute-start(f32[6,32,128]{2,1,0:T(8,128)S(1)} %shard_map.127.refs_10_.refs_0_), channel_id=1, source_target_pairs={{0,4},{2,6},{4,0},{6,2},{8,12},{10,14},{12,8},{14,10},{16,20},{18,... | collective-permute-start | bytes 294920 | tf_op jit(solution)/shard_map/ppermute | solution.py:667
  25.4 16.4 %collective-permute-start.9 = (f32[5,56,128]{2,1,0:T(8,128)S(1)}, f32[5,56,128]{2,1,0:T(8,128)S(1)}, u32[]{:S(2)}, u32[]{:S(2)}) collective-permute-start(f32[5,56,128]{2,1,0:T(8,128)S(1)} %get-tuple-element.49), channel_id=1, source_target_pairs={{0,1},{1,0},{2,3},{3,2},{4,5},{5,4},{6,7},{7,6},{8,9},{9,8},{10,11... | collective-permute-start | bytes 430088 | tf_op jit(solution)/shard_map/ppermute | solution.py:671
  26.0 15.8 %collective-permute-start.7 = (f32[2,2,5,32,128]{4,3,2,1,0:T(8,128)S(1)}, f32[2,2,5,32,128]{4,3,2,1,0:T(8,128)S(1)}, u32[]{:S(2)}, u32[]{:S(2)}) collective-permute-start(f32[2,2,5,32,128]{4,3,2,1,0:T(8,128)S(1)} %get-tuple-element.47), channel_id=1, source_target_pairs={{0,2},{2,0},{4,6},{6,4},{8,10},{10,8},{12,14},{14,12},{16,18},{18,... | collective-permute-start | bytes 983048 | tf_op jit(solution)/shard_map/ppermute | solution.py:803
  26.0 15.8 %collective-permute-start.8 = (f32[2,2,5,32,128]{4,3,2,1,0:T(8,128)S(1)}, f32[2,2,5,32,128]{4,3,2,1,0:T(8,128)S(1)}, u32[]{:S(2)}, u32[]{:S(2)}) collective-permute-start(f32[2,2,5,32,128]{4,3,2,1,0:T(8,128)S(1)} %get-tuple-element.48), channel_id=1, source_target_pairs={{0,30},{2,4},{4,2},{6,8},{8,6},{10,12},{12,10},{14,16},{16,14},{18... | collective-permute-start | bytes 983048 | tf_op jit(solution)/shard_map/ppermute | solution.py:802
  29.8 7.3 %collective-permute-start.5 = (f32[5,32,128]{2,1,0:T(8,128)S(1)}, f32[5,32,128]{2,1,0:T(8,128)S(1)}, u32[]{:S(2)}, u32[]{:S(2)}) collective-permute-start(f32[5,32,128]{2,1,0:T(8,128)S(1)} %shard_map.130.refs_4_.refs_0_), channel_id=1, source_target_pairs={{0,8},{2,10},{4,12},{6,14},{8,0},{10,2},{12,4},{14,6},{16,24},{18,... | collective-permute-start | bytes 245768 | tf_op jit(solution)/shard_map/ppermute | solution.py:667
  30.0 11.7 %collective-permute-start.10 = (f32[6,32,128]{2,1,0:T(8,128)S(1)}, f32[6,32,128]{2,1,0:T(8,128)S(1)}, u32[]{:S(2)}, u32[]{:S(2)}) collective-permute-start(f32[6,32,128]{2,1,0:T(8,128)S(1)} %shard_map.131.refs_5_.refs_0_), channel_id=1, source_target_pairs={{0,8},{2,10},{4,12},{6,14},{8,0},{10,2},{12,4},{14,6},{16,24},{18,... | collective-permute-start | bytes 294920 | tf_op jit(solution)/shard_map/ppermute | solution.py:667
  37.2 6.4 %collective-permute-start.12 = (f32[5,32,128]{2,1,0:T(8,128)S(1)}, f32[5,32,128]{2,1,0:T(8,128)S(1)}, u32[]{:S(2)}, u32[]{:S(2)}) collective-permute-start(f32[5,32,128]{2,1,0:T(8,128)S(1)} %shard_map.133.refs_3_.refs_0_), channel_id=1, source_target_pairs={{0,16},{2,18},{4,20},{6,22},{8,24},{10,26},{12,28},{14,30},{16,0},... | collective-permute-start | bytes 245768 | tf_op jit(solution)/shard_map/ppermute | solution.py:667
  41.7 3.8 %collective-permute-start.11 = (f32[6,32,128]{2,1,0:T(8,128)S(1)}, f32[6,32,128]{2,1,0:T(8,128)S(1)}, u32[]{:S(2)}, u32[]{:S(2)}) collective-permute-start(f32[6,32,128]{2,1,0:T(8,128)S(1)} %shard_map.135.refs_8_.refs_5_), channel_id=1, source_target_pairs={{0,2},{2,0},{4,6},{6,4},{8,10},{10,8},{12,14},{14,12},{16,18},{18,... | collective-permute-start | bytes 294920 | tf_op jit(solution)/shard_map/ppermute | solution.py:667
  43.6 1.3 %copy-start = (f32[5,32,16,128]{3,2,1,0:T(8,128)S(1)}, f32[5,32,16,128]{3,2,1,0:T(8,128)}, u32[]{:S(2)}) copy-start(f32[5,32,16,128]{3,2,1,0:T(8,128)} %get-tuple-element.25.refs_2_) | copy-start | bytes 3932164
  44.9 3.8 %collective-permute-start.13 = (f32[5,32,128]{2,1,0:T(8,128)S(1)}, f32[5,32,128]{2,1,0:T(8,128)S(1)}, u32[]{:S(2)}, u32[]{:S(2)}) collective-permute-start(f32[5,32,128]{2,1,0:T(8,128)S(1)} %shard_map.138.refs_0_), channel_id=1, source_target_pairs={{0,2},{2,0},{4,6},{6,4},{8,10},{10,8},{12,14},{14,12},{16,18},{18,... | collective-permute-start | bytes 245768 | tf_op jit(solution)/shard_map/ppermute | solution.py:667

commit v2 on v1

--- a/solution.py
+++ b/solution.py
@@ -89,14 +89,6 @@
     return jnp.dot(
         jnp.concatenate([high, low], axis=1), band[...], preferred_element_type=f32
     )
-
-
-def lap_inside(cells, lane_part, x):
-    count = len(cells)
-    ones = [cells[x + i] for i in (-1, 1) if 0 <= x + i < count]
-    twos = [cells[x + i] for i in (-2, 2) if 0 <= x + i < count]
-    total = lane_part + 16.0 * functools.reduce(jnp.add, ones) - functools.reduce(jnp.add, twos)
-    return total * (1.0 / 12.0)
 
 
 def pack_lanes(x, base, values, packed):
@@ -317,23 +309,19 @@
         my[f, g.K + g.X : g.K + g.X + span, :] = total
 
 
-class Column:
-    def __init__(self, ref, f, rows, count):
-        self.ref, self.f, self.rows, self.count = ref, f, rows, count
-
-    def __len__(self):
-        return self.count
-
-    def __getitem__(self, x):
-        return self.ref[self.f, x, self.rows, :]
-
-
-def lane_parts(g, source, rows, band, parts):
+def fill_laps(g, source, rows, band, laps):
     for f in range(g.F):
-        parts[f] = along_lanes(source[f, :, rows, :].reshape(8 * g.X, 128), band)
-
-
-def adjoint_inside_kernel(g, scaled, relax, mix, ps, qs, out, rx, band, parts):
+        cells = source[f, :, rows, :]
+        parts = along_lanes(cells.reshape(8 * g.X, 128), band)
+        for x in range(g.X):
+            ones = [cells[x + i] for i in (-1, 1) if 0 <= x + i < g.X]
+            twos = [cells[x + i] for i in (-2, 2) if 0 <= x + i < g.X]
+            total = parts[8 * x : 8 * x + 8] + 16.0 * functools.reduce(jnp.add, ones)
+            total = total - functools.reduce(jnp.add, twos)
+            laps[f, x] = total * (1.0 / 12.0)
+
+
+def adjoint_inside_kernel(g, scaled, relax, mix, ps, qs, out, rx, band, laps):
     width = relax[0]
     table = mix_table(mix, True)
     fill_band(band)
@@ -343,33 +331,31 @@
 
     def tile_step(tile, carry):
         rows = rows_of(tile)
-        lane_parts(g, qs, rows, band, parts)
+        fill_laps(g, qs, rows, band, laps)
         for x in range(g.X):
             p = [ps[f, x, rows, :] for f in range(g.F)]
             if scaled:
                 open_xy = open_y * (1.0 - rx[x])
                 p = [open_xy * value for value in p]
             for f in range(g.F):
-                lap = lap_inside(Column(qs, f, rows, g.X), parts[f, 8 * x : 8 * x + 8, :], x)
-                out[f, x, rows, :] = mixed(table, f, p) + lap
+                out[f, x, rows, :] = mixed(table, f, p) + laps[f, x]
         return carry
 
     lax.fori_loop(0, g.tiles, tile_step, 0)
 
 
-def forward_inside_kernel(g, mix, ut, dt, out, band, parts):
+def forward_inside_kernel(g, mix, ut, dt, out, band, laps):
     table = mix_table(mix, False)
     fill_band(band)
 
     def tile_step(tile, carry):
         rows = rows_of(tile)
-        lane_parts(g, ut, rows, band, parts)
+        fill_laps(g, ut, rows, band, laps)
         for x in range(g.X):
             u = [ut[f, x, rows, :] for f in range(g.F)]
             d = dt[x, rows, :]
             for f in range(g.F):
-                lap = lap_inside(Column(ut, f, rows, g.X), parts[f, 8 * x : 8 * x + 8, :], x)
-                out[f, x, rows, :] = mixed(table, f, u) + d * lap
+                out[f, x, rows, :] = mixed(table, f, u) + d * laps[f, x]
         return carry
 
     lax.fori_loop(0, g.tiles, tile_step, 0)
@@ -466,9 +452,10 @@
 
 
 def forward_last_kernel(
-    g, relax, mix, inside, dt, fa, fb, fy, sides, kept, swapped, out, rx, lx
+    g, relax, mix, inside, dt, fa, fb, fy, sides, kept, swapped, out, mark, rx, lx
 ):
     width = relax[0]
+    mark[...] = jnp.zeros((8, 128), f32)
     for x in range(-2, g.X + 2):
         rx[x + 2] = ramp_x(g, width, x)
     for x in range(g.X):
@@ -583,6 +570,20 @@
     for i in range(g.F + 1):
         keep[i] = jnp.where(odd, parts[1][i], parts[0][i])
         send[i] = jnp.where(odd, parts[0][i], parts[1][i])
+
+
+def join_kernel(g, sums, bounds, more_bounds, out):
+    for f in range(g.F):
+        out[f] = sums[f]
+    for f in range(g.F + 1):
+        out[g.F + f] = bounds[f] + more_bounds[f]
+
+
+def split_kernel(g, state, moved, sums, bounds):
+    for f in range(g.F):
+        sums[f] = state[f] + moved[f]
+    for f in range(g.F + 1):
+        bounds[f] = state[g.F + f] + moved[g.F + f]
 
 
 def add_kernel(g, first, second, out):
@@ -658,7 +659,7 @@
     edge_shape = (F, K, 128)
     ramps = (X, 8, 128)
     band = pltpu.VMEM((256, 128), jnp.bfloat16)
-    parts = (F, 8 * X, 128)
+    laps = (F, X, 8, 128)
 
     def bind(kernel, *args):
         return functools.partial(kernel, g, *args)
@@ -707,21 +708,21 @@
         ],
         3,
     )
+    fy = to_y(my)
+    fa = lax.ppermute(ma, "gx", evens)
     fb = lax.ppermute(mb, "gx", odds)
-    fa = lax.ppermute(ma, "gx", evens)
-    fy = to_y(my)
 
     (inside_a,) = call(
         bind(adjoint_inside_kernel, True),
         [block],
-        [ramps, band, parts],
+        [ramps, band, laps],
         [("s", relax_width), ("s", field_mix), ("v", at), ("v", qt)],
         2.5,
     )
     (inside_u,) = call(
         bind(forward_inside_kernel),
         [block],
-        [band, parts],
+        [band, laps],
         [("s", field_mix), ("v", ut), ("v", dt)],
         2.5,
         after=[inside_a],
@@ -734,7 +735,6 @@
         0.3,
     )
     first_bounds = swapped(send, nx // 2)
-
     if g.pair:
         (bsn,) = call(
             bind(side_bounds_kernel),
@@ -765,9 +765,14 @@
         3,
         after=[keep, sides],
     )
-    first_sums = swapped(dwe, 2)
-    bounds = add(keep, first_bounds, [dwe])
-    second_bounds = swapped(bounds, 2)
+    (state,) = call(
+        bind(join_kernel),
+        [(2 * F + 1, K, 128)],
+        [],
+        [("v", dwe), ("v", keep), ("v", first_bounds)],
+        0.1,
+    )
+    moved = swapped(state, 2)
     u1, ma, mb, my = call(
         bind(forward_first_kernel),
         [block, row_shape, row_shape, lane_shape],
@@ -786,7 +791,7 @@
         ],
         2.5,
         {7: 1, 8: 2, 9: 3},
-        after=[bounds],
+        after=[state],
     )
     if g.pair:
         gsn_own, my = call(
@@ -799,55 +804,45 @@
         )
     else:
         gsn_own = dsn
+    fy = to_y(my)
+    fa = lax.ppermute(ma, "gx", evens)
     fb = lax.ppermute(mb, "gx", odds)
-    fa = lax.ppermute(ma, "gx", evens)
-    fy = to_y(my)
-
-    sums = add(dwe, first_sums, [gsn_own])
-    second_sums = swapped(sums, 4)
-    bounds = add(bounds, second_bounds, [gsn_own])
-    third_bounds = swapped(bounds, 4)
+
+    state = add(state, moved, [gsn_own])
+    distance = 4
+    while distance < nx // 4:
+        state = state + swapped(state, distance)
+        distance *= 2
+    moved = swapped(state, distance)
     (inside_a,) = call(
         bind(adjoint_inside_kernel, False),
         [block],
-        [ramps, band, parts],
+        [ramps, band, laps],
         [("s", relax_width), ("s", field_mix), ("v", p1), ("v", q1)],
         2.5,
-        after=[sums, bounds],
-    )
-    sums = add(sums, second_sums, [inside_a])
-    third_sums = swapped(sums, 8)
+        after=[state],
+    )
     (inside_u,) = call(
         bind(forward_inside_kernel),
         [block],
-        [band, parts],
+        [band, laps],
         [("s", field_mix), ("v", u1), ("v", dt)],
         2.5,
-        after=[sums],
-    )
-    bounds = add(bounds, third_bounds, [inside_u])
-    distance = 8
-    while distance < nx // 2:
-        bounds = bounds + swapped(bounds, distance)
-        distance *= 2
+        after=[inside_a],
+    )
+    sums, bounds = call(
+        bind(split_kernel),
+        [edge_shape, (F + 1, K, 128)],
+        [],
+        [("v", state), ("v", moved)],
+        0.1,
+        after=[inside_u],
+    )
     other_bounds = swapped(bounds, 1)
-    grad_state, grad_sn = call(
-        bind(adjoint_last_kernel),
-        [child_state.shape, sn_turned.shape],
-        [],
-        [("v", inside_a), ("v", fa), ("v", fb), ("v", fy), ("v", gsn_own)],
-        2.5,
-        after=[bounds],
-    )
-    sums = add(sums, third_sums, [grad_state])
-    distance = 16
-    while distance < nx:
-        sums = sums + swapped(sums, distance)
-        distance *= 2
-    other_sums = swapped(sums, 1)
-    (child_final,) = call(
+    moved = swapped(sums, nx // 2)
+    child_final, mark = call(
         bind(forward_last_kernel),
-        [child_state.shape],
+        [child_state.shape, (8, 128)],
         [(X + 4, 8, 128), ramps],
         [
             ("s", relax_width),
@@ -862,6 +857,16 @@
             ("v", other_bounds),
         ],
         3,
+    )
+    sums = add(sums, moved, [mark])
+    other_sums = swapped(sums, 1)
+    grad_state, grad_sn = call(
+        bind(adjoint_last_kernel),
+        [child_state.shape, sn_turned.shape],
+        [],
+        [("v", inside_a), ("v", fa), ("v", fb), ("v", fy), ("v", gsn_own)],
+        2.5,
+        after=[sums],
     )
     (grad_we,) = call(
         bind(spread_kernel),

time: 49.6 us -> 47.7 us (0.962)
  starting transfers between devices: 19.7 us -> 15.7 us
  waiting for transfers between devices: 3.27 us -> 6.66 us
  local copies, waits for them, and re-layouts: 1.35 us -> 0.03 us
    ppermute x8 -> x6, starting transfers between devices: 7.57 us -> 2.97 us  [swapped(): return lax.ppermute(values, 'gx', [(i, i ^ distance) for i in range(nx)])]
    ppermute x8 -> x6, waiting for transfers between devices: 3.26 us -> 6.64 us  [swapped(): return lax.ppermute(values, 'gx', [(i, i ^ distance) for i in range(nx)])]
    unnamed x12 -> x10, local copies, waits for them, and re-layouts: 1.35 us -> 0.03 us
    ppermute x2, starting transfers between devices: 8.53 us -> 9.06 us  [body(): fb = lax.ppermute(mb, 'gx', odds)]
    pallas_call x20 -> x18, Pallas kernels: 23.6 us -> 23.5 us  [call(): pl.pallas_call(run, out_shape=out_shape, in_specs=[places[where] for wher...]
  transfers between devices with their start and end apart: 14 -> 12, of which waited for: 1 -> 3; matrix products, arithmetic and copies ran while one was open for 0% -> 0% of each run, Pallas kernels for 40% -> 41%
where the time goes in v2:
time: 47.7 us; the launch traced here: 47.5 us
  Pallas kernels  23.5 us (49%)
  starting transfers between devices  15.7 us (33%)
  waiting for transfers between devices  6.66 us (14%)
  between operations  1.49 us (3%)
    pallas_call x18, Pallas kernels, call(): pl.pallas_call(run, out_shape=out_shape, in_specs=[places[where] for wher...  23.5 us
    ppermute x2, starting transfers between devices, body(): fb = lax.ppermute(mb, 'gx', odds)  9.06 us
    ppermute x6, waiting for transfers between devices, swapped(): return lax.ppermute(values, 'gx', [(i, i ^ distance) for i in range(nx)])  6.64 us
    ppermute x2, starting transfers between devices, to_y(): return lax.ppermute(message, 'gy', [(0, 1), (1, 0)])  3.7 us
    ppermute x6, starting transfers between devices, swapped(): return lax.ppermute(values, 'gx', [(i, i ^ distance) for i in range(nx)])  2.97 us
  transfers between devices with their start and end apart: 12, of which 3 were waited for; matrix products, arithmetic and copies ran while one was open for 0% of the time, Pallas kernels for 41%

profile of v2, /device:TPU:0, one launch (start us, length us, event | category | flops | bytes accessed | tf_op | source)
XLA Modules:
  0.0 47.5 jit_solution(11893854054962783677)
XLA Ops:
  1.3 3.1 %shard_map.120 = (f32[5,16,32,128]{3,2,1,0:T(8,128)S(1)}, f32[5,16,32,128]{3,2,1,0:T(8,128)S(1)}, f32[16,32,128]{2,1,0:T(8,128)S(1)}, f32[5,16,32,128]{3,2,1,0:T...) custom-call(s32[1]{0:T(128)S(6)} %copy.21.refs_0_, ...), custom_call_target="tpu_custom_call" | custom-call | flops 3300000000 | bytes 9986048 | tf_op jit(solution)/shard_map/pallas_call | solution.py:628
  4.4 3.0 %collective-permute-start.2 = (f32[5,56,128]{2,1,0:T(8,128)S(1)}, f32[5,56,128]{2,1,0:T(8,128)S(1)}, u32[]{:S(2)}, u32[]{:S(2)}) collective-permute-start(f32[5,56,128]{2,1,0:T(8,128)S(1)} %get-tuple-element.38), channel_id=1, source_target_pairs={{0,1},{1,0},{2,3},{3,2},{4,5},{5,4},{6,7},{7,6},{8,9},{9,8},{10,11... | collective-permute-start | bytes 430088 | tf_op jit(solution)/shard_map/ppermute | solution.py:672
  7.4 4.7 %collective-permute-start.1 = (f32[2,2,5,32,128]{4,3,2,1,0:T(8,128)S(1)}, f32[2,2,5,32,128]{4,3,2,1,0:T(8,128)S(1)}, u32[]{:S(2)}, u32[]{:S(2)}) collective-permute-start(f32[2,2,5,32,128]{4,3,2,1,0:T(8,128)S(1)} %get-tuple-element.37), channel_id=1, source_target_pairs={{0,30},{2,4},{4,2},{6,8},{8,6},{10,12},{12,10},{14,16},{16,14},{18... | collective-permute-start | bytes 983048 | tf_op jit(solution)/shard_map/ppermute | solution.py:713
  12.1 1.9 %shard_map.121.refs_3_.refs_1_ = f32[5,16,32,128]{3,2,1,0:T(8,128)S(1)} custom-call(s32[1]{0:T(128)S(6)} %copy.21.refs_0_, f32[5,5]{1,0:T(8,128)S(1)} %copy-done.2, f32[5,16,32,128]{3,2,1,0:T(8,128)S(1)} %get-tuple-element.34.refs_2_, f32[5,16,32,128]{3,2,1,0:T(8,128)S(1)} %get-tuple-element.35.refs_3_), custom_call_target="tpu_custom_call" | custom-call | flops 2750000128 | bytes 2621440 | tf_op jit(solution)/shard_map/pallas_call | solution.py:628
  14.0 0.0 copy-start.1
  14.0 0.0 copy-start.4
  14.0 0.0 copy-start
  14.1 0.0 copy-start.3
  14.1 1.9 %shard_map.122.refs_1_ = f32[5,16,32,128]{3,2,1,0:T(8,128)S(1)} custom-call(f32[5,5]{1,0:T(8,128)S(1)} %copy-done.2, f32[5,16,32,128]{3,2,1,0:T(8,128)S(1)} %get-tuple-element.32.refs_1_, f32[16,32,128]{2,1,0:T(8,128)S(1)} %get-tuple-element.33.refs_2_.refs_3_, f32[5,16,32,128]{3,2,1,0:T(8,128)S(1)} %shard_map.121.refs_3_.refs_1_), custom_call_target="tpu_custom_call" | custom-call | flops 2750000128 | bytes 2621440 | tf_op jit(solution)/shard_map/pallas_call | solution.py:628
  16.0 0.0 collective-permute-done.2.refs_1_.refs_2_.refs_6_.refs_5_
  16.0 0.1 shard_map.125
  16.1 0.1 collective-permute-start.3
  16.2 0.7 %shard_map.123.refs_1_ = f32[5,32,128]{2,1,0:T(8,128)S(1)} custom-call(f32[2,5,16,64]{3,2,1,0:T(8,128)S(1)} %bitcast.3, f32[5,56,128]{2,1,0:T(8,128)S(1)} %collective-permute-done.2.refs_1_.refs_2_.refs_6_.refs_5_, s32[2,16]{1,0:T(2,128)S(1)} %copy-done.3), custom_call_target="tpu_custom_call" | custom-call | flops 770000000 | bytes 163840 | tf_op jit(solution)/shard_map/pallas_call | solution.py:628
  16.9 0.9 %shard_map.124.refs_8_.refs_6_.refs_7_ = f32[5,16,32,128]{3,2,1,0:T(8,128)S(1)} custom-call(s32[1]{0:T(128)S(6)} %copy.21.refs_0_, f32[5,32,128]{2,1,0:T(8,128)S(1)} %shard_map.123.refs_1_), custom_call_target="tpu_custom_call" | custom-call | flops 770000000 | bytes 2621440 | tf_op jit(solution)/shard_map/pallas_call | solution.py:628
  17.8 3.0 %shard_map.126 = (f32[5,16,32,128]{3,2,1,0:T(8,128)S(1)}, f32[5,16,32,128]{3,2,1,0:T(8,128)S(1)}, f32[2,2,5,32,128]{4,3,2,1,0:T(8,128)S(1)}, f32[2,2,5,32,128]{4...) custom-call(s32[1]{0:T(128)S(6)} %copy.21.refs_0_, ...), custom_call_target="tpu_custom_call" | custom-call | flops 3300000000 | bytes 7168000 | tf_op jit(solution)/shard_map/pallas_call | solution.py:628
  20.8 0.9 %collective-permute-done.3.refs_2_ = f32[6,32,128]{2,1,0:T(8,128)S(1)} collective-permute-done((f32[6,32,128]{2,1,0:T(8,128)S(1)}, f32[6,32,128]{2,1,0:T(8,128)S(1)}, u32[]{:S(2)}, u32[]{:S(2)}) %collective-permute-start.3) | collective-permute-done | bytes 98336 | tf_op jit(solution)/shard_map/ppermute | solution.py:668
  21.7 0.6 %collective-permute-start.4 = (f32[11,32,128]{2,1,0:T(8,128)S(1)}, f32[11,32,128]{2,1,0:T(8,128)S(1)}, u32[]{:S(2)}, u32[]{:S(2)}) collective-permute-start(f32[11,32,128]{2,1,0:T(8,128)S(1)} %shard_map.127.refs_10_.refs_0_), channel_id=1, source_target_pairs={{0,4},{2,6},{4,0},{6,2},{8,12},{10,14},{12,8},{14,10},{16,20},{18,... | collective-permute-start | bytes 540680 | tf_op jit(solution)/shard_map/ppermute | solution.py:668
  22.4 1.7 %shard_map.128 = (f32[5,16,32,128]{3,2,1,0:T(8,128)S(1)}, f32[2,2,5,32,128]{4,3,2,1,0:T(8,128)S(1)}, f32[2,2,5,32,128]{4,3,2,1,0:T(8,128)S(1)}, f32[5,56,128]{2,1,0:T(8,128)S(1)}) custom-call(s32[1]{0:T(128)S(6)} %copy.21.refs_0_, f32[5,16,32,128]{3,2,1,0:T(8,128)S(1)} %shard_map.122.refs_1_, ...), custom_call_target="tpu_custom_call", output_to_operand_aliasing={{1}: (7, {}), {2}: (8, {}), {3}: (9, {})} | custom-call | flops 2750000128 | bytes 4218880 | tf_op jit(solution)/shard_map/pallas_call | solution.py:628
  24.0 0.7 %shard_map.129 = (f32[5,16,128]{2,1,0:T(8,128)S(1)}, f32[5,56,128]{2,1,0:T(8,128)S(1)}) custom-call(f32[5,32,128]{2,1,0:T(8,128)S(1)} %get-tuple-element.48.refs_0_, s32[2,16]{1,0:T(2,128)S(1)} %copy-done.3, f32[5,56,128]{2,1,0:T(8,128)S(1)} %get-tuple-element.49.refs_2_), custom_call_target="tpu_custom_call", output_to_operand_aliasing={{1}: (2, {})} | custom-call | flops 660000000 | bytes 368640 | tf_op jit(solution)/shard_map/pallas_call | solution.py:628
  24.7 0.7 %collective-permute-start.7 = (f32[5,56,128]{2,1,0:T(8,128)S(1)}, f32[5,56,128]{2,1,0:T(8,128)S(1)}, u32[]{:S(2)}, u32[]{:S(2)}) collective-permute-start(f32[5,56,128]{2,1,0:T(8,128)S(1)} %get-tuple-element.53), channel_id=1, source_target_pairs={{0,1},{1,0},{2,3},{3,2},{4,5},{5,4},{6,7},{7,6},{8,9},{9,8},{10,11... | collective-permute-start | bytes 430088 | tf_op jit(solution)/shard_map/ppermute | solution.py:672
  25.4 4.4 %collective-permute-start.6 = (f32[2,2,5,32,128]{4,3,2,1,0:T(8,128)S(1)}, f32[2,2,5,32,128]{4,3,2,1,0:T(8,128)S(1)}, u32[]{:S(2)}, u32[]{:S(2)}) collective-permute-start(f32[2,2,5,32,128]{4,3,2,1,0:T(8,128)S(1)} %get-tuple-element.52), channel_id=1, source_target_pairs={{0,30},{2,4},{4,2},{6,8},{8,6},{10,12},{12,10},{14,16},{16,14},{18... | collective-permute-start | bytes 983048 | tf_op jit(solution)/shard_map/ppermute | solution.py:809
  29.8 0.1 collective-permute-start.8
  29.9 1.9 %shard_map.131.refs_3_.refs_0_ = f32[5,16,32,128]{3,2,1,0:T(8,128)S(1)} custom-call(s32[1]{0:T(128)S(6)} %copy.21.refs_0_, f32[5,5]{1,0:T(8,128)S(1)} %copy-done.2, f32[5,16,32,128]{3,2,1,0:T(8,128)S(1)} %get-tuple-element.46.refs_2_, f32[5,16,32,128]{3,2,1,0:T(8,128)S(1)} %get-tuple-element.47.refs_3_, f32[11,32,128]{2,1,0:T(8,128)S(1)} %shard_map.130.refs_4_.refs_0_), custom_call_target="tpu_custom_call" | custom-call | flops 2750000128 | bytes 2621440 | tf_op jit(solution)/shard_map/pallas_call | solution.py:628
  31.8 1.9 %shard_map.132.refs_2_ = f32[5,16,32,128]{3,2,1,0:T(8,128)S(1)} custom-call(f32[5,5]{1,0:T(8,128)S(1)} %copy-done.2, f32[5,16,32,128]{3,2,1,0:T(8,128)S(1)} %get-tuple-element.45.refs_1_, f32[16,32,128]{2,1,0:T(8,128)S(1)} %get-tuple-element.33.refs_2_.refs_3_, f32[5,16,32,128]{3,2,1,0:T(8,128)S(1)} %shard_map.131.refs_3_.refs_0_), custom_call_target="tpu_custom_call" | custom-call | flops 2750000128 | bytes 2621440 | tf_op jit(solution)/shard_map/pallas_call | solution.py:628
  33.7 3.5 %collective-permute-done.8.refs_1_ = f32[11,32,128]{2,1,0:T(8,128)S(1)} collective-permute-done((f32[11,32,128]{2,1,0:T(8,128)S(1)}, f32[11,32,128]{2,1,0:T(8,128)S(1)}, u32[]{:S(2)}, u32[]{:S(2)}) %collective-permute-start.8) | collective-permute-done | bytes 180256 | tf_op jit(solution)/shard_map/ppermute | solution.py:668
  37.3 0.1 collective-permute-start.9
  37.4 2.0 %collective-permute-start.10 = (f32[5,32,128]{2,1,0:T(8,128)S(1)}, f32[5,32,128]{2,1,0:T(8,128)S(1)}, u32[]{:S(2)}, u32[]{:S(2)}) collective-permute-start(f32[5,32,128]{2,1,0:T(8,128)S(1)} %get-tuple-element.56.refs_0_), channel_id=1, source_target_pairs={{0,16},{2,18},{4,20},{6,22},{8,24},{10,26},{12,28},{14,30},{16,0},... | collective-permute-start | bytes 245768 | tf_op jit(solution)/shard_map/ppermute | solution.py:668
  39.4 3.3 %shard_map.134 = (f32[5,32,16,128]{3,2,1,0:T(8,128)}, f32[8,128]{1,0:T(8,128)S(1)}) custom-call(s32[1]{0:T(128)S(6)} %copy.21.refs_0_, f32[5,5]{1,0:T(8,128)S(1)} %copy-done.2, f32[5,16,32,128]{3,2,1,0:T(8,128)S(1)} %shard_map.132.refs_2_, f32[16,32,128]{2,1,0:T(8,128)S(1)} %get-tuple-element.33.refs_2_.refs_3_, ...), custom_call_target="tpu_custom_call" | custom-call | flops 3300000000 | bytes 2629632 | tf_op jit(solution)/shard_map/pallas_call | solution.py:628
  42.7 2.2 %collective-permute-done.10.refs_1_ = f32[5,32,128]{2,1,0:T(8,128)S(1)} collective-permute-done((f32[5,32,128]{2,1,0:T(8,128)S(1)}, f32[5,32,128]{2,1,0:T(8,128)S(1)}, u32[]{:S(2)}, u32[]{:S(2)}) %collective-permute-start.10) | collective-permute-done | bytes 81952 | tf_op jit(solution)/shard_map/ppermute | solution.py:668
  44.9 0.1 collective-permute-start.11
  45.0 1.8 %shard_map.136 = (f32[5,32,16,128]{3,2,1,0:T(8,128)}, f32[2,5,16,64]{3,2,1,0:T(8,128)}) custom-call(f32[5,16,32,128]{3,2,1,0:T(8,128)S(1)} %shard_map.131.refs_3_.refs_0_, f32[2,2,5,32,128]{4,3,2,1,0:T(8,128)S(1)} %collective-permute-done.5.refs_4_.refs_1_, f32[2,2,5,32,128]{4,3,2,1,0:T(8,128)S(1)} %collective-permute-done.6.refs_5_.refs_2_, ...), custom_call_target="tpu_custom_call" | custom-call | flops 2750000128 | bytes 2703360 | tf_op jit(solution)/shard_map/pallas_call | solution.py:628
  46.8 0.7 %shard_map.137 = f32[2,5,8,128]{3,2,1,0:T(8,128)} custom-call(f32[5,32,128]{2,1,0:T(8,128)S(1)} %shard_map.135.refs_5_.refs_0_, f32[5,32,128]{2,1,0:T(8,128)S(1)} %collective-permute-done.11.refs_1_, s32[2,128]{1,0:T(2,128)S(1)} %copy-done.4), custom_call_target="tpu_custom_call" | custom-call | flops 770000000 | bytes 81920 | tf_op jit(solution)/shard_map/pallas_call | solution.py:628
  (20 shorter events, 0.1 us)
Async XLA Ops:
  1.3 10.8 %copy-start.2 = (f32[5,5]{1,0:T(8,128)S(1)}, f32[5,5]{1,0:T(8,128)}, u32[]{:S(2)}) copy-start(f32[5,5]{1,0:T(8,128)} %refs_1_.11) | copy-start | bytes 304
  4.4 11.5 %collective-permute-start.2 = (f32[5,56,128]{2,1,0:T(8,128)S(1)}, f32[5,56,128]{2,1,0:T(8,128)S(1)}, u32[]{:S(2)}, u32[]{:S(2)}) collective-permute-start(f32[5,56,128]{2,1,0:T(8,128)S(1)} %get-tuple-element.38), channel_id=1, source_target_pairs={{0,1},{1,0},{2,3},{3,2},{4,5},{5,4},{6,7},{7,6},{8,9},{9,8},{10,11... | collective-permute-start | bytes 430088 | tf_op jit(solution)/shard_map/ppermute | solution.py:672
  7.4 10.3 %collective-permute-start = (f32[2,2,5,32,128]{4,3,2,1,0:T(8,128)S(1)}, f32[2,2,5,32,128]{4,3,2,1,0:T(8,128)S(1)}, u32[]{:S(2)}, u32[]{:S(2)}) collective-permute-start(f32[2,2,5,32,128]{4,3,2,1,0:T(8,128)S(1)} %get-tuple-element.36), channel_id=1, source_target_pairs={{0,2},{2,0},{4,6},{6,4},{8,10},{10,8},{12,14},{14,12},{16,18},{18,... | collective-permute-start | bytes 983048 | tf_op jit(solution)/shard_map/ppermute | solution.py:712
  7.4 10.3 %collective-permute-start.1 = (f32[2,2,5,32,128]{4,3,2,1,0:T(8,128)S(1)}, f32[2,2,5,32,128]{4,3,2,1,0:T(8,128)S(1)}, u32[]{:S(2)}, u32[]{:S(2)}) collective-permute-start(f32[2,2,5,32,128]{4,3,2,1,0:T(8,128)S(1)} %get-tuple-element.37), channel_id=1, source_target_pairs={{0,30},{2,4},{4,2},{6,8},{8,6},{10,12},{12,10},{14,16},{16,14},{18... | collective-permute-start | bytes 983048 | tf_op jit(solution)/shard_map/ppermute | solution.py:713
  14.0 2.0 %copy-start.1 = (f32[2,5,8,128]{3,2,1,0:T(8,128)S(1)}, f32[2,5,8,128]{3,2,1,0:T(8,128)}, u32[]{:S(2)}) copy-start(f32[2,5,8,128]{3,2,1,0:T(8,128)} %refs_0_.11) | copy-start | bytes 122884
  14.0 2.0 %copy-start.4 = (s32[2,128]{1,0:T(2,128)S(1)}, s32[2,128]{1,0:T(2,128)}, u32[]{:S(2)}) copy-start(s32[2,128]{1,0:T(2,128)} %refs_2_.5) | copy-start | bytes 3076
  14.0 2.2 %copy-start = (f32[2,5,64,16]{2,3,1,0:T(8,128)S(1)}, f32[2,5,64,16]{2,3,1,0:T(8,128)}, u32[]{:S(2)}) copy-start(f32[2,5,64,16]{2,3,1,0:T(8,128)} %param.14) | copy-start | bytes 122884
  14.1 2.2 %copy-start.3 = (s32[2,16]{1,0:T(2,128)S(1)}, s32[2,16]{1,0:T(2,128)}, u32[]{:S(2)}) copy-start(s32[2,16]{1,0:T(2,128)} %refs_1_.9) | copy-start | bytes 388
  16.1 5.6 %collective-permute-start.3 = (f32[6,32,128]{2,1,0:T(8,128)S(1)}, f32[6,32,128]{2,1,0:T(8,128)S(1)}, u32[]{:S(2)}, u32[]{:S(2)}) collective-permute-start(f32[6,32,128]{2,1,0:T(8,128)S(1)} %get-tuple-element.44), channel_id=1, source_target_pairs={{0,16},{2,18},{4,20},{6,22},{8,24},{10,26},{12,28},{14,30},{16,0},... | collective-permute-start | bytes 294920 | tf_op jit(solution)/shard_map/ppermute | solution.py:668
  21.7 8.1 %collective-permute-start.4 = (f32[11,32,128]{2,1,0:T(8,128)S(1)}, f32[11,32,128]{2,1,0:T(8,128)S(1)}, u32[]{:S(2)}, u32[]{:S(2)}) collective-permute-start(f32[11,32,128]{2,1,0:T(8,128)S(1)} %shard_map.127.refs_10_.refs_0_), channel_id=1, source_target_pairs={{0,4},{2,6},{4,0},{6,2},{8,12},{10,14},{12,8},{14,10},{16,20},{18,... | collective-permute-start | bytes 540680 | tf_op jit(solution)/shard_map/ppermute | solution.py:668
  24.7 14.7 %collective-permute-start.7 = (f32[5,56,128]{2,1,0:T(8,128)S(1)}, f32[5,56,128]{2,1,0:T(8,128)S(1)}, u32[]{:S(2)}, u32[]{:S(2)}) collective-permute-start(f32[5,56,128]{2,1,0:T(8,128)S(1)} %get-tuple-element.53), channel_id=1, source_target_pairs={{0,1},{1,0},{2,3},{3,2},{4,5},{5,4},{6,7},{7,6},{8,9},{9,8},{10,11... | collective-permute-start | bytes 430088 | tf_op jit(solution)/shard_map/ppermute | solution.py:672
  25.4 14.0 %collective-permute-start.5 = (f32[2,2,5,32,128]{4,3,2,1,0:T(8,128)S(1)}, f32[2,2,5,32,128]{4,3,2,1,0:T(8,128)S(1)}, u32[]{:S(2)}, u32[]{:S(2)}) collective-permute-start(f32[2,2,5,32,128]{4,3,2,1,0:T(8,128)S(1)} %get-tuple-element.51), channel_id=1, source_target_pairs={{0,2},{2,0},{4,6},{6,4},{8,10},{10,8},{12,14},{14,12},{16,18},{18,... | collective-permute-start | bytes 983048 | tf_op jit(solution)/shard_map/ppermute | solution.py:808
  25.4 14.0 %collective-permute-start.6 = (f32[2,2,5,32,128]{4,3,2,1,0:T(8,128)S(1)}, f32[2,2,5,32,128]{4,3,2,1,0:T(8,128)S(1)}, u32[]{:S(2)}, u32[]{:S(2)}) collective-permute-start(f32[2,2,5,32,128]{4,3,2,1,0:T(8,128)S(1)} %get-tuple-element.52), channel_id=1, source_target_pairs={{0,30},{2,4},{4,2},{6,8},{8,6},{10,12},{12,10},{14,16},{16,14},{18... | collective-permute-start | bytes 983048 | tf_op jit(solution)/shard_map/ppermute | solution.py:809
  29.8 7.4 %collective-permute-start.8 = (f32[11,32,128]{2,1,0:T(8,128)S(1)}, f32[11,32,128]{2,1,0:T(8,128)S(1)}, u32[]{:S(2)}, u32[]{:S(2)}) collective-permute-start(f32[11,32,128]{2,1,0:T(8,128)S(1)} %shard_map.130.refs_4_.refs_0_), channel_id=1, source_target_pairs={{0,8},{2,10},{4,12},{6,14},{8,0},{10,2},{12,4},{14,6},{16,24},{18,... | collective-permute-start | bytes 540680 | tf_op jit(solution)/shard_map/ppermute | solution.py:668
  37.3 2.1 %collective-permute-start.9 = (f32[6,32,128]{2,1,0:T(8,128)S(1)}, f32[6,32,128]{2,1,0:T(8,128)S(1)}, u32[]{:S(2)}, u32[]{:S(2)}) collective-permute-start(f32[6,32,128]{2,1,0:T(8,128)S(1)} %get-tuple-element.54.refs_8_), channel_id=1, source_target_pairs={{0,2},{2,0},{4,6},{6,4},{8,10},{10,8},{12,14},{14,12},{16,18},{18,... | collective-permute-start | bytes 294920 | tf_op jit(solution)/shard_map/ppermute | solution.py:668
  37.4 7.5 %collective-permute-start.10 = (f32[5,32,128]{2,1,0:T(8,128)S(1)}, f32[5,32,128]{2,1,0:T(8,128)S(1)}, u32[]{:S(2)}, u32[]{:S(2)}) collective-permute-start(f32[5,32,128]{2,1,0:T(8,128)S(1)} %get-tuple-element.56.refs_0_), channel_id=1, source_target_pairs={{0,16},{2,18},{4,20},{6,22},{8,24},{10,26},{12,28},{14,30},{16,0},... | collective-permute-start | bytes 245768 | tf_op jit(solution)/shard_map/ppermute | solution.py:668
  44.9 1.9 %collective-permute-start.11 = (f32[5,32,128]{2,1,0:T(8,128)S(1)}, f32[5,32,128]{2,1,0:T(8,128)S(1)}, u32[]{:S(2)}, u32[]{:S(2)}) collective-permute-start(f32[5,32,128]{2,1,0:T(8,128)S(1)} %shard_map.135.refs_5_.refs_0_), channel_id=1, source_target_pairs={{0,2},{2,0},{4,6},{6,4},{8,10},{10,8},{12,14},{14,12},{16,18},{18,... | collective-permute-start | bytes 245768 | tf_op jit(solution)/shard_map/ppermute | solution.py:668

commit v3 on v2

--- a/solution.py
+++ b/solution.py
@@ -189,10 +189,8 @@
 
 
 class Beyond:
-    def __init__(self, g, s, fa, fb, fy):
-        self.g, self.s, self.fa, self.fb, self.fy = g, s, fa, fb, fy
-        self.edge = border()
-        self.valid = valid_lanes(g)
+    def __init__(self, g, s, fa, fb):
+        self.g, self.s, self.fa, self.fb = g, s, fa, fb
         here = lax.axis_index("gx")
         self.odd = here % 2 == 1
         self.first, self.last = here == 0, here == g.nx - 1
@@ -207,21 +205,34 @@
         value = jnp.where(self.odd, self.fb[at], self.fa[at])
         return jnp.where(self.last, jnp.zeros_like(value), value)
 
-    def lanes_of(self, f, rows):
+    def columns(self, f, x, rows):
+        last = self.g.X - 1
+        if x == 0:
+            return near * self.left(1, f, rows) + far * self.left(0, f, rows)
+        if x == 1:
+            return far * self.left(1, f, rows)
+        if x == last - 1:
+            return far * self.right(0, f, rows)
+        if x == last:
+            return near * self.right(0, f, rows) + far * self.right(1, f, rows)
+        return None
+
+
+class BeyondLanes:
+    def __init__(self, g, s, fy):
+        self.s, self.fy = s, fy
+        self.edge = border()
+        self.valid = valid_lanes(g)
+
+    def tile(self, f, rows):
         return self.fy[f, rows, :] * self.valid
 
-    def add(self, f, x, rows, packed):
-        s, last = self.s, self.g.X - 1
-        total = unpack_lanes(x, 64 * s, packed, self.edge)
-        if x == 0:
-            total = total + near * self.left(1, f, rows) + far * self.left(0, f, rows)
-        if x == 1:
-            total = total + far * self.left(1, f, rows)
-        if x == last - 1:
-            total = total + far * self.right(0, f, rows)
-        if x == last:
-            total = total + near * self.right(0, f, rows) + far * self.right(1, f, rows)
-        return total
+    def column(self, x, packed):
+        return unpack_lanes(x, 64 * self.s, packed, self.edge)
+
+
+def plus(value, more):
+    return value if more is None else value + more
 
 
 def lane_sums(vectors):
@@ -321,7 +332,8 @@
             laps[f, x] = total * (1.0 / 12.0)
 
 
-def adjoint_inside_kernel(g, scaled, relax, mix, ps, qs, out, rx, band, laps):
+def adjoint_inside_kernel(g, scaled, relax, mix, ps, qs, fy, out, rx, band, laps):
+    beyond = BeyondLanes(g, 1, fy)
     width = relax[0]
     table = mix_table(mix, True)
     fill_band(band)
@@ -332,55 +344,62 @@
     def tile_step(tile, carry):
         rows = rows_of(tile)
         fill_laps(g, qs, rows, band, laps)
+        halo = [beyond.tile(f, rows) for f in range(g.F)]
         for x in range(g.X):
             p = [ps[f, x, rows, :] for f in range(g.F)]
             if scaled:
                 open_xy = open_y * (1.0 - rx[x])
                 p = [open_xy * value for value in p]
             for f in range(g.F):
-                out[f, x, rows, :] = mixed(table, f, p) + laps[f, x]
+                out[f, x, rows, :] = mixed(table, f, p) + laps[f, x] + beyond.column(x, halo[f])
         return carry
 
     lax.fori_loop(0, g.tiles, tile_step, 0)
 
 
-def forward_inside_kernel(g, mix, ut, dt, out, band, laps):
+def forward_inside_kernel(g, mix, ut, dt, *rest):
+    *fy, out, band, laps = rest
     table = mix_table(mix, False)
     fill_band(band)
+    beyond = BeyondLanes(g, 0, fy[0]) if fy else None
 
     def tile_step(tile, carry):
         rows = rows_of(tile)
         fill_laps(g, ut, rows, band, laps)
+        if fy:
+            halo = [beyond.tile(f, rows) for f in range(g.F)]
         for x in range(g.X):
             u = [ut[f, x, rows, :] for f in range(g.F)]
             d = dt[x, rows, :]
             for f in range(g.F):
-                out[f, x, rows, :] = mixed(table, f, u) + d * laps[f, x]
+                lap = laps[f, x]
+                if fy:
+                    lap = lap + beyond.column(x, halo[f])
+                out[f, x, rows, :] = mixed(table, f, u) + d * lap
         return carry
 
     lax.fori_loop(0, g.tiles, tile_step, 0)
 
 
 def adjoint_first_kernel(
-    g, relax, inside, at, dt, fa, fb, fy, p1, q1, ma, mb, my, dwe, dsn, rx
+    g, relax, inside, at, dt, fa, fb, p1, q1, ma, mb, my, dwe, dsn, rx
 ):
     width = relax[0]
     fill_ramp_x(g, width, rx)
     slope_y = ramp_y(g, width)
     open_y = 1.0 - slope_y
-    beyond = Beyond(g, 1, fa, fb, fy)
+    beyond = Beyond(g, 1, fa, fb)
 
     def tile_step(tile, carry):
         rows = rows_of(tile)
         for f in range(g.F):
-            halo = beyond.lanes_of(f, rows)
             packed = jnp.zeros((8, 128), f32)
             share = jnp.zeros((8, 128), f32)
             pushes = []
             for x in range(g.X):
                 slope_x = rx[x]
                 open_xy = open_y * (1.0 - slope_x)
-                middle = inside[f, x, rows, :] + beyond.add(f, x, rows, halo)
+                middle = plus(inside[f, x, rows, :], beyond.columns(f, x, rows))
                 carried = at[f, x, rows, :] + middle
                 share = share + slope_x * carried
                 pushes.append(slope_y * carried)
@@ -406,17 +425,19 @@
     width = relax[0]
     fill_ramp_x(g, width, rx)
     open_y = 1.0 - ramp_y(g, width)
-    beyond = Beyond(g, 0, fa, fb, fy)
+    beyond = Beyond(g, 0, fa, fb)
+    beyond_lanes = BeyondLanes(g, 0, fy)
     lane = lanes()
 
     def tile_step(tile, carry):
         rows = rows_of(tile)
         for f in range(g.F):
-            halo = beyond.lanes_of(f, rows)
+            halo = beyond_lanes.tile(f, rows)
             packed = jnp.zeros((8, 128), f32)
             for x in range(g.X):
                 open_xy = open_y * (1.0 - rx[x])
-                stepped = inside[f, x, rows, :] + dt[x, rows, :] * beyond.add(f, x, rows, halo)
+                lap = plus(beyond_lanes.column(x, halo), beyond.columns(f, x, rows))
+                stepped = inside[f, x, rows, :] + dt[x, rows, :] * lap
                 done = open_xy * stepped + sides[f, x, rows, :]
                 u1[f, x, rows, :] = done
                 packed = pack_lanes(x, 0, done, packed)
@@ -427,16 +448,16 @@
     lax.fori_loop(0, g.tiles, tile_step, 0)
 
 
-def adjoint_last_kernel(g, inside, fa, fb, fy, gsn_own, out, gsn):
+def adjoint_last_kernel(g, inside, fa, fb, gsn_own, gsn_other, out, gsn, mark):
+    mark[...] = jnp.zeros((8, 128), f32)
     out2 = out.reshape(g.F * g.K * g.X, g.Y)
-    beyond = Beyond(g, 1, fa, fb, fy)
+    beyond = Beyond(g, 1, fa, fb)
 
     def tile_step(tile, carry):
         rows = rows_of(tile)
         for f in range(g.F):
-            halo = beyond.lanes_of(f, rows)
             for x in range(g.X):
-                value = inside[f, x, rows, :] + beyond.add(f, x, rows, halo)
+                value = plus(inside[f, x, rows, :], beyond.columns(f, x, rows))
                 strided(out2, g, f, tile, x)[...] = value
         return carry
 
@@ -446,13 +467,13 @@
         span = gsn.shape[3]
         for f in range(g.F):
             gsn[here, f] = gsn_own[f, :, :span]
-            gsn[1 - here, f] = fy[f, g.K : g.K + g.X, :span]
+            gsn[1 - here, f] = gsn_other[f, :, :span]
     else:
         gsn[...] = jnp.zeros(gsn.shape, f32)
 
 
 def forward_last_kernel(
-    g, relax, mix, inside, dt, fa, fb, fy, sides, kept, swapped, out, mark, rx, lx
+    g, relax, mix, inside, dt, fa, fb, sides, kept, swapped, out, mark, rx, lx
 ):
     width = relax[0]
     mark[...] = jnp.zeros((8, 128), f32)
@@ -464,7 +485,8 @@
     open_y = 1.0 - ramp_y(g, width)
     masks = lap_masks()
     table = mix_table(mix, False)
-    beyond = Beyond(g, 0, fa, fb, fy)
+    beyond = Beyond(g, 0, fa, fb)
+    edge, valid = border(), valid_lanes(g)
     out2 = out.reshape(g.F * g.K * g.X, g.Y)
 
     def tile_step(tile, carry):
@@ -472,17 +494,16 @@
         bound = [
             open_y * (kept[f, rows, :] + swapped[f, rows, :]) for f in range(g.F)
         ]
-        past = packed_message(kept[g.F, rows, :] + swapped[g.F, rows, :]) * beyond.valid
+        past = packed_message(kept[g.F, rows, :] + swapped[g.F, rows, :]) * valid
         for f in range(g.F):
-            lap_y = unpack_lanes(f, 0, past, beyond.edge)
+            lap_y = unpack_lanes(f, 0, past, edge)
             for shift, mask in masks:
                 lap_y = lap_y + mask * turn(bound[f], shift)
             mixed_bound = mixed(table, f, bound)
-            halo = beyond.lanes_of(f, rows)
             for x in range(g.X):
                 slope_x = rx[x + 2]
                 open_xy = open_y * (1.0 - slope_x)
-                lap = beyond.add(f, x, rows, halo) + slope_x * lap_y + lx[x] * bound[f]
+                lap = plus(slope_x * lap_y + lx[x] * bound[f], beyond.columns(f, x, rows))
                 stepped = inside[f, x, rows, :] + slope_x * mixed_bound + dt[x, rows, :] * lap
                 done = open_xy * stepped + slope_x * bound[f] + sides[f, x, rows, :]
                 strided(out2, g, f, tile, x)[...] = done
@@ -491,7 +512,7 @@
     lax.fori_loop(0, g.tiles, tile_step, 0)
 
 
-def side_sums_kernel(g, dsn, tsn, my_in, gsn, my, wide):
+def side_sums_kernel(g, dsn, tsn, gsn, sent, wide):
     here = lax.axis_index("gy")
     shift = column_of(jnp.where(here == 0, tsn[0:1, :], tsn[1:2, :]))
     lane = lax.broadcasted_iota(jnp.int32, (g.X, 128), 1)
@@ -506,7 +527,7 @@
             whole = shift_levels(levels, shift, 1)
             moved = turn(whole, 64)
             gsn[f] = jnp.where(here == 0, whole, moved)
-            my[f, g.K : g.K + g.X, :] = jnp.where(here == 0, moved, whole)
+            sent[f] = jnp.where(here == 0, moved, whole)
 
 
 def side_bounds_kernel(g, sn, fsn, tsn, bsn, wide):
@@ -712,20 +733,20 @@
     fa = lax.ppermute(ma, "gx", evens)
     fb = lax.ppermute(mb, "gx", odds)
 
-    (inside_a,) = call(
-        bind(adjoint_inside_kernel, True),
-        [block],
-        [ramps, band, laps],
-        [("s", relax_width), ("s", field_mix), ("v", at), ("v", qt)],
-        2.5,
-    )
     (inside_u,) = call(
         bind(forward_inside_kernel),
         [block],
         [band, laps],
         [("s", field_mix), ("v", ut), ("v", dt)],
         2.5,
-        after=[inside_a],
+    )
+    (inside_a,) = call(
+        bind(adjoint_inside_kernel, True),
+        [block],
+        [ramps, band, laps],
+        [("s", relax_width), ("s", field_mix), ("v", at), ("v", qt), ("v", fy)],
+        2.5,
+        after=[inside_u],
     )
     keep, send = call(
         bind(fold_kernel),
@@ -760,7 +781,6 @@
             ("v", dt),
             ("v", fa),
             ("v", fb),
-            ("v", fy),
         ],
         3,
         after=[keep, sides],
@@ -793,22 +813,22 @@
         {7: 1, 8: 2, 9: 3},
         after=[state],
     )
-    if g.pair:
-        gsn_own, my = call(
-            bind(side_sums_kernel),
-            [(F, X, 128), lane_shape],
-            [(128, 128)],
-            [("v", dsn), ("v", terrain_sn), ("v", my)],
-            0.6,
-            {2: 1},
-        )
-    else:
-        gsn_own = dsn
     fy = to_y(my)
     fa = lax.ppermute(ma, "gx", evens)
     fb = lax.ppermute(mb, "gx", odds)
 
-    state = add(state, moved, [gsn_own])
+    state = add(state, moved, [u1])
+    gsn_own = gsn_other = dsn
+    if g.pair:
+        gsn_own, sent = call(
+            bind(side_sums_kernel),
+            [(F, X, 128)] * 2,
+            [(128, 128)],
+            [("v", dsn), ("v", terrain_sn)],
+            0.6,
+            after=[state],
+        )
+        gsn_other = lax.ppermute(sent, "gy", [(0, 1), (1, 0)])
     distance = 4
     while distance < nx // 4:
         state = state + swapped(state, distance)
@@ -818,7 +838,7 @@
         bind(adjoint_inside_kernel, False),
         [block],
         [ramps, band, laps],
-        [("s", relax_width), ("s", field_mix), ("v", p1), ("v", q1)],
+        [("s", relax_width), ("s", field_mix), ("v", p1), ("v", q1), ("v", fy)],
         2.5,
         after=[state],
     )
@@ -826,9 +846,17 @@
         bind(forward_inside_kernel),
         [block],
         [band, laps],
-        [("s", field_mix), ("v", u1), ("v", dt)],
+        [("s", field_mix), ("v", u1), ("v", dt), ("v", fy)],
         2.5,
         after=[inside_a],
+    )
+    grad_state, grad_sn, early = call(
+        bind(adjoint_last_kernel),
+        [child_state.shape, sn_turned.shape, (8, 128)],
+        [],
+        [("v", inside_a), ("v", fa), ("v", fb), ("v", gsn_own), ("v", gsn_other)],
+        2.5,
+        after=[inside_u],
     )
     sums, bounds = call(
         bind(split_kernel),
@@ -836,7 +864,7 @@
         [],
         [("v", state), ("v", moved)],
         0.1,
-        after=[inside_u],
+        after=[early],
     )
     other_bounds = swapped(bounds, 1)
     moved = swapped(sums, nx // 2)
@@ -851,7 +879,6 @@
             ("v", dt),
             ("v", fa),
             ("v", fb),
-            ("v", fy),
             ("v", sides),
             ("v", bounds),
             ("v", other_bounds),
@@ -860,14 +887,6 @@
     )
     sums = add(sums, moved, [mark])
     other_sums = swapped(sums, 1)
-    grad_state, grad_sn = call(
-        bind(adjoint_last_kernel),
-        [child_state.shape, sn_turned.shape],
-        [],
-        [("v", inside_a), ("v", fa), ("v", fb), ("v", fy), ("v", gsn_own)],
-        2.5,
-        after=[sums],
-    )
     (grad_we,) = call(
         bind(spread_kernel),
         [parent_we.shape],

time: 47.7 us -> 47 us (0.985)
  waiting for transfers between devices: 6.66 us -> 3.69 us
  starting transfers between devices: 15.7 us -> 18.4 us
    ppermute x6, waiting for transfers between devices: 6.64 us -> 3.67 us  [swapped(): return lax.ppermute(values, 'gx', [(i, i ^ distance) for i in range(nx)])]
    ppermute x0 -> x1, starting transfers between devices: none -> 1.55 us  [body(): gsn_other = lax.ppermute(sent, 'gy', [(0, 1), (1, 0)])]
    ppermute x2, starting transfers between devices: 3.7 us -> 4.56 us  [to_y(): return lax.ppermute(message, 'gy', [(0, 1), (1, 0)])]
    ppermute x6, starting transfers between devices: 2.97 us -> 3.77 us  [swapped(): return lax.ppermute(values, 'gx', [(i, i ^ distance) for i in range(nx)])]
    ppermute x2, starting transfers between devices: 9.06 us -> 8.5 us  [body(): fb = lax.ppermute(mb, 'gx', odds)]
  transfers between devices with their start and end apart: 12 -> 13, of which waited for: 3 -> 3; matrix products, arithmetic and copies ran while one was open for 0% -> 0% of each run, Pallas kernels for 41% -> 41%
where the time goes in v3:
time: 47 us; the launch traced here: 46.9 us
  Pallas kernels  23.3 us (50%)
  starting transfers between devices  18.4 us (39%)
  waiting for transfers between devices  3.69 us (8%)
  between operations  1.48 us (3%)
    pallas_call x18, Pallas kernels, call(): pl.pallas_call(run, out_shape=out_shape, in_specs=[places[where] for wher...  23.3 us
    ppermute x2, starting transfers between devices, body(): fb = lax.ppermute(mb, 'gx', odds)  8.5 us
    ppermute x2, starting transfers between devices, to_y(): return lax.ppermute(message, 'gy', [(0, 1), (1, 0)])  4.56 us
    ppermute x6, starting transfers between devices, swapped(): return lax.ppermute(values, 'gx', [(i, i ^ distance) for i in range(nx)])  3.77 us
    ppermute x6, waiting for transfers between devices, swapped(): return lax.ppermute(values, 'gx', [(i, i ^ distance) for i in range(nx)])  3.67 us
    ppermute x1, starting transfers between devices, body(): gsn_other = lax.ppermute(sent, 'gy', [(0, 1), (1, 0)])  1.55 us
  transfers between devices with their start and end apart: 13, of which 3 were waited for; matrix products, arithmetic and copies ran while one was open for 0% of the time, Pallas kernels for 41%

profile of v3, /device:TPU:0, one launch (start us, length us, event | category | flops | bytes accessed | tf_op | source)
XLA Modules:
  0.0 46.9 jit_solution(15518793591737164568)
XLA Ops:
  1.3 3.2 %shard_map.120 = (f32[5,16,32,128]{3,2,1,0:T(8,128)S(1)}, f32[5,16,32,128]{3,2,1,0:T(8,128)S(1)}, f32[16,32,128]{2,1,0:T(8,128)S(1)}, f32[5,16,32,128]{3,2,1,0:T...) custom-call(s32[1]{0:T(128)S(6)} %copy.19.refs_0_, ...), custom_call_target="tpu_custom_call" | custom-call | flops 3300000000 | bytes 9986048 | tf_op jit(solution)/shard_map/pallas_call | solution.py:649
  4.5 3.0 %collective-permute-start.2 = (f32[5,56,128]{2,1,0:T(8,128)S(1)}, f32[5,56,128]{2,1,0:T(8,128)S(1)}, u32[]{:S(2)}, u32[]{:S(2)}) collective-permute-start(f32[5,56,128]{2,1,0:T(8,128)S(1)} %get-tuple-element.37), channel_id=1, source_target_pairs={{0,1},{1,0},{2,3},{3,2},{4,5},{5,4},{6,7},{7,6},{8,9},{9,8},{10,11... | collective-permute-start | bytes 430088 | tf_op jit(solution)/shard_map/ppermute | solution.py:693
  7.5 0.0 collective-permute-start
  7.5 4.7 %collective-permute-start.1 = (f32[2,2,5,32,128]{4,3,2,1,0:T(8,128)S(1)}, f32[2,2,5,32,128]{4,3,2,1,0:T(8,128)S(1)}, u32[]{:S(2)}, u32[]{:S(2)}) collective-permute-start(f32[2,2,5,32,128]{4,3,2,1,0:T(8,128)S(1)} %get-tuple-element.36), channel_id=1, source_target_pairs={{0,30},{2,4},{4,2},{6,8},{8,6},{10,12},{12,10},{14,16},{16,14},{18... | collective-permute-start | bytes 983048 | tf_op jit(solution)/shard_map/ppermute | solution.py:734
  12.1 0.0 copy-start.3
  12.2 1.9 %shard_map.121.refs_5_.refs_1_ = f32[5,16,32,128]{3,2,1,0:T(8,128)S(1)} custom-call(f32[5,5]{1,0:T(8,128)S(1)} %copy-done.2, f32[5,16,32,128]{3,2,1,0:T(8,128)S(1)} %get-tuple-element.33.refs_1_, f32[16,32,128]{2,1,0:T(8,128)S(1)} %get-tuple-element.34.refs_2_.refs_3_), custom_call_target="tpu_custom_call" | custom-call | flops 2750000128 | bytes 2621440 | tf_op jit(solution)/shard_map/pallas_call | solution.py:649
  14.1 0.1 shard_map.125
  14.2 0.1 collective-permute-start.3
  14.3 0.7 %shard_map.122.refs_1_ = f32[5,32,128]{2,1,0:T(8,128)S(1)} custom-call(f32[2,5,16,64]{3,2,1,0:T(8,128)S(1)} %bitcast.3, f32[5,56,128]{2,1,0:T(8,128)S(1)} %collective-permute-done.2.refs_1_.refs_4_.refs_2_.refs_5_, s32[2,16]{1,0:T(2,128)S(1)} %copy-done.3), custom_call_target="tpu_custom_call" | custom-call | flops 770000000 | bytes 163840 | tf_op jit(solution)/shard_map/pallas_call | solution.py:649
  15.0 0.9 %shard_map.123.refs_7_.refs_6_ = f32[5,16,32,128]{3,2,1,0:T(8,128)S(1)} custom-call(s32[1]{0:T(128)S(6)} %copy.19.refs_0_, f32[5,32,128]{2,1,0:T(8,128)S(1)} %shard_map.122.refs_1_), custom_call_target="tpu_custom_call" | custom-call | flops 770000000 | bytes 2621440 | tf_op jit(solution)/shard_map/pallas_call | solution.py:649
  15.9 2.0 %shard_map.124.refs_1_ = f32[5,16,32,128]{3,2,1,0:T(8,128)S(1)} custom-call(s32[1]{0:T(128)S(6)} %copy.19.refs_0_, f32[5,5]{1,0:T(8,128)S(1)} %copy-done.2, f32[5,16,32,128]{3,2,1,0:T(8,128)S(1)} %get-tuple-element.38.refs_2_, f32[5,16,32,128]{3,2,1,0:T(8,128)S(1)} %get-tuple-element.39.refs_3_, ...), custom_call_target="tpu_custom_call" | custom-call | flops 2750000128 | bytes 2621440 | tf_op jit(solution)/shard_map/pallas_call | solution.py:649
  17.9 0.0 collective-permute-done.1.refs_5_.refs_4_
  17.9 2.6 %shard_map.126 = (f32[5,16,32,128]{3,2,1,0:T(8,128)S(1)}, f32[5,16,32,128]{3,2,1,0:T(8,128)S(1)}, f32[2,2,5,32,128]{4,3,2,1,0:T(8,128)S(1)}, f32[2,2,5,32,128]{4...) custom-call(s32[1]{0:T(128)S(6)} %copy.19.refs_0_, ...), custom_call_target="tpu_custom_call" | custom-call | flops 3300000000 | bytes 7168000 | tf_op jit(solution)/shard_map/pallas_call | solution.py:649
  20.5 0.4 collective-permute-done.3.refs_2_
  20.9 1.2 %collective-permute-start.5 = (f32[11,32,128]{2,1,0:T(8,128)S(1)}, f32[11,32,128]{2,1,0:T(8,128)S(1)}, u32[]{:S(2)}, u32[]{:S(2)}) collective-permute-start(f32[11,32,128]{2,1,0:T(8,128)S(1)} %shard_map.127.refs_10_.refs_0_), channel_id=1, source_target_pairs={{0,4},{2,6},{4,0},{6,2},{8,12},{10,14},{12,8},{14,10},{16,20},{18,... | collective-permute-start | bytes 540680 | tf_op jit(solution)/shard_map/ppermute | solution.py:689
  22.1 1.7 %shard_map.128 = (f32[5,16,32,128]{3,2,1,0:T(8,128)S(1)}, f32[2,2,5,32,128]{4,3,2,1,0:T(8,128)S(1)}, f32[2,2,5,32,128]{4,3,2,1,0:T(8,128)S(1)}, f32[5,56,128]{2,1,0:T(8,128)S(1)}) custom-call(s32[1]{0:T(128)S(6)} %copy.19.refs_0_, f32[5,16,32,128]{3,2,1,0:T(8,128)S(1)} %shard_map.121.refs_5_.refs_1_, ...), custom_call_target="tpu_custom_call", output_to_operand_aliasing={{1}: (7, {}), {2}: (8, {}), {3}: (9, {})} | custom-call | flops 2750000128 | bytes 4218880 | tf_op jit(solution)/shard_map/pallas_call | solution.py:649
  23.7 1.6 %collective-permute-start.4 = (f32[5,56,128]{2,1,0:T(8,128)S(1)}, f32[5,56,128]{2,1,0:T(8,128)S(1)}, u32[]{:S(2)}, u32[]{:S(2)}) collective-permute-start(f32[5,56,128]{2,1,0:T(8,128)S(1)} %get-tuple-element.47), channel_id=1, source_target_pairs={{0,1},{1,0},{2,3},{3,2},{4,5},{5,4},{6,7},{7,6},{8,9},{9,8},{10,11... | collective-permute-start | bytes 430088 | tf_op jit(solution)/shard_map/ppermute | solution.py:693
  25.3 0.0 collective-permute-start.6
  25.3 3.8 %collective-permute-start.7 = (f32[2,2,5,32,128]{4,3,2,1,0:T(8,128)S(1)}, f32[2,2,5,32,128]{4,3,2,1,0:T(8,128)S(1)}, u32[]{:S(2)}, u32[]{:S(2)}) collective-permute-start(f32[2,2,5,32,128]{4,3,2,1,0:T(8,128)S(1)} %get-tuple-element.51), channel_id=1, source_target_pairs={{0,30},{2,4},{4,2},{6,8},{8,6},{10,12},{12,10},{14,16},{16,14},{18... | collective-permute-start | bytes 983048 | tf_op jit(solution)/shard_map/ppermute | solution.py:818
  29.2 0.1 collective-permute-start.8
  29.3 0.7 %shard_map.132 = (f32[5,16,128]{2,1,0:T(8,128)S(1)}, f32[5,16,128]{2,1,0:T(8,128)S(1)}) custom-call(f32[5,32,128]{2,1,0:T(8,128)S(1)} %get-tuple-element.52.refs_0_, s32[2,16]{1,0:T(2,128)S(1)} %copy-done.3, f32[11,32,128]{2,1,0:T(8,128)S(1)} %shard_map.129.refs_5_.refs_2_.refs_0_), custom_call_target="tpu_custom_call" | custom-call | flops 660000000 | bytes 163840 | tf_op jit(solution)/shard_map/pallas_call | solution.py:649
  30.0 1.6 %collective-permute-start.9 = (f32[5,16,128]{2,1,0:T(8,128)S(1)}, f32[5,16,128]{2,1,0:T(8,128)S(1)}, u32[]{:S(2)}, u32[]{:S(2)}) collective-permute-start(f32[5,16,128]{2,1,0:T(8,128)S(1)} %get-tuple-element.54), channel_id=1, source_target_pairs={{0,1},{1,0},{2,3},{3,2},{4,5},{5,4},{6,7},{7,6},{8,9},{9,8},{10,11... | collective-permute-start | bytes 122888 | tf_op jit(solution)/shard_map/ppermute | solution.py:831
  31.5 2.0 %shard_map.130.refs_4_.refs_0_ = f32[5,16,32,128]{3,2,1,0:T(8,128)S(1)} custom-call(s32[1]{0:T(128)S(6)} %copy.19.refs_0_, f32[5,5]{1,0:T(8,128)S(1)} %copy-done.2, f32[5,16,32,128]{3,2,1,0:T(8,128)S(1)} %get-tuple-element.48.refs_2_, f32[5,16,32,128]{3,2,1,0:T(8,128)S(1)} %get-tuple-element.49.refs_3_, ...), custom_call_target="tpu_custom_call" | custom-call | flops 2750000128 | bytes 2621440 | tf_op jit(solution)/shard_map/pallas_call | solution.py:649
  33.5 2.0 %shard_map.131.refs_5_.refs_2_ = f32[5,16,32,128]{3,2,1,0:T(8,128)S(1)} custom-call(f32[5,5]{1,0:T(8,128)S(1)} %copy-done.2, f32[5,16,32,128]{3,2,1,0:T(8,128)S(1)} %get-tuple-element.46.refs_2_.refs_1_, f32[16,32,128]{2,1,0:T(8,128)S(1)} %get-tuple-element.34.refs_2_.refs_3_, f32[5,56,128]{2,1,0:T(8,128)S(1)} %collective-permute-done.4.refs_4_.refs_3_, ...), custom_call_target="tpu_custom_call" | custom-call | flops 2750000128 | bytes 2621440 | tf_op jit(solution)/shard_map/pallas_call | solution.py:649
  35.6 1.5 %shard_map.133 = (f32[5,32,16,128]{3,2,1,0:T(8,128)}, f32[2,5,16,64]{3,2,1,0:T(8,128)}, f32[8,128]{1,0:T(8,128)S(1)}) custom-call(f32[5,16,32,128]{3,2,1,0:T(8,128)S(1)} %shard_map.130.refs_4_.refs_0_, f32[2,2,5,32,128]{4,3,2,1,0:T(8,128)S(1)} %collective-permute-done.6.refs_1_.refs_4_, f32[2,2,5,32,128]{4,3,2,1,0:T(8,128)S(1)} %collective-permute-done.7.refs_2_.refs_5_, ...), custom_call_target="tpu_custom_call" | custom-call | flops 2750000128 | bytes 2711552 | tf_op jit(solution)/shard_map/pallas_call | solution.py:649
  37.2 0.6 %collective-permute-start.10 = (f32[6,32,128]{2,1,0:T(8,128)S(1)}, f32[6,32,128]{2,1,0:T(8,128)S(1)}, u32[]{:S(2)}, u32[]{:S(2)}) collective-permute-start(f32[6,32,128]{2,1,0:T(8,128)S(1)} %get-tuple-element.56.refs_7_), channel_id=1, source_target_pairs={{0,2},{2,0},{4,6},{6,4},{8,10},{10,8},{12,14},{14,12},{16,18},{18,... | collective-permute-start | bytes 294920 | tf_op jit(solution)/shard_map/ppermute | solution.py:689
  37.8 1.8 %collective-permute-start.11 = (f32[5,32,128]{2,1,0:T(8,128)S(1)}, f32[5,32,128]{2,1,0:T(8,128)S(1)}, u32[]{:S(2)}, u32[]{:S(2)}) collective-permute-start(f32[5,32,128]{2,1,0:T(8,128)S(1)} %get-tuple-element.59.refs_0_), channel_id=1, source_target_pairs={{0,16},{2,18},{4,20},{6,22},{8,24},{10,26},{12,28},{14,30},{16,0},... | collective-permute-start | bytes 245768 | tf_op jit(solution)/shard_map/ppermute | solution.py:689
  39.5 3.3 %shard_map.135 = (f32[5,32,16,128]{3,2,1,0:T(8,128)}, f32[8,128]{1,0:T(8,128)S(1)}) custom-call(s32[1]{0:T(128)S(6)} %copy.19.refs_0_, f32[5,5]{1,0:T(8,128)S(1)} %copy-done.2, f32[5,16,32,128]{3,2,1,0:T(8,128)S(1)} %shard_map.131.refs_5_.refs_2_, f32[16,32,128]{2,1,0:T(8,128)S(1)} %get-tuple-element.34.refs_2_.refs_3_, ...), custom_call_target="tpu_custom_call" | custom-call | flops 3300000000 | bytes 2629632 | tf_op jit(solution)/shard_map/pallas_call | solution.py:649
  42.8 2.0 %collective-permute-done.11.refs_1_ = f32[5,32,128]{2,1,0:T(8,128)S(1)} collective-permute-done((f32[5,32,128]{2,1,0:T(8,128)S(1)}, f32[5,32,128]{2,1,0:T(8,128)S(1)}, u32[]{:S(2)}, u32[]{:S(2)}) %collective-permute-start.11) | collective-permute-done | bytes 81952 | tf_op jit(solution)/shard_map/ppermute | solution.py:689
  44.9 0.1 collective-permute-start.12
  44.9 1.3 %collective-permute-done.12.refs_1_ = f32[5,32,128]{2,1,0:T(8,128)S(1)} collective-permute-done((f32[5,32,128]{2,1,0:T(8,128)S(1)}, f32[5,32,128]{2,1,0:T(8,128)S(1)}, u32[]{:S(2)}, u32[]{:S(2)}) %collective-permute-start.12) | collective-permute-done | bytes 81952 | tf_op jit(solution)/shard_map/ppermute | solution.py:689
  46.2 0.7 %shard_map.137 = f32[2,5,8,128]{3,2,1,0:T(8,128)} custom-call(f32[5,32,128]{2,1,0:T(8,128)S(1)} %shard_map.136.refs_0_, f32[5,32,128]{2,1,0:T(8,128)S(1)} %collective-permute-done.12.refs_1_, s32[2,128]{1,0:T(2,128)S(1)} %copy-done.4), custom_call_target="tpu_custom_call" | custom-call | flops 770000000 | bytes 81920 | tf_op jit(solution)/shard_map/pallas_call | solution.py:649
  (22 shorter events, 0.1 us)
Async XLA Ops:
  1.3 10.9 %copy-start.2 = (f32[5,5]{1,0:T(8,128)S(1)}, f32[5,5]{1,0:T(8,128)}, u32[]{:S(2)}) copy-start(f32[5,5]{1,0:T(8,128)} %refs_1_.11) | copy-start | bytes 304
  4.5 9.6 %collective-permute-start.2 = (f32[5,56,128]{2,1,0:T(8,128)S(1)}, f32[5,56,128]{2,1,0:T(8,128)S(1)}, u32[]{:S(2)}, u32[]{:S(2)}) collective-permute-start(f32[5,56,128]{2,1,0:T(8,128)S(1)} %get-tuple-element.37), channel_id=1, source_target_pairs={{0,1},{1,0},{2,3},{3,2},{4,5},{5,4},{6,7},{7,6},{8,9},{9,8},{10,11... | collective-permute-start | bytes 430088 | tf_op jit(solution)/shard_map/ppermute | solution.py:693
  7.5 10.4 %collective-permute-start = (f32[2,2,5,32,128]{4,3,2,1,0:T(8,128)S(1)}, f32[2,2,5,32,128]{4,3,2,1,0:T(8,128)S(1)}, u32[]{:S(2)}, u32[]{:S(2)}) collective-permute-start(f32[2,2,5,32,128]{4,3,2,1,0:T(8,128)S(1)} %get-tuple-element.35), channel_id=1, source_target_pairs={{0,2},{2,0},{4,6},{6,4},{8,10},{10,8},{12,14},{14,12},{16,18},{18,... | collective-permute-start | bytes 983048 | tf_op jit(solution)/shard_map/ppermute | solution.py:733
  7.5 10.5 %collective-permute-start.1 = (f32[2,2,5,32,128]{4,3,2,1,0:T(8,128)S(1)}, f32[2,2,5,32,128]{4,3,2,1,0:T(8,128)S(1)}, u32[]{:S(2)}, u32[]{:S(2)}) collective-permute-start(f32[2,2,5,32,128]{4,3,2,1,0:T(8,128)S(1)} %get-tuple-element.36), channel_id=1, source_target_pairs={{0,30},{2,4},{4,2},{6,8},{8,6},{10,12},{12,10},{14,16},{16,14},{18... | collective-permute-start | bytes 983048 | tf_op jit(solution)/shard_map/ppermute | solution.py:734
  12.1 1.9 %copy-start.1 = (f32[2,5,8,128]{3,2,1,0:T(8,128)S(1)}, f32[2,5,8,128]{3,2,1,0:T(8,128)}, u32[]{:S(2)}) copy-start(f32[2,5,8,128]{3,2,1,0:T(8,128)} %refs_0_.11) | copy-start | bytes 122884
  12.1 1.9 %copy-start.4 = (s32[2,128]{1,0:T(2,128)S(1)}, s32[2,128]{1,0:T(2,128)}, u32[]{:S(2)}) copy-start(s32[2,128]{1,0:T(2,128)} %refs_2_.5) | copy-start | bytes 3076
  12.1 2.2 %copy-start = (f32[2,5,64,16]{2,3,1,0:T(8,128)S(1)}, f32[2,5,64,16]{2,3,1,0:T(8,128)}, u32[]{:S(2)}) copy-start(f32[2,5,64,16]{2,3,1,0:T(8,128)} %param.14) | copy-start | bytes 122884
  12.1 2.2 %copy-start.3 = (s32[2,16]{1,0:T(2,128)S(1)}, s32[2,16]{1,0:T(2,128)}, u32[]{:S(2)}) copy-start(s32[2,16]{1,0:T(2,128)} %refs_1_.10) | copy-start | bytes 388
  14.2 6.7 %collective-permute-start.3 = (f32[6,32,128]{2,1,0:T(8,128)S(1)}, f32[6,32,128]{2,1,0:T(8,128)S(1)}, u32[]{:S(2)}, u32[]{:S(2)}) collective-permute-start(f32[6,32,128]{2,1,0:T(8,128)S(1)} %get-tuple-element.45), channel_id=1, source_target_pairs={{0,16},{2,18},{4,20},{6,22},{8,24},{10,26},{12,28},{14,30},{16,0},... | collective-permute-start | bytes 294920 | tf_op jit(solution)/shard_map/ppermute | solution.py:689
  20.9 8.3 %collective-permute-start.5 = (f32[11,32,128]{2,1,0:T(8,128)S(1)}, f32[11,32,128]{2,1,0:T(8,128)S(1)}, u32[]{:S(2)}, u32[]{:S(2)}) collective-permute-start(f32[11,32,128]{2,1,0:T(8,128)S(1)} %shard_map.127.refs_10_.refs_0_), channel_id=1, source_target_pairs={{0,4},{2,6},{4,0},{6,2},{8,12},{10,14},{12,8},{14,10},{16,20},{18,... | collective-permute-start | bytes 540680 | tf_op jit(solution)/shard_map/ppermute | solution.py:689
  23.7 7.8 %collective-permute-start.4 = (f32[5,56,128]{2,1,0:T(8,128)S(1)}, f32[5,56,128]{2,1,0:T(8,128)S(1)}, u32[]{:S(2)}, u32[]{:S(2)}) collective-permute-start(f32[5,56,128]{2,1,0:T(8,128)S(1)} %get-tuple-element.47), channel_id=1, source_target_pairs={{0,1},{1,0},{2,3},{3,2},{4,5},{5,4},{6,7},{7,6},{8,9},{9,8},{10,11... | collective-permute-start | bytes 430088 | tf_op jit(solution)/shard_map/ppermute | solution.py:693
  25.3 10.3 %collective-permute-start.6 = (f32[2,2,5,32,128]{4,3,2,1,0:T(8,128)S(1)}, f32[2,2,5,32,128]{4,3,2,1,0:T(8,128)S(1)}, u32[]{:S(2)}, u32[]{:S(2)}) collective-permute-start(f32[2,2,5,32,128]{4,3,2,1,0:T(8,128)S(1)} %get-tuple-element.50), channel_id=1, source_target_pairs={{0,2},{2,0},{4,6},{6,4},{8,10},{10,8},{12,14},{14,12},{16,18},{18,... | collective-permute-start | bytes 983048 | tf_op jit(solution)/shard_map/ppermute | solution.py:817
  25.3 10.3 %collective-permute-start.7 = (f32[2,2,5,32,128]{4,3,2,1,0:T(8,128)S(1)}, f32[2,2,5,32,128]{4,3,2,1,0:T(8,128)S(1)}, u32[]{:S(2)}, u32[]{:S(2)}) collective-permute-start(f32[2,2,5,32,128]{4,3,2,1,0:T(8,128)S(1)} %get-tuple-element.51), channel_id=1, source_target_pairs={{0,30},{2,4},{4,2},{6,8},{8,6},{10,12},{12,10},{14,16},{16,14},{18... | collective-permute-start | bytes 983048 | tf_op jit(solution)/shard_map/ppermute | solution.py:818
  29.2 8.0 %collective-permute-start.8 = (f32[11,32,128]{2,1,0:T(8,128)S(1)}, f32[11,32,128]{2,1,0:T(8,128)S(1)}, u32[]{:S(2)}, u32[]{:S(2)}) collective-permute-start(f32[11,32,128]{2,1,0:T(8,128)S(1)} %shard_map.129.refs_5_.refs_2_.refs_0_), channel_id=1, source_target_pairs={{0,8},{2,10},{4,12},{6,14},{8,0},{10,2},{12,4},{14,6},{16,24},{18,... | collective-permute-start | bytes 540680 | tf_op jit(solution)/shard_map/ppermute | solution.py:689
  30.0 5.6 %collective-permute-start.9 = (f32[5,16,128]{2,1,0:T(8,128)S(1)}, f32[5,16,128]{2,1,0:T(8,128)S(1)}, u32[]{:S(2)}, u32[]{:S(2)}) collective-permute-start(f32[5,16,128]{2,1,0:T(8,128)S(1)} %get-tuple-element.54), channel_id=1, source_target_pairs={{0,1},{1,0},{2,3},{3,2},{4,5},{5,4},{6,7},{7,6},{8,9},{9,8},{10,11... | collective-permute-start | bytes 122888 | tf_op jit(solution)/shard_map/ppermute | solution.py:831
  37.2 2.4 %collective-permute-start.10 = (f32[6,32,128]{2,1,0:T(8,128)S(1)}, f32[6,32,128]{2,1,0:T(8,128)S(1)}, u32[]{:S(2)}, u32[]{:S(2)}) collective-permute-start(f32[6,32,128]{2,1,0:T(8,128)S(1)} %get-tuple-element.56.refs_7_), channel_id=1, source_target_pairs={{0,2},{2,0},{4,6},{6,4},{8,10},{10,8},{12,14},{14,12},{16,18},{18,... | collective-permute-start | bytes 294920 | tf_op jit(solution)/shard_map/ppermute | solution.py:689
  37.8 7.1 %collective-permute-start.11 = (f32[5,32,128]{2,1,0:T(8,128)S(1)}, f32[5,32,128]{2,1,0:T(8,128)S(1)}, u32[]{:S(2)}, u32[]{:S(2)}) collective-permute-start(f32[5,32,128]{2,1,0:T(8,128)S(1)} %get-tuple-element.59.refs_0_), channel_id=1, source_target_pairs={{0,16},{2,18},{4,20},{6,22},{8,24},{10,26},{12,28},{14,30},{16,0},... | collective-permute-start | bytes 245768 | tf_op jit(solution)/shard_map/ppermute | solution.py:689
  44.9 1.3 %collective-permute-start.12 = (f32[5,32,128]{2,1,0:T(8,128)S(1)}, f32[5,32,128]{2,1,0:T(8,128)S(1)}, u32[]{:S(2)}, u32[]{:S(2)}) collective-permute-start(f32[5,32,128]{2,1,0:T(8,128)S(1)} %shard_map.136.refs_0_), channel_id=1, source_target_pairs={{0,2},{2,0},{4,6},{6,4},{8,10},{10,8},{12,14},{14,12},{16,18},{18,... | collective-permute-start | bytes 245768 | tf_op jit(solution)/shard_map/ppermute | solution.py:689

commit v4 on v3

--- a/solution.py
+++ b/solution.py
@@ -431,17 +431,19 @@
 
     def tile_step(tile, carry):
         rows = rows_of(tile)
-        for f in range(g.F):
-            halo = beyond_lanes.tile(f, rows)
-            packed = jnp.zeros((8, 128), f32)
-            for x in range(g.X):
-                open_xy = open_y * (1.0 - rx[x])
-                lap = plus(beyond_lanes.column(x, halo), beyond.columns(f, x, rows))
-                stepped = inside[f, x, rows, :] + dt[x, rows, :] * lap
+        halo = [beyond_lanes.tile(f, rows) for f in range(g.F)]
+        packed = [jnp.zeros((8, 128), f32) for _ in range(g.F)]
+        for x in range(g.X):
+            open_xy = open_y * (1.0 - rx[x])
+            d = dt[x, rows, :]
+            for f in range(g.F):
+                lap = plus(beyond_lanes.column(x, halo[f]), beyond.columns(f, x, rows))
+                stepped = inside[f, x, rows, :] + d * lap
                 done = open_xy * stepped + sides[f, x, rows, :]
                 u1[f, x, rows, :] = done
-                packed = pack_lanes(x, 0, done, packed)
-            my[f, rows, :] = jnp.where(lane < 64, packed_message(packed), my_in[f, rows, :])
+                packed[f] = pack_lanes(x, 0, done, packed[f])
+        for f in range(g.F):
+            my[f, rows, :] = jnp.where(lane < 64, packed_message(packed[f]), my_in[f, rows, :])
         send_ends(g, 0, lambda f, x: u1[f, x, rows, :], rows, ma, mb)
         return carry
 
@@ -495,16 +497,25 @@
             open_y * (kept[f, rows, :] + swapped[f, rows, :]) for f in range(g.F)
         ]
         past = packed_message(kept[g.F, rows, :] + swapped[g.F, rows, :]) * valid
+        lap_y, mixed_bound = [], []
         for f in range(g.F):
-            lap_y = unpack_lanes(f, 0, past, edge)
+            total = unpack_lanes(f, 0, past, edge)
             for shift, mask in masks:
-                lap_y = lap_y + mask * turn(bound[f], shift)
-            mixed_bound = mixed(table, f, bound)
-            for x in range(g.X):
-                slope_x = rx[x + 2]
-                open_xy = open_y * (1.0 - slope_x)
-                lap = plus(slope_x * lap_y + lx[x] * bound[f], beyond.columns(f, x, rows))
-                stepped = inside[f, x, rows, :] + slope_x * mixed_bound + dt[x, rows, :] * lap
+                total = total + mask * turn(bound[f], shift)
+            lap_y.append(total)
+            mixed_bound.append(mixed(table, f, bound))
+        for x in range(g.X):
+            slope_x, lap_x = rx[x + 2], lx[x]
+            open_xy = open_y * (1.0 - slope_x)
+            d = dt[x, rows, :]
+            along = slope_x * d
+            across = lap_x * d
+            for f in range(g.F):
+                share = slope_x * mixed_bound[f] + along * lap_y[f] + across * bound[f]
+                stepped = inside[f, x, rows, :] + share
+                beside = beyond.columns(f, x, rows)
+                if beside is not None:
+                    stepped = stepped + d * beside
                 done = open_xy * stepped + slope_x * bound[f] + sides[f, x, rows, :]
                 strided(out2, g, f, tile, x)[...] = done
         return carry
@@ -867,7 +878,9 @@
         after=[early],
     )
     other_bounds = swapped(bounds, 1)
-    moved = swapped(sums, nx // 2)
+    west = [(i, i + nx // 2) for i in range(0, nx // 2, 2)]
+    east = [(nx - 1 - i, nx - 1 - j) for i, j in west]
+    moved = lax.ppermute(sums, "gx", west + east)
     child_final, mark = call(
         bind(forward_last_kernel),
         [child_state.shape, (8, 128)],

time: 47 us -> 46.8 us (level)
  waiting for transfers between devices: 3.69 us -> 1.64 us
  starting transfers between devices: 18.4 us -> 20.2 us
    ppermute x0 -> x1, starting transfers between devices: none -> 3.63 us  [body(): moved = lax.ppermute(sums, 'gx', west + east)]
    ppermute x6 -> x5, waiting for transfers between devices: 3.67 us -> 1.62 us  [swapped(): return lax.ppermute(values, 'gx', [(i, i ^ distance) for i in range(nx)])]
    ppermute x6 -> x5, starting transfers between devices: 3.77 us -> 1.99 us  [swapped(): return lax.ppermute(values, 'gx', [(i, i ^ distance) for i in range(nx)])]
  transfers between devices with their start and end apart: 13 -> 13, of which waited for: 3 -> 2; matrix products, arithmetic and copies ran while one was open for 0% -> 0% of each run, Pallas kernels for 41% -> 41%
where the time goes in v4:
time: 46.8 us; the launch traced here: 46.6 us
  Pallas kernels  23.2 us (50%)
  starting transfers between devices  20.2 us (43%)
  waiting for transfers between devices  1.64 us (4%)
  between operations  1.5 us (3%)
    pallas_call x18, Pallas kernels, call(): pl.pallas_call(run, out_shape=out_shape, in_specs=[places[where] for wher...  23.2 us
    ppermute x2, starting transfers between devices, body(): fb = lax.ppermute(mb, 'gx', odds)  8.5 us
    ppermute x2, starting transfers between devices, to_y(): return lax.ppermute(message, 'gy', [(0, 1), (1, 0)])  4.56 us
    ppermute x1, starting transfers between devices, body(): moved = lax.ppermute(sums, 'gx', west + east)  3.63 us
    ppermute x5, starting transfers between devices, swapped(): return lax.ppermute(values, 'gx', [(i, i ^ distance) for i in range(nx)])  1.99 us
    ppermute x5, waiting for transfers between devices, swapped(): return lax.ppermute(values, 'gx', [(i, i ^ distance) for i in range(nx)])  1.62 us
    ppermute x1, starting transfers between devices, body(): gsn_other = lax.ppermute(sent, 'gy', [(0, 1), (1, 0)])  1.55 us
  transfers between devices with their start and end apart: 13, of which 2 were waited for; matrix products, arithmetic and copies ran while one was open for 0% of the time, Pallas kernels for 41%

profile of v4, /device:TPU:0, one launch (start us, length us, event | category | flops | bytes accessed | tf_op | source)
XLA Modules:
  0.0 46.6 jit_solution(822758340340397607)
XLA Ops:
  1.3 3.2 %shard_map.120 = (f32[5,16,32,128]{3,2,1,0:T(8,128)S(1)}, f32[5,16,32,128]{3,2,1,0:T(8,128)S(1)}, f32[16,32,128]{2,1,0:T(8,128)S(1)}, f32[5,16,32,128]{3,2,1,0:T...) custom-call(s32[1]{0:T(128)S(6)} %copy.19.refs_0_, ...), custom_call_target="tpu_custom_call" | custom-call | flops 3300000000 | bytes 9986048 | tf_op jit(solution)/shard_map/pallas_call | solution.py:660
  4.5 3.0 %collective-permute-start.2 = (f32[5,56,128]{2,1,0:T(8,128)S(1)}, f32[5,56,128]{2,1,0:T(8,128)S(1)}, u32[]{:S(2)}, u32[]{:S(2)}) collective-permute-start(f32[5,56,128]{2,1,0:T(8,128)S(1)} %get-tuple-element.37), channel_id=1, source_target_pairs={{0,1},{1,0},{2,3},{3,2},{4,5},{5,4},{6,7},{7,6},{8,9},{9,8},{10,11... | collective-permute-start | bytes 430088 | tf_op jit(solution)/shard_map/ppermute | solution.py:704
  7.5 0.0 collective-permute-start
  7.5 4.7 %collective-permute-start.1 = (f32[2,2,5,32,128]{4,3,2,1,0:T(8,128)S(1)}, f32[2,2,5,32,128]{4,3,2,1,0:T(8,128)S(1)}, u32[]{:S(2)}, u32[]{:S(2)}) collective-permute-start(f32[2,2,5,32,128]{4,3,2,1,0:T(8,128)S(1)} %get-tuple-element.36), channel_id=1, source_target_pairs={{0,30},{2,4},{4,2},{6,8},{8,6},{10,12},{12,10},{14,16},{16,14},{18... | collective-permute-start | bytes 983048 | tf_op jit(solution)/shard_map/ppermute | solution.py:745
  12.1 0.0 copy-start.3
  12.2 1.9 %shard_map.121.refs_5_.refs_1_ = f32[5,16,32,128]{3,2,1,0:T(8,128)S(1)} custom-call(f32[5,5]{1,0:T(8,128)S(1)} %copy-done.2, f32[5,16,32,128]{3,2,1,0:T(8,128)S(1)} %get-tuple-element.33.refs_1_, f32[16,32,128]{2,1,0:T(8,128)S(1)} %get-tuple-element.34.refs_2_.refs_3_), custom_call_target="tpu_custom_call" | custom-call | flops 2750000128 | bytes 2621440 | tf_op jit(solution)/shard_map/pallas_call | solution.py:660
  14.0 0.0 collective-permute-done.2.refs_1_.refs_4_.refs_2_.refs_5_
  14.1 0.1 shard_map.125
  14.2 0.1 collective-permute-start.3
  14.3 0.7 %shard_map.122.refs_1_ = f32[5,32,128]{2,1,0:T(8,128)S(1)} custom-call(f32[2,5,16,64]{3,2,1,0:T(8,128)S(1)} %bitcast.3, f32[5,56,128]{2,1,0:T(8,128)S(1)} %collective-permute-done.2.refs_1_.refs_4_.refs_2_.refs_5_, s32[2,16]{1,0:T(2,128)S(1)} %copy-done.3), custom_call_target="tpu_custom_call" | custom-call | flops 770000000 | bytes 163840 | tf_op jit(solution)/shard_map/pallas_call | solution.py:660
  15.0 0.9 %shard_map.123.refs_7_.refs_6_ = f32[5,16,32,128]{3,2,1,0:T(8,128)S(1)} custom-call(s32[1]{0:T(128)S(6)} %copy.19.refs_0_, f32[5,32,128]{2,1,0:T(8,128)S(1)} %shard_map.122.refs_1_), custom_call_target="tpu_custom_call" | custom-call | flops 770000000 | bytes 2621440 | tf_op jit(solution)/shard_map/pallas_call | solution.py:660
  15.9 2.0 %shard_map.124.refs_1_ = f32[5,16,32,128]{3,2,1,0:T(8,128)S(1)} custom-call(s32[1]{0:T(128)S(6)} %copy.19.refs_0_, f32[5,5]{1,0:T(8,128)S(1)} %copy-done.2, f32[5,16,32,128]{3,2,1,0:T(8,128)S(1)} %get-tuple-element.38.refs_2_, f32[5,16,32,128]{3,2,1,0:T(8,128)S(1)} %get-tuple-element.39.refs_3_, ...), custom_call_target="tpu_custom_call" | custom-call | flops 2750000128 | bytes 2621440 | tf_op jit(solution)/shard_map/pallas_call | solution.py:660
  17.9 0.0 collective-permute-done.refs_4_.refs_3_
  17.9 0.0 collective-permute-done.1.refs_5_.refs_4_
  17.9 2.6 %shard_map.126 = (f32[5,16,32,128]{3,2,1,0:T(8,128)S(1)}, f32[5,16,32,128]{3,2,1,0:T(8,128)S(1)}, f32[2,2,5,32,128]{4,3,2,1,0:T(8,128)S(1)}, f32[2,2,5,32,128]{4...) custom-call(s32[1]{0:T(128)S(6)} %copy.19.refs_0_, ...), custom_call_target="tpu_custom_call" | custom-call | flops 3300000000 | bytes 7168000 | tf_op jit(solution)/shard_map/pallas_call | solution.py:660
  20.5 0.4 collective-permute-done.3.refs_2_
  20.9 1.2 %collective-permute-start.5 = (f32[11,32,128]{2,1,0:T(8,128)S(1)}, f32[11,32,128]{2,1,0:T(8,128)S(1)}, u32[]{:S(2)}, u32[]{:S(2)}) collective-permute-start(f32[11,32,128]{2,1,0:T(8,128)S(1)} %shard_map.127.refs_10_.refs_0_), channel_id=1, source_target_pairs={{0,4},{2,6},{4,0},{6,2},{8,12},{10,14},{12,8},{14,10},{16,20},{18,... | collective-permute-start | bytes 540680 | tf_op jit(solution)/shard_map/ppermute | solution.py:700
  22.1 1.6 %shard_map.128 = (f32[5,16,32,128]{3,2,1,0:T(8,128)S(1)}, f32[2,2,5,32,128]{4,3,2,1,0:T(8,128)S(1)}, f32[2,2,5,32,128]{4,3,2,1,0:T(8,128)S(1)}, f32[5,56,128]{2,1,0:T(8,128)S(1)}) custom-call(s32[1]{0:T(128)S(6)} %copy.19.refs_0_, f32[5,16,32,128]{3,2,1,0:T(8,128)S(1)} %shard_map.121.refs_5_.refs_1_, ...), custom_call_target="tpu_custom_call", output_to_operand_aliasing={{1}: (7, {}), {2}: (8, {}), {3}: (9, {})} | custom-call | flops 2750000128 | bytes 4218880 | tf_op jit(solution)/shard_map/pallas_call | solution.py:660
  23.7 1.6 %collective-permute-start.4 = (f32[5,56,128]{2,1,0:T(8,128)S(1)}, f32[5,56,128]{2,1,0:T(8,128)S(1)}, u32[]{:S(2)}, u32[]{:S(2)}) collective-permute-start(f32[5,56,128]{2,1,0:T(8,128)S(1)} %get-tuple-element.47), channel_id=1, source_target_pairs={{0,1},{1,0},{2,3},{3,2},{4,5},{5,4},{6,7},{7,6},{8,9},{9,8},{10,11... | collective-permute-start | bytes 430088 | tf_op jit(solution)/shard_map/ppermute | solution.py:704
  25.3 3.8 %collective-permute-start.7 = (f32[2,2,5,32,128]{4,3,2,1,0:T(8,128)S(1)}, f32[2,2,5,32,128]{4,3,2,1,0:T(8,128)S(1)}, u32[]{:S(2)}, u32[]{:S(2)}) collective-permute-start(f32[2,2,5,32,128]{4,3,2,1,0:T(8,128)S(1)} %get-tuple-element.51), channel_id=1, source_target_pairs={{0,30},{2,4},{4,2},{6,8},{8,6},{10,12},{12,10},{14,16},{16,14},{18... | collective-permute-start | bytes 983048 | tf_op jit(solution)/shard_map/ppermute | solution.py:829
  29.1 0.1 collective-permute-start.8
  29.2 0.7 %shard_map.132 = (f32[5,16,128]{2,1,0:T(8,128)S(1)}, f32[5,16,128]{2,1,0:T(8,128)S(1)}) custom-call(f32[5,32,128]{2,1,0:T(8,128)S(1)} %get-tuple-element.52.refs_0_, s32[2,16]{1,0:T(2,128)S(1)} %copy-done.3, f32[11,32,128]{2,1,0:T(8,128)S(1)} %shard_map.129.refs_5_.refs_2_.refs_0_), custom_call_target="tpu_custom_call" | custom-call | flops 660000000 | bytes 163840 | tf_op jit(solution)/shard_map/pallas_call | solution.py:660
  29.9 1.6 %collective-permute-start.9 = (f32[5,16,128]{2,1,0:T(8,128)S(1)}, f32[5,16,128]{2,1,0:T(8,128)S(1)}, u32[]{:S(2)}, u32[]{:S(2)}) collective-permute-start(f32[5,16,128]{2,1,0:T(8,128)S(1)} %get-tuple-element.54), channel_id=1, source_target_pairs={{0,1},{1,0},{2,3},{3,2},{4,5},{5,4},{6,7},{7,6},{8,9},{9,8},{10,11... | collective-permute-start | bytes 122888 | tf_op jit(solution)/shard_map/ppermute | solution.py:842
  31.5 2.0 %shard_map.130.refs_4_.refs_0_ = f32[5,16,32,128]{3,2,1,0:T(8,128)S(1)} custom-call(s32[1]{0:T(128)S(6)} %copy.19.refs_0_, f32[5,5]{1,0:T(8,128)S(1)} %copy-done.2, f32[5,16,32,128]{3,2,1,0:T(8,128)S(1)} %get-tuple-element.48.refs_2_, f32[5,16,32,128]{3,2,1,0:T(8,128)S(1)} %get-tuple-element.49.refs_3_, ...), custom_call_target="tpu_custom_call" | custom-call | flops 2750000128 | bytes 2621440 | tf_op jit(solution)/shard_map/pallas_call | solution.py:660
  33.5 2.0 %shard_map.131.refs_5_.refs_2_ = f32[5,16,32,128]{3,2,1,0:T(8,128)S(1)} custom-call(f32[5,5]{1,0:T(8,128)S(1)} %copy-done.2, f32[5,16,32,128]{3,2,1,0:T(8,128)S(1)} %get-tuple-element.46.refs_2_.refs_1_, f32[16,32,128]{2,1,0:T(8,128)S(1)} %get-tuple-element.34.refs_2_.refs_3_, f32[5,56,128]{2,1,0:T(8,128)S(1)} %collective-permute-done.4.refs_4_.refs_3_, ...), custom_call_target="tpu_custom_call" | custom-call | flops 2750000128 | bytes 2621440 | tf_op jit(solution)/shard_map/pallas_call | solution.py:660
  35.6 1.5 %shard_map.133 = (f32[5,32,16,128]{3,2,1,0:T(8,128)}, f32[2,5,16,64]{3,2,1,0:T(8,128)}, f32[8,128]{1,0:T(8,128)S(1)}) custom-call(f32[5,16,32,128]{3,2,1,0:T(8,128)S(1)} %shard_map.130.refs_4_.refs_0_, f32[2,2,5,32,128]{4,3,2,1,0:T(8,128)S(1)} %collective-permute-done.6.refs_1_.refs_4_, f32[2,2,5,32,128]{4,3,2,1,0:T(8,128)S(1)} %collective-permute-done.7.refs_2_.refs_5_, ...), custom_call_target="tpu_custom_call" | custom-call | flops 2750000128 | bytes 2711552 | tf_op jit(solution)/shard_map/pallas_call | solution.py:660
  37.1 0.6 %collective-permute-start.10 = (f32[6,32,128]{2,1,0:T(8,128)S(1)}, f32[6,32,128]{2,1,0:T(8,128)S(1)}, u32[]{:S(2)}, u32[]{:S(2)}) collective-permute-start(f32[6,32,128]{2,1,0:T(8,128)S(1)} %get-tuple-element.56.refs_7_), channel_id=1, source_target_pairs={{0,2},{2,0},{4,6},{6,4},{8,10},{10,8},{12,14},{14,12},{16,18},{18,... | collective-permute-start | bytes 294920 | tf_op jit(solution)/shard_map/ppermute | solution.py:700
  37.7 3.6 %collective-permute-start.11 = (f32[5,32,128]{2,1,0:T(8,128)S(1)}, f32[5,32,128]{2,1,0:T(8,128)S(1)}, u32[]{:S(2)}, u32[]{:S(2)}) collective-permute-start(f32[5,32,128]{2,1,0:T(8,128)S(1)} %get-tuple-element.59.refs_0_), channel_id=1, source_target_pairs={{0,16},{4,20},{8,24},{12,28},{30,14},{26,10},{22,6},{18,2},{1,17},... | collective-permute-start | bytes 245768 | tf_op jit(solution)/shard_map/ppermute | solution.py:883
  41.4 3.2 %shard_map.135 = (f32[5,32,16,128]{3,2,1,0:T(8,128)}, f32[8,128]{1,0:T(8,128)S(1)}) custom-call(s32[1]{0:T(128)S(6)} %copy.19.refs_0_, f32[5,5]{1,0:T(8,128)S(1)} %copy-done.2, f32[5,16,32,128]{3,2,1,0:T(8,128)S(1)} %shard_map.131.refs_5_.refs_2_, f32[16,32,128]{2,1,0:T(8,128)S(1)} %get-tuple-element.34.refs_2_.refs_3_, ...), custom_call_target="tpu_custom_call" | custom-call | flops 3300000000 | bytes 2629632 | tf_op jit(solution)/shard_map/pallas_call | solution.py:660
  44.6 0.1 collective-permute-start.12
  44.6 1.3 %collective-permute-done.12.refs_1_ = f32[5,32,128]{2,1,0:T(8,128)S(1)} collective-permute-done((f32[5,32,128]{2,1,0:T(8,128)S(1)}, f32[5,32,128]{2,1,0:T(8,128)S(1)}, u32[]{:S(2)}, u32[]{:S(2)}) %collective-permute-start.12) | collective-permute-done | bytes 81952 | tf_op jit(solution)/shard_map/ppermute | solution.py:700
  45.9 0.7 %shard_map.137 = f32[2,5,8,128]{3,2,1,0:T(8,128)} custom-call(f32[5,32,128]{2,1,0:T(8,128)S(1)} %shard_map.136.refs_0_, f32[5,32,128]{2,1,0:T(8,128)S(1)} %collective-permute-done.12.refs_1_, s32[2,128]{1,0:T(2,128)S(1)} %copy-done.4), custom_call_target="tpu_custom_call" | custom-call | flops 770000000 | bytes 81920 | tf_op jit(solution)/shard_map/pallas_call | solution.py:660
  (22 shorter events, 0.1 us)
Async XLA Ops:
  1.3 10.9 %copy-start.2 = (f32[5,5]{1,0:T(8,128)S(1)}, f32[5,5]{1,0:T(8,128)}, u32[]{:S(2)}) copy-start(f32[5,5]{1,0:T(8,128)} %refs_1_.11) | copy-start | bytes 304
  4.5 9.6 %collective-permute-start.2 = (f32[5,56,128]{2,1,0:T(8,128)S(1)}, f32[5,56,128]{2,1,0:T(8,128)S(1)}, u32[]{:S(2)}, u32[]{:S(2)}) collective-permute-start(f32[5,56,128]{2,1,0:T(8,128)S(1)} %get-tuple-element.37), channel_id=1, source_target_pairs={{0,1},{1,0},{2,3},{3,2},{4,5},{5,4},{6,7},{7,6},{8,9},{9,8},{10,11... | collective-permute-start | bytes 430088 | tf_op jit(solution)/shard_map/ppermute | solution.py:704
  7.5 10.4 %collective-permute-start = (f32[2,2,5,32,128]{4,3,2,1,0:T(8,128)S(1)}, f32[2,2,5,32,128]{4,3,2,1,0:T(8,128)S(1)}, u32[]{:S(2)}, u32[]{:S(2)}) collective-permute-start(f32[2,2,5,32,128]{4,3,2,1,0:T(8,128)S(1)} %get-tuple-element.35), channel_id=1, source_target_pairs={{0,2},{2,0},{4,6},{6,4},{8,10},{10,8},{12,14},{14,12},{16,18},{18,... | collective-permute-start | bytes 983048 | tf_op jit(solution)/shard_map/ppermute | solution.py:744
  7.5 10.5 %collective-permute-start.1 = (f32[2,2,5,32,128]{4,3,2,1,0:T(8,128)S(1)}, f32[2,2,5,32,128]{4,3,2,1,0:T(8,128)S(1)}, u32[]{:S(2)}, u32[]{:S(2)}) collective-permute-start(f32[2,2,5,32,128]{4,3,2,1,0:T(8,128)S(1)} %get-tuple-element.36), channel_id=1, source_target_pairs={{0,30},{2,4},{4,2},{6,8},{8,6},{10,12},{12,10},{14,16},{16,14},{18... | collective-permute-start | bytes 983048 | tf_op jit(solution)/shard_map/ppermute | solution.py:745
  12.1 1.9 %copy-start.1 = (f32[2,5,8,128]{3,2,1,0:T(8,128)S(1)}, f32[2,5,8,128]{3,2,1,0:T(8,128)}, u32[]{:S(2)}) copy-start(f32[2,5,8,128]{3,2,1,0:T(8,128)} %refs_0_.11) | copy-start | bytes 122884
  12.1 1.9 %copy-start.4 = (s32[2,128]{1,0:T(2,128)S(1)}, s32[2,128]{1,0:T(2,128)}, u32[]{:S(2)}) copy-start(s32[2,128]{1,0:T(2,128)} %refs_2_.5) | copy-start | bytes 3076
  12.1 2.2 %copy-start = (f32[2,5,64,16]{2,3,1,0:T(8,128)S(1)}, f32[2,5,64,16]{2,3,1,0:T(8,128)}, u32[]{:S(2)}) copy-start(f32[2,5,64,16]{2,3,1,0:T(8,128)} %param.14) | copy-start | bytes 122884
  12.1 2.2 %copy-start.3 = (s32[2,16]{1,0:T(2,128)S(1)}, s32[2,16]{1,0:T(2,128)}, u32[]{:S(2)}) copy-start(s32[2,16]{1,0:T(2,128)} %refs_1_.10) | copy-start | bytes 388
  14.2 6.7 %collective-permute-start.3 = (f32[6,32,128]{2,1,0:T(8,128)S(1)}, f32[6,32,128]{2,1,0:T(8,128)S(1)}, u32[]{:S(2)}, u32[]{:S(2)}) collective-permute-start(f32[6,32,128]{2,1,0:T(8,128)S(1)} %get-tuple-element.45), channel_id=1, source_target_pairs={{0,16},{2,18},{4,20},{6,22},{8,24},{10,26},{12,28},{14,30},{16,0},... | collective-permute-start | bytes 294920 | tf_op jit(solution)/shard_map/ppermute | solution.py:700
  20.9 8.2 %collective-permute-start.5 = (f32[11,32,128]{2,1,0:T(8,128)S(1)}, f32[11,32,128]{2,1,0:T(8,128)S(1)}, u32[]{:S(2)}, u32[]{:S(2)}) collective-permute-start(f32[11,32,128]{2,1,0:T(8,128)S(1)} %shard_map.127.refs_10_.refs_0_), channel_id=1, source_target_pairs={{0,4},{2,6},{4,0},{6,2},{8,12},{10,14},{12,8},{14,10},{16,20},{18,... | collective-permute-start | bytes 540680 | tf_op jit(solution)/shard_map/ppermute | solution.py:700
  23.7 7.8 %collective-permute-start.4 = (f32[5,56,128]{2,1,0:T(8,128)S(1)}, f32[5,56,128]{2,1,0:T(8,128)S(1)}, u32[]{:S(2)}, u32[]{:S(2)}) collective-permute-start(f32[5,56,128]{2,1,0:T(8,128)S(1)} %get-tuple-element.47), channel_id=1, source_target_pairs={{0,1},{1,0},{2,3},{3,2},{4,5},{5,4},{6,7},{7,6},{8,9},{9,8},{10,11... | collective-permute-start | bytes 430088 | tf_op jit(solution)/shard_map/ppermute | solution.py:704
  25.3 10.3 %collective-permute-start.6 = (f32[2,2,5,32,128]{4,3,2,1,0:T(8,128)S(1)}, f32[2,2,5,32,128]{4,3,2,1,0:T(8,128)S(1)}, u32[]{:S(2)}, u32[]{:S(2)}) collective-permute-start(f32[2,2,5,32,128]{4,3,2,1,0:T(8,128)S(1)} %get-tuple-element.50), channel_id=1, source_target_pairs={{0,2},{2,0},{4,6},{6,4},{8,10},{10,8},{12,14},{14,12},{16,18},{18,... | collective-permute-start | bytes 983048 | tf_op jit(solution)/shard_map/ppermute | solution.py:828
  25.3 10.3 %collective-permute-start.7 = (f32[2,2,5,32,128]{4,3,2,1,0:T(8,128)S(1)}, f32[2,2,5,32,128]{4,3,2,1,0:T(8,128)S(1)}, u32[]{:S(2)}, u32[]{:S(2)}) collective-permute-start(f32[2,2,5,32,128]{4,3,2,1,0:T(8,128)S(1)} %get-tuple-element.51), channel_id=1, source_target_pairs={{0,30},{2,4},{4,2},{6,8},{8,6},{10,12},{12,10},{14,16},{16,14},{18... | collective-permute-start | bytes 983048 | tf_op jit(solution)/shard_map/ppermute | solution.py:829
  29.1 8.0 %collective-permute-start.8 = (f32[11,32,128]{2,1,0:T(8,128)S(1)}, f32[11,32,128]{2,1,0:T(8,128)S(1)}, u32[]{:S(2)}, u32[]{:S(2)}) collective-permute-start(f32[11,32,128]{2,1,0:T(8,128)S(1)} %shard_map.129.refs_5_.refs_2_.refs_0_), channel_id=1, source_target_pairs={{0,8},{2,10},{4,12},{6,14},{8,0},{10,2},{12,4},{14,6},{16,24},{18,... | collective-permute-start | bytes 540680 | tf_op jit(solution)/shard_map/ppermute | solution.py:700
  29.9 5.6 %collective-permute-start.9 = (f32[5,16,128]{2,1,0:T(8,128)S(1)}, f32[5,16,128]{2,1,0:T(8,128)S(1)}, u32[]{:S(2)}, u32[]{:S(2)}) collective-permute-start(f32[5,16,128]{2,1,0:T(8,128)S(1)} %get-tuple-element.54), channel_id=1, source_target_pairs={{0,1},{1,0},{2,3},{3,2},{4,5},{5,4},{6,7},{7,6},{8,9},{9,8},{10,11... | collective-permute-start | bytes 122888 | tf_op jit(solution)/shard_map/ppermute | solution.py:842
  37.1 4.2 %collective-permute-start.10 = (f32[6,32,128]{2,1,0:T(8,128)S(1)}, f32[6,32,128]{2,1,0:T(8,128)S(1)}, u32[]{:S(2)}, u32[]{:S(2)}) collective-permute-start(f32[6,32,128]{2,1,0:T(8,128)S(1)} %get-tuple-element.56.refs_7_), channel_id=1, source_target_pairs={{0,2},{2,0},{4,6},{6,4},{8,10},{10,8},{12,14},{14,12},{16,18},{18,... | collective-permute-start | bytes 294920 | tf_op jit(solution)/shard_map/ppermute | solution.py:700
  37.7 6.8 %collective-permute-start.11 = (f32[5,32,128]{2,1,0:T(8,128)S(1)}, f32[5,32,128]{2,1,0:T(8,128)S(1)}, u32[]{:S(2)}, u32[]{:S(2)}) collective-permute-start(f32[5,32,128]{2,1,0:T(8,128)S(1)} %get-tuple-element.59.refs_0_), channel_id=1, source_target_pairs={{0,16},{4,20},{8,24},{12,28},{30,14},{26,10},{22,6},{18,2},{1,17},... | collective-permute-start | bytes 245768 | tf_op jit(solution)/shard_map/ppermute | solution.py:883
  44.6 1.3 %collective-permute-start.12 = (f32[5,32,128]{2,1,0:T(8,128)S(1)}, f32[5,32,128]{2,1,0:T(8,128)S(1)}, u32[]{:S(2)}, u32[]{:S(2)}) collective-permute-start(f32[5,32,128]{2,1,0:T(8,128)S(1)} %shard_map.136.refs_0_), channel_id=1, source_target_pairs={{0,2},{2,0},{4,6},{6,4},{8,10},{10,8},{12,14},{14,12},{16,18},{18,... | collective-permute-start | bytes 245768 | tf_op jit(solution)/shard_map/ppermute | solution.py:700

commit v5 on v4

--- a/solution.py
+++ b/solution.py
@@ -450,8 +450,7 @@
     lax.fori_loop(0, g.tiles, tile_step, 0)
 
 
-def adjoint_last_kernel(g, inside, fa, fb, gsn_own, gsn_other, out, gsn, mark):
-    mark[...] = jnp.zeros((8, 128), f32)
+def adjoint_last_kernel(g, inside, fa, fb, fy, gsn_own, out, gsn):
     out2 = out.reshape(g.F * g.K * g.X, g.Y)
     beyond = Beyond(g, 1, fa, fb)
 
@@ -469,7 +468,7 @@
         span = gsn.shape[3]
         for f in range(g.F):
             gsn[here, f] = gsn_own[f, :, :span]
-            gsn[1 - here, f] = gsn_other[f, :, :span]
+            gsn[1 - here, f] = fy[f, g.K : g.K + g.X, :span]
     else:
         gsn[...] = jnp.zeros(gsn.shape, f32)
 
@@ -523,7 +522,7 @@
     lax.fori_loop(0, g.tiles, tile_step, 0)
 
 
-def side_sums_kernel(g, dsn, tsn, gsn, sent, wide):
+def side_sums_kernel(g, dsn, tsn, my_in, gsn, my, wide):
     here = lax.axis_index("gy")
     shift = column_of(jnp.where(here == 0, tsn[0:1, :], tsn[1:2, :]))
     lane = lax.broadcasted_iota(jnp.int32, (g.X, 128), 1)
@@ -538,7 +537,7 @@
             whole = shift_levels(levels, shift, 1)
             moved = turn(whole, 64)
             gsn[f] = jnp.where(here == 0, whole, moved)
-            sent[f] = jnp.where(here == 0, moved, whole)
+            my[f, g.K : g.K + g.X, :] = jnp.where(here == 0, moved, whole)
 
 
 def side_bounds_kernel(g, sn, fsn, tsn, bsn, wide):
@@ -622,18 +621,19 @@
     out[...] = first[...] + second[...]
 
 
-def spread_kernel(g, kept, swapped, terrain, out):
+def spread_kernel(g, flip, sums, terrain, out):
     here = lax.axis_index("gx")
-    odd = here % 2
-    span = out.shape[2]
+    pair = (here ^ flip) // 2
+    count = out.shape[1]
     row = lax.broadcasted_iota(jnp.int32, (8, 128), 0)
     zero = jnp.zeros((8, 128), f32)
-    for e in range(2):
-        start = jnp.broadcast_to(here * span - terrain[e : e + 1, :], (8, 128)) + 8
+    base = jnp.where(here % 2 == 1, terrain[1:2, :], terrain[0:1, :])
+    for block in range(count // 8):
+        start = jnp.broadcast_to(pair * count + 8 * block - base, (8, 128)) + 8
         inside = (start > 0) & (start < g.K + 8)
         tile, rest = start >> 3, start & 7
         for f in range(g.F):
-            chosen = jnp.where(odd == e, kept[f], swapped[f])
+            chosen = sums[f]
             tiles = [zero] + [chosen[8 * i : 8 * i + 8] for i in range(g.tiles)] + [zero]
             low, high = zero, zero
             for i in range(g.tiles + 1):
@@ -645,7 +645,24 @@
                 up_high = pltpu.roll(high, 8 - step, 0)
                 low = jnp.where(moves, jnp.where(row < 8 - step, up_low, up_high), low)
                 high = jnp.where(moves, up_high, high)
-            out[e, f] = jnp.where(inside, low, zero)[:span]
+            out[f, 8 * block : 8 * block + 8, :] = jnp.where(inside, low, zero)
+
+
+def halves_kernel(g, own, moved, kept, sent):
+    odd = odd_column()
+    span = kept.shape[1]
+    for f in range(g.F):
+        both = own[f] + moved[f]
+        low, high = both[:span], both[span:]
+        kept[f] = jnp.where(odd, high, low)
+        sent[f] = jnp.where(odd, low, high)
+
+
+def assemble_kernel(g, kept, other, out):
+    odd = lax.axis_index("gx") % 2
+    for f in range(g.F):
+        out[odd, f] = kept[f]
+        out[1 - odd, f] = other[f]
 
 
 def call(kernel, outs, scratch, ins, time, aliases=None, after=()):
@@ -824,22 +841,22 @@
         {7: 1, 8: 2, 9: 3},
         after=[state],
     )
+    if g.pair:
+        gsn_own, my = call(
+            bind(side_sums_kernel),
+            [(F, X, 128), lane_shape],
+            [(128, 128)],
+            [("v", dsn), ("v", terrain_sn), ("v", my)],
+            0.6,
+            {2: 1},
+        )
+    else:
+        gsn_own = dsn
     fy = to_y(my)
     fa = lax.ppermute(ma, "gx", evens)
     fb = lax.ppermute(mb, "gx", odds)
 
-    state = add(state, moved, [u1])
-    gsn_own = gsn_other = dsn
-    if g.pair:
-        gsn_own, sent = call(
-            bind(side_sums_kernel),
-            [(F, X, 128)] * 2,
-            [(128, 128)],
-            [("v", dsn), ("v", terrain_sn)],
-            0.6,
-            after=[state],
-        )
-        gsn_other = lax.ppermute(sent, "gy", [(0, 1), (1, 0)])
+    state = add(state, moved, [gsn_own])
     distance = 4
     while distance < nx // 4:
         state = state + swapped(state, distance)
@@ -861,26 +878,21 @@
         2.5,
         after=[inside_a],
     )
-    grad_state, grad_sn, early = call(
-        bind(adjoint_last_kernel),
-        [child_state.shape, sn_turned.shape, (8, 128)],
-        [],
-        [("v", inside_a), ("v", fa), ("v", fb), ("v", gsn_own), ("v", gsn_other)],
-        2.5,
-        after=[inside_u],
-    )
     sums, bounds = call(
         bind(split_kernel),
         [edge_shape, (F + 1, K, 128)],
         [],
         [("v", state), ("v", moved)],
         0.1,
-        after=[early],
+        after=[inside_u],
     )
     other_bounds = swapped(bounds, 1)
-    west = [(i, i + nx // 2) for i in range(0, nx // 2, 2)]
-    east = [(nx - 1 - i, nx - 1 - j) for i, j in west]
-    moved = lax.ppermute(sums, "gx", west + east)
+    span = parent_we.shape[2]
+    pair_shape = (F, 2 * span, 128)
+    (gone,) = call(
+        bind(spread_kernel, nx // 2), [pair_shape], [], [("v", sums), ("v", terrain_we)], 0.7
+    )
+    moved = swapped(gone, nx // 2)
     child_final, mark = call(
         bind(forward_last_kernel),
         [child_state.shape, (8, 128)],
@@ -898,14 +910,32 @@
         ],
         3,
     )
-    sums = add(sums, moved, [mark])
-    other_sums = swapped(sums, 1)
+    (own,) = call(
+        bind(spread_kernel, 0),
+        [pair_shape],
+        [],
+        [("v", sums), ("v", terrain_we)],
+        0.7,
+        after=[mark],
+    )
+    kept, sent = call(
+        bind(halves_kernel), [(F, span, 128)] * 2, [], [("v", own), ("v", moved)], 0.1
+    )
+    other_kept = swapped(sent, 1)
+    grad_state, grad_sn = call(
+        bind(adjoint_last_kernel),
+        [child_state.shape, sn_turned.shape],
+        [],
+        [("v", inside_a), ("v", fa), ("v", fb), ("v", fy), ("v", gsn_own)],
+        2.5,
+        after=[kept],
+    )
     (grad_we,) = call(
-        bind(spread_kernel),
+        bind(assemble_kernel),
         [parent_we.shape],
         [],
-        [("v", sums), ("v", other_sums), ("v", terrain_we)],
-        0.7,
+        [("v", kept), ("v", other_kept)],
+        0.1,
     )
     if g.pair:
         grad_sn = jnp.swapaxes(grad_sn, 2, 3)

time: 46.8 us -> 45.2 us (0.966)
  starting transfers between devices: 20.2 us -> 17.2 us
  waiting for transfers between devices: 1.64 us -> 3.11 us
    ppermute x2 -> x0, starting transfers between devices: 5.18 us -> none  [the longest x1 3.63 us: body(): moved = lax.ppermute(sums, 'gx', west + east)]
    ppermute x5 -> x6, starting transfers between devices: 1.99 us -> 4.1 us  [swapped(): return lax.ppermute(values, 'gx', [(i, i ^ distance) for i in range(nx)])]
    ppermute x5 -> x6, waiting for transfers between devices: 1.62 us -> 3.1 us  [swapped(): return lax.ppermute(values, 'gx', [(i, i ^ distance) for i in range(nx)])]
    pallas_call x18 -> x20, Pallas kernels: 23.2 us -> 23.2 us  [call(): pl.pallas_call(run, out_shape=out_shape, in_specs=[places[where] for wher...]
  transfers between devices with their start and end apart: 13 -> 12, of which waited for: 2 -> 2; matrix products, arithmetic and copies ran while one was open for 0% -> 0% of each run, Pallas kernels for 41% -> 43%
where the time goes in v5:
time: 45.2 us; the launch traced here: 45 us
  Pallas kernels  23.2 us (51%)
  starting transfers between devices  17.2 us (38%)
  waiting for transfers between devices  3.11 us (7%)
  between operations  1.49 us (3%)
    pallas_call x20, Pallas kernels, call(): pl.pallas_call(run, out_shape=out_shape, in_specs=[places[where] for wher...  23.2 us
    ppermute x2, starting transfers between devices, body(): fb = lax.ppermute(mb, 'gx', odds)  8.5 us
    ppermute x2, starting transfers between devices, to_y(): return lax.ppermute(message, 'gy', [(0, 1), (1, 0)])  4.56 us
    ppermute x6, starting transfers between devices, swapped(): return lax.ppermute(values, 'gx', [(i, i ^ distance) for i in range(nx)])  4.1 us
    ppermute x6, waiting for transfers between devices, swapped(): return lax.ppermute(values, 'gx', [(i, i ^ distance) for i in range(nx)])  3.1 us
  transfers between devices with their start and end apart: 12, of which 2 were waited for; matrix products, arithmetic and copies ran while one was open for 0% of the time, Pallas kernels for 43%

profile of v5, /device:TPU:0, one launch (start us, length us, event | category | flops | bytes accessed | tf_op | source)
XLA Modules:
  0.0 45.0 jit_solution(10075374807881868836)
XLA Ops:
  1.3 3.2 %shard_map.120 = (f32[5,16,32,128]{3,2,1,0:T(8,128)S(1)}, f32[5,16,32,128]{3,2,1,0:T(8,128)S(1)}, f32[16,32,128]{2,1,0:T(8,128)S(1)}, f32[5,16,32,128]{3,2,1,0:T...) custom-call(s32[1]{0:T(128)S(6)} %copy.21.refs_0_, ...), custom_call_target="tpu_custom_call" | custom-call | flops 3300000000 | bytes 9986048 | tf_op jit(solution)/shard_map/pallas_call | solution.py:677
  4.5 3.0 %collective-permute-start.2 = (f32[5,56,128]{2,1,0:T(8,128)S(1)}, f32[5,56,128]{2,1,0:T(8,128)S(1)}, u32[]{:S(2)}, u32[]{:S(2)}) collective-permute-start(f32[5,56,128]{2,1,0:T(8,128)S(1)} %get-tuple-element.38), channel_id=1, source_target_pairs={{0,1},{1,0},{2,3},{3,2},{4,5},{5,4},{6,7},{7,6},{8,9},{9,8},{10,11... | collective-permute-start | bytes 430088 | tf_op jit(solution)/shard_map/ppermute | solution.py:721
  7.5 0.0 collective-permute-start
  7.5 4.7 %collective-permute-start.1 = (f32[2,2,5,32,128]{4,3,2,1,0:T(8,128)S(1)}, f32[2,2,5,32,128]{4,3,2,1,0:T(8,128)S(1)}, u32[]{:S(2)}, u32[]{:S(2)}) collective-permute-start(f32[2,2,5,32,128]{4,3,2,1,0:T(8,128)S(1)} %get-tuple-element.37), channel_id=1, source_target_pairs={{0,30},{2,4},{4,2},{6,8},{8,6},{10,12},{12,10},{14,16},{16,14},{18... | collective-permute-start | bytes 983048 | tf_op jit(solution)/shard_map/ppermute | solution.py:762
  12.1 0.0 copy-start.3
  12.2 1.9 %shard_map.121.refs_5_.refs_1_ = f32[5,16,32,128]{3,2,1,0:T(8,128)S(1)} custom-call(f32[5,5]{1,0:T(8,128)S(1)} %copy-done.2, f32[5,16,32,128]{3,2,1,0:T(8,128)S(1)} %get-tuple-element.34.refs_1_, f32[16,32,128]{2,1,0:T(8,128)S(1)} %get-tuple-element.35.refs_2_.refs_3_), custom_call_target="tpu_custom_call" | custom-call | flops 2750000128 | bytes 2621440 | tf_op jit(solution)/shard_map/pallas_call | solution.py:677
  14.1 0.1 shard_map.125
  14.2 0.1 collective-permute-start.3
  14.3 0.7 %shard_map.122.refs_1_ = f32[5,32,128]{2,1,0:T(8,128)S(1)} custom-call(f32[2,5,16,64]{3,2,1,0:T(8,128)S(1)} %bitcast.3, f32[5,56,128]{2,1,0:T(8,128)S(1)} %collective-permute-done.2.refs_1_.refs_4_.refs_2_.refs_5_, s32[2,16]{1,0:T(2,128)S(1)} %copy-done.3), custom_call_target="tpu_custom_call" | custom-call | flops 770000000 | bytes 163840 | tf_op jit(solution)/shard_map/pallas_call | solution.py:677
  15.0 0.9 %shard_map.123.refs_7_.refs_6_ = f32[5,16,32,128]{3,2,1,0:T(8,128)S(1)} custom-call(s32[1]{0:T(128)S(6)} %copy.21.refs_0_, f32[5,32,128]{2,1,0:T(8,128)S(1)} %shard_map.122.refs_1_), custom_call_target="tpu_custom_call" | custom-call | flops 770000000 | bytes 2621440 | tf_op jit(solution)/shard_map/pallas_call | solution.py:677
  15.9 2.0 %shard_map.124.refs_1_ = f32[5,16,32,128]{3,2,1,0:T(8,128)S(1)} custom-call(s32[1]{0:T(128)S(6)} %copy.21.refs_0_, f32[5,5]{1,0:T(8,128)S(1)} %copy-done.2, f32[5,16,32,128]{3,2,1,0:T(8,128)S(1)} %get-tuple-element.39.refs_2_, f32[5,16,32,128]{3,2,1,0:T(8,128)S(1)} %get-tuple-element.40.refs_3_, ...), custom_call_target="tpu_custom_call" | custom-call | flops 2750000128 | bytes 2621440 | tf_op jit(solution)/shard_map/pallas_call | solution.py:677
  17.9 0.0 collective-permute-done.refs_4_.refs_3_
  17.9 0.0 collective-permute-done.1.refs_5_.refs_4_
  17.9 2.6 %shard_map.126 = (f32[5,16,32,128]{3,2,1,0:T(8,128)S(1)}, f32[5,16,32,128]{3,2,1,0:T(8,128)S(1)}, f32[2,2,5,32,128]{4,3,2,1,0:T(8,128)S(1)}, f32[2,2,5,32,128]{4...) custom-call(s32[1]{0:T(128)S(6)} %copy.21.refs_0_, ...), custom_call_target="tpu_custom_call" | custom-call | flops 3300000000 | bytes 7168000 | tf_op jit(solution)/shard_map/pallas_call | solution.py:677
  20.5 0.4 collective-permute-done.3.refs_2_
  20.9 1.2 %collective-permute-start.5 = (f32[11,32,128]{2,1,0:T(8,128)S(1)}, f32[11,32,128]{2,1,0:T(8,128)S(1)}, u32[]{:S(2)}, u32[]{:S(2)}) collective-permute-start(f32[11,32,128]{2,1,0:T(8,128)S(1)} %shard_map.127.refs_10_.refs_0_), channel_id=1, source_target_pairs={{0,4},{2,6},{4,0},{6,2},{8,12},{10,14},{12,8},{14,10},{16,20},{18,... | collective-permute-start | bytes 540680 | tf_op jit(solution)/shard_map/ppermute | solution.py:717
  22.1 1.6 %shard_map.128 = (f32[5,16,32,128]{3,2,1,0:T(8,128)S(1)}, f32[2,2,5,32,128]{4,3,2,1,0:T(8,128)S(1)}, f32[2,2,5,32,128]{4,3,2,1,0:T(8,128)S(1)}, f32[5,56,128]{2,1,0:T(8,128)S(1)}) custom-call(s32[1]{0:T(128)S(6)} %copy.21.refs_0_, f32[5,16,32,128]{3,2,1,0:T(8,128)S(1)} %shard_map.121.refs_5_.refs_1_, ...), custom_call_target="tpu_custom_call", output_to_operand_aliasing={{1}: (7, {}), {2}: (8, {}), {3}: (9, {})} | custom-call | flops 2750000128 | bytes 4218880 | tf_op jit(solution)/shard_map/pallas_call | solution.py:677
  23.7 0.7 %shard_map.129 = (f32[5,16,128]{2,1,0:T(8,128)S(1)}, f32[5,56,128]{2,1,0:T(8,128)S(1)}) custom-call(f32[5,32,128]{2,1,0:T(8,128)S(1)} %get-tuple-element.48.refs_0_, s32[2,16]{1,0:T(2,128)S(1)} %copy-done.3, f32[5,56,128]{2,1,0:T(8,128)S(1)} %get-tuple-element.49.refs_2_), custom_call_target="tpu_custom_call", output_to_operand_aliasing={{1}: (2, {})} | custom-call | flops 660000000 | bytes 368640 | tf_op jit(solution)/shard_map/pallas_call | solution.py:677
  24.4 1.6 %collective-permute-start.4 = (f32[5,56,128]{2,1,0:T(8,128)S(1)}, f32[5,56,128]{2,1,0:T(8,128)S(1)}, u32[]{:S(2)}, u32[]{:S(2)}) collective-permute-start(f32[5,56,128]{2,1,0:T(8,128)S(1)} %get-tuple-element.50), channel_id=1, source_target_pairs={{0,1},{1,0},{2,3},{3,2},{4,5},{5,4},{6,7},{7,6},{8,9},{9,8},{10,11... | collective-permute-start | bytes 430088 | tf_op jit(solution)/shard_map/ppermute | solution.py:721
  26.0 3.8 %collective-permute-start.7 = (f32[2,2,5,32,128]{4,3,2,1,0:T(8,128)S(1)}, f32[2,2,5,32,128]{4,3,2,1,0:T(8,128)S(1)}, u32[]{:S(2)}, u32[]{:S(2)}) collective-permute-start(f32[2,2,5,32,128]{4,3,2,1,0:T(8,128)S(1)} %get-tuple-element.55), channel_id=1, source_target_pairs={{0,30},{2,4},{4,2},{6,8},{8,6},{10,12},{12,10},{14,16},{16,14},{18... | collective-permute-start | bytes 983048 | tf_op jit(solution)/shard_map/ppermute | solution.py:857
  29.9 0.1 collective-permute-start.8
  29.9 0.0 collective-permute-done.4.refs_4_.refs_3_
  29.9 2.0 %shard_map.131.refs_4_.refs_0_ = f32[5,16,32,128]{3,2,1,0:T(8,128)S(1)} custom-call(s32[1]{0:T(128)S(6)} %copy.21.refs_0_, f32[5,5]{1,0:T(8,128)S(1)} %copy-done.2, f32[5,16,32,128]{3,2,1,0:T(8,128)S(1)} %get-tuple-element.51.refs_2_, f32[5,16,32,128]{3,2,1,0:T(8,128)S(1)} %get-tuple-element.52.refs_3_, ...), custom_call_target="tpu_custom_call" | custom-call | flops 2750000128 | bytes 2621440 | tf_op jit(solution)/shard_map/pallas_call | solution.py:677
  32.0 2.0 %shard_map.132.refs_2_ = f32[5,16,32,128]{3,2,1,0:T(8,128)S(1)} custom-call(f32[5,5]{1,0:T(8,128)S(1)} %copy-done.2, f32[5,16,32,128]{3,2,1,0:T(8,128)S(1)} %get-tuple-element.47.refs_1_, f32[16,32,128]{2,1,0:T(8,128)S(1)} %get-tuple-element.35.refs_2_.refs_3_, f32[5,56,128]{2,1,0:T(8,128)S(1)} %collective-permute-done.4.refs_4_.refs_3_, ...), custom_call_target="tpu_custom_call" | custom-call | flops 2750000128 | bytes 2621440 | tf_op jit(solution)/shard_map/pallas_call | solution.py:677
  34.0 2.7 %collective-permute-done.8.refs_1_ = f32[11,32,128]{2,1,0:T(8,128)S(1)} collective-permute-done((f32[11,32,128]{2,1,0:T(8,128)S(1)}, f32[11,32,128]{2,1,0:T(8,128)S(1)}, u32[]{:S(2)}, u32[]{:S(2)}) %collective-permute-start.8) | collective-permute-done | bytes 180256 | tf_op jit(solution)/shard_map/ppermute | solution.py:717
  36.7 0.1 collective-permute-start.9
  36.8 0.1 shard_map.136
  36.9 2.4 %collective-permute-start.10 = (f32[5,16,128]{2,1,0:T(8,128)S(1)}, f32[5,16,128]{2,1,0:T(8,128)S(1)}, u32[]{:S(2)}, u32[]{:S(2)}) collective-permute-start(f32[5,16,128]{2,1,0:T(8,128)S(1)} %shard_map.136), channel_id=1, source_target_pairs={{0,16},{2,18},{4,20},{6,22},{8,24},{10,26},{12,28},{14,30},{16,0},... | collective-permute-start | bytes 122888 | tf_op jit(solution)/shard_map/ppermute | solution.py:717
  39.3 3.2 %shard_map.134 = (f32[5,32,16,128]{3,2,1,0:T(8,128)}, f32[8,128]{1,0:T(8,128)S(1)}) custom-call(s32[1]{0:T(128)S(6)} %copy.21.refs_0_, f32[5,5]{1,0:T(8,128)S(1)} %copy-done.2, f32[5,16,32,128]{3,2,1,0:T(8,128)S(1)} %shard_map.132.refs_2_, f32[16,32,128]{2,1,0:T(8,128)S(1)} %get-tuple-element.35.refs_2_.refs_3_, ...), custom_call_target="tpu_custom_call" | custom-call | flops 3300000000 | bytes 2629632 | tf_op jit(solution)/shard_map/pallas_call | solution.py:677
  42.6 0.3 collective-permute-start.11
  42.9 1.5 %shard_map.138 = (f32[5,32,16,128]{3,2,1,0:T(8,128)}, f32[2,5,16,64]{3,2,1,0:T(8,128)}) custom-call(f32[5,16,32,128]{3,2,1,0:T(8,128)S(1)} %shard_map.131.refs_4_.refs_0_, f32[2,2,5,32,128]{4,3,2,1,0:T(8,128)S(1)} %collective-permute-done.6.refs_4_.refs_1_, f32[2,2,5,32,128]{4,3,2,1,0:T(8,128)S(1)} %collective-permute-done.7.refs_5_.refs_2_, ...), custom_call_target="tpu_custom_call" | custom-call | flops 2750000128 | bytes 2703360 | tf_op jit(solution)/shard_map/pallas_call | solution.py:677
  44.4 0.6 %shard_map.139 = f32[2,5,8,128]{3,2,1,0:T(8,128)} custom-call(f32[5,8,128]{2,1,0:T(8,128)S(1)} %get-tuple-element.60.refs_5_.refs_0_, f32[5,8,128]{2,1,0:T(8,128)S(1)} %collective-permute-done.11.refs_1_), custom_call_target="tpu_custom_call" | custom-call | flops 110000000 | bytes 81920 | tf_op jit(solution)/shard_map/pallas_call | solution.py:677
  (22 shorter events, 0.2 us)
Async XLA Ops:
  1.3 10.9 %copy-start.2 = (f32[5,5]{1,0:T(8,128)S(1)}, f32[5,5]{1,0:T(8,128)}, u32[]{:S(2)}) copy-start(f32[5,5]{1,0:T(8,128)} %refs_1_.13) | copy-start | bytes 304
  4.5 9.6 %collective-permute-start.2 = (f32[5,56,128]{2,1,0:T(8,128)S(1)}, f32[5,56,128]{2,1,0:T(8,128)S(1)}, u32[]{:S(2)}, u32[]{:S(2)}) collective-permute-start(f32[5,56,128]{2,1,0:T(8,128)S(1)} %get-tuple-element.38), channel_id=1, source_target_pairs={{0,1},{1,0},{2,3},{3,2},{4,5},{5,4},{6,7},{7,6},{8,9},{9,8},{10,11... | collective-permute-start | bytes 430088 | tf_op jit(solution)/shard_map/ppermute | solution.py:721
  7.5 10.4 %collective-permute-start = (f32[2,2,5,32,128]{4,3,2,1,0:T(8,128)S(1)}, f32[2,2,5,32,128]{4,3,2,1,0:T(8,128)S(1)}, u32[]{:S(2)}, u32[]{:S(2)}) collective-permute-start(f32[2,2,5,32,128]{4,3,2,1,0:T(8,128)S(1)} %get-tuple-element.36), channel_id=1, source_target_pairs={{0,2},{2,0},{4,6},{6,4},{8,10},{10,8},{12,14},{14,12},{16,18},{18,... | collective-permute-start | bytes 983048 | tf_op jit(solution)/shard_map/ppermute | solution.py:761
  7.5 10.5 %collective-permute-start.1 = (f32[2,2,5,32,128]{4,3,2,1,0:T(8,128)S(1)}, f32[2,2,5,32,128]{4,3,2,1,0:T(8,128)S(1)}, u32[]{:S(2)}, u32[]{:S(2)}) collective-permute-start(f32[2,2,5,32,128]{4,3,2,1,0:T(8,128)S(1)} %get-tuple-element.37), channel_id=1, source_target_pairs={{0,30},{2,4},{4,2},{6,8},{8,6},{10,12},{12,10},{14,16},{16,14},{18... | collective-permute-start | bytes 983048 | tf_op jit(solution)/shard_map/ppermute | solution.py:762
  12.1 1.9 %copy-start.1 = (f32[2,5,8,128]{3,2,1,0:T(8,128)S(1)}, f32[2,5,8,128]{3,2,1,0:T(8,128)}, u32[]{:S(2)}) copy-start(f32[2,5,8,128]{3,2,1,0:T(8,128)} %refs_0_.11) | copy-start | bytes 122884
  12.1 1.9 %copy-start.4 = (s32[2,128]{1,0:T(2,128)S(1)}, s32[2,128]{1,0:T(2,128)}, u32[]{:S(2)}) copy-start(s32[2,128]{1,0:T(2,128)} %refs_1_.15) | copy-start | bytes 3076
  12.1 2.2 %copy-start = (f32[2,5,64,16]{2,3,1,0:T(8,128)S(1)}, f32[2,5,64,16]{2,3,1,0:T(8,128)}, u32[]{:S(2)}) copy-start(f32[2,5,64,16]{2,3,1,0:T(8,128)} %param.14) | copy-start | bytes 122884
  12.1 2.2 %copy-start.3 = (s32[2,16]{1,0:T(2,128)S(1)}, s32[2,16]{1,0:T(2,128)}, u32[]{:S(2)}) copy-start(s32[2,16]{1,0:T(2,128)} %refs_1_.11) | copy-start | bytes 388
  14.2 6.7 %collective-permute-start.3 = (f32[6,32,128]{2,1,0:T(8,128)S(1)}, f32[6,32,128]{2,1,0:T(8,128)S(1)}, u32[]{:S(2)}, u32[]{:S(2)}) collective-permute-start(f32[6,32,128]{2,1,0:T(8,128)S(1)} %get-tuple-element.46), channel_id=1, source_target_pairs={{0,16},{2,18},{4,20},{6,22},{8,24},{10,26},{12,28},{14,30},{16,0},... | collective-permute-start | bytes 294920 | tf_op jit(solution)/shard_map/ppermute | solution.py:717
  20.9 8.9 %collective-permute-start.5 = (f32[11,32,128]{2,1,0:T(8,128)S(1)}, f32[11,32,128]{2,1,0:T(8,128)S(1)}, u32[]{:S(2)}, u32[]{:S(2)}) collective-permute-start(f32[11,32,128]{2,1,0:T(8,128)S(1)} %shard_map.127.refs_10_.refs_0_), channel_id=1, source_target_pairs={{0,4},{2,6},{4,0},{6,2},{8,12},{10,14},{12,8},{14,10},{16,20},{18,... | collective-permute-start | bytes 540680 | tf_op jit(solution)/shard_map/ppermute | solution.py:717
  24.4 5.5 %collective-permute-start.4 = (f32[5,56,128]{2,1,0:T(8,128)S(1)}, f32[5,56,128]{2,1,0:T(8,128)S(1)}, u32[]{:S(2)}, u32[]{:S(2)}) collective-permute-start(f32[5,56,128]{2,1,0:T(8,128)S(1)} %get-tuple-element.50), channel_id=1, source_target_pairs={{0,1},{1,0},{2,3},{3,2},{4,5},{5,4},{6,7},{7,6},{8,9},{9,8},{10,11... | collective-permute-start | bytes 430088 | tf_op jit(solution)/shard_map/ppermute | solution.py:721
  26.0 13.3 %collective-permute-start.6 = (f32[2,2,5,32,128]{4,3,2,1,0:T(8,128)S(1)}, f32[2,2,5,32,128]{4,3,2,1,0:T(8,128)S(1)}, u32[]{:S(2)}, u32[]{:S(2)}) collective-permute-start(f32[2,2,5,32,128]{4,3,2,1,0:T(8,128)S(1)} %get-tuple-element.54), channel_id=1, source_target_pairs={{0,2},{2,0},{4,6},{6,4},{8,10},{10,8},{12,14},{14,12},{16,18},{18,... | collective-permute-start | bytes 983048 | tf_op jit(solution)/shard_map/ppermute | solution.py:856
  26.0 13.3 %collective-permute-start.7 = (f32[2,2,5,32,128]{4,3,2,1,0:T(8,128)S(1)}, f32[2,2,5,32,128]{4,3,2,1,0:T(8,128)S(1)}, u32[]{:S(2)}, u32[]{:S(2)}) collective-permute-start(f32[2,2,5,32,128]{4,3,2,1,0:T(8,128)S(1)} %get-tuple-element.55), channel_id=1, source_target_pairs={{0,30},{2,4},{4,2},{6,8},{8,6},{10,12},{12,10},{14,16},{16,14},{18... | collective-permute-start | bytes 983048 | tf_op jit(solution)/shard_map/ppermute | solution.py:857
  29.9 6.9 %collective-permute-start.8 = (f32[11,32,128]{2,1,0:T(8,128)S(1)}, f32[11,32,128]{2,1,0:T(8,128)S(1)}, u32[]{:S(2)}, u32[]{:S(2)}) collective-permute-start(f32[11,32,128]{2,1,0:T(8,128)S(1)} %shard_map.130.refs_5_.refs_0_), channel_id=1, source_target_pairs={{0,8},{2,10},{4,12},{6,14},{8,0},{10,2},{12,4},{14,6},{16,24},{18,... | collective-permute-start | bytes 540680 | tf_op jit(solution)/shard_map/ppermute | solution.py:717
  36.7 2.6 %collective-permute-start.9 = (f32[6,32,128]{2,1,0:T(8,128)S(1)}, f32[6,32,128]{2,1,0:T(8,128)S(1)}, u32[]{:S(2)}, u32[]{:S(2)}) collective-permute-start(f32[6,32,128]{2,1,0:T(8,128)S(1)} %get-tuple-element.56.refs_7_), channel_id=1, source_target_pairs={{0,2},{2,0},{4,6},{6,4},{8,10},{10,8},{12,14},{14,12},{16,18},{18,... | collective-permute-start | bytes 294920 | tf_op jit(solution)/shard_map/ppermute | solution.py:717
  36.9 5.7 %collective-permute-start.10 = (f32[5,16,128]{2,1,0:T(8,128)S(1)}, f32[5,16,128]{2,1,0:T(8,128)S(1)}, u32[]{:S(2)}, u32[]{:S(2)}) collective-permute-start(f32[5,16,128]{2,1,0:T(8,128)S(1)} %shard_map.136), channel_id=1, source_target_pairs={{0,16},{2,18},{4,20},{6,22},{8,24},{10,26},{12,28},{14,30},{16,0},... | collective-permute-start | bytes 122888 | tf_op jit(solution)/shard_map/ppermute | solution.py:717
  42.6 1.8 %collective-permute-start.11 = (f32[5,8,128]{2,1,0:T(8,128)S(1)}, f32[5,8,128]{2,1,0:T(8,128)S(1)}, u32[]{:S(2)}, u32[]{:S(2)}) collective-permute-start(f32[5,8,128]{2,1,0:T(8,128)S(1)} %get-tuple-element.62), channel_id=1, source_target_pairs={{0,2},{2,0},{4,6},{6,4},{8,10},{10,8},{12,14},{14,12},{16,18},{18,... | collective-permute-start | bytes 61448 | tf_op jit(solution)/shard_map/ppermute | solution.py:717

commit v6 on v5

--- a/solution.py
+++ b/solution.py
@@ -450,7 +450,8 @@
     lax.fori_loop(0, g.tiles, tile_step, 0)
 
 
-def adjoint_last_kernel(g, inside, fa, fb, fy, gsn_own, out, gsn):
+def adjoint_last_kernel(g, inside, fa, fb, fy, gsn_own, out_far, gsn, out, sems):
+    pairs = ((out, out_far),)
     out2 = out.reshape(g.F * g.K * g.X, g.Y)
     beyond = Beyond(g, 1, fa, fb)
 
@@ -460,6 +461,8 @@
             for x in range(g.X):
                 value = plus(inside[f, x, rows, :], beyond.columns(f, x, rows))
                 strided(out2, g, f, tile, x)[...] = value
+        for copy in level_copies(g, pairs, sems, tile):
+            copy.start()
         return carry
 
     lax.fori_loop(0, g.tiles, tile_step, 0)
@@ -471,10 +474,13 @@
             gsn[1 - here, f] = fy[f, g.K : g.K + g.X, :span]
     else:
         gsn[...] = jnp.zeros(gsn.shape, f32)
+    for tile in range(g.tiles):
+        for copy in level_copies(g, pairs, sems, tile):
+            copy.wait()
 
 
 def forward_last_kernel(
-    g, relax, mix, inside, dt, fa, fb, sides, kept, swapped, out, mark, rx, lx
+    g, relax, mix, inside, dt, fa, fb, sides, kept, swapped, out_far, mark, rx, lx, out, sems
 ):
     width = relax[0]
     mark[...] = jnp.zeros((8, 128), f32)
@@ -488,6 +494,7 @@
     table = mix_table(mix, False)
     beyond = Beyond(g, 0, fa, fb)
     edge, valid = border(), valid_lanes(g)
+    pairs = ((out, out_far),)
     out2 = out.reshape(g.F * g.K * g.X, g.Y)
 
     def tile_step(tile, carry):
@@ -517,9 +524,14 @@
                     stepped = stepped + d * beside
                 done = open_xy * stepped + slope_x * bound[f] + sides[f, x, rows, :]
                 strided(out2, g, f, tile, x)[...] = done
+        for copy in level_copies(g, pairs, sems, tile):
+            copy.start()
         return carry
 
     lax.fori_loop(0, g.tiles, tile_step, 0)
+    for tile in range(g.tiles):
+        for copy in level_copies(g, pairs, sems, tile):
+            copy.wait()
 
 
 def side_sums_kernel(g, dsn, tsn, my_in, gsn, my, wide):
@@ -665,7 +677,7 @@
         out[1 - odd, f] = other[f]
 
 
-def call(kernel, outs, scratch, ins, time, aliases=None, after=()):
+def call(kernel, outs, scratch, ins, time, aliases=None, after=(), far=False):
     count = len(ins)
     ins = ins + [("a", value) for value in after]
 
@@ -678,7 +690,7 @@
         run,
         out_shape=out_shape,
         in_specs=[places[where] for where, _ in ins],
-        out_specs=[places["v"]] * len(outs),
+        out_specs=[places["h" if far and i == 0 else "v"] for i in range(len(outs))],
         scratch_shapes=[pltpu.VMEM(s, f32) if isinstance(s, tuple) else s for s in scratch],
         input_output_aliases=aliases or {},
         compiler_params=pltpu.CompilerParams(vmem_limit_bytes=24 * 1024 * 1024),
@@ -707,6 +719,7 @@
     lane_shape = (F, g.tall, 128)
     edge_shape = (F, K, 128)
     ramps = (X, 8, 128)
+    out_sems = pltpu.SemaphoreType.DMA((1, g.tiles))
     band = pltpu.VMEM((256, 128), jnp.bfloat16)
     laps = (F, X, 8, 128)
 
@@ -896,7 +909,7 @@
     child_final, mark = call(
         bind(forward_last_kernel),
         [child_state.shape, (8, 128)],
-        [(X + 4, 8, 128), ramps],
+        [(X + 4, 8, 128), ramps, child_state.shape, out_sems],
         [
             ("s", relax_width),
             ("s", field_mix),
@@ -909,6 +922,7 @@
             ("v", other_bounds),
         ],
         3,
+        far=True,
     )
     (own,) = call(
         bind(spread_kernel, 0),
@@ -925,10 +939,11 @@
     grad_state, grad_sn = call(
         bind(adjoint_last_kernel),
         [child_state.shape, sn_turned.shape],
-        [],
+        [child_state.shape, out_sems],
         [("v", inside_a), ("v", fa), ("v", fb), ("v", fy), ("v", gsn_own)],
         2.5,
         after=[kept],
+        far=True,
     )
     (grad_we,) = call(
         bind(assemble_kernel),

time: 45.2 us -> 45.3 us (level)
  no operation moved by 1% of the time
where the time goes in v6:
time: 45.3 us; the launch traced here: 45.1 us
  Pallas kernels  23.3 us (51%)
  starting transfers between devices  17.2 us (38%)
  waiting for transfers between devices  3.11 us (7%)
  between operations  1.51 us (3%)
    pallas_call x20, Pallas kernels, call(): pl.pallas_call(run, out_shape=out_shape, in_specs=[places[where] for wher...  23.3 us
    ppermute x2, starting transfers between devices, body(): fb = lax.ppermute(mb, 'gx', odds)  8.5 us
    ppermute x2, starting transfers between devices, to_y(): return lax.ppermute(message, 'gy', [(0, 1), (1, 0)])  4.56 us
    ppermute x6, starting transfers between devices, swapped(): return lax.ppermute(values, 'gx', [(i, i ^ distance) for i in range(nx)])  4.1 us
    ppermute x6, waiting for transfers between devices, swapped(): return lax.ppermute(values, 'gx', [(i, i ^ distance) for i in range(nx)])  3.1 us
  transfers between devices with their start and end apart: 12, of which 2 were waited for; matrix products, arithmetic and copies ran while one was open for 0% of the time, Pallas kernels for 43%

profile of v6, /device:TPU:0, one launch (start us, length us, event | category | flops | bytes accessed | tf_op | source)
XLA Modules:
  0.0 45.1 jit_solution(6305540002902547939)
XLA Ops:
  1.3 3.2 %shard_map.120 = (f32[5,16,32,128]{3,2,1,0:T(8,128)S(1)}, f32[5,16,32,128]{3,2,1,0:T(8,128)S(1)}, f32[16,32,128]{2,1,0:T(8,128)S(1)}, f32[5,16,32,128]{3,2,1,0:T...) custom-call(s32[1]{0:T(128)S(6)} %copy.21.refs_0_, ...), custom_call_target="tpu_custom_call" | custom-call | flops 3300000000 | bytes 9986048 | tf_op jit(solution)/shard_map/pallas_call | solution.py:689
  4.5 3.0 %collective-permute-start.2 = (f32[5,56,128]{2,1,0:T(8,128)S(1)}, f32[5,56,128]{2,1,0:T(8,128)S(1)}, u32[]{:S(2)}, u32[]{:S(2)}) collective-permute-start(f32[5,56,128]{2,1,0:T(8,128)S(1)} %get-tuple-element.38), channel_id=1, source_target_pairs={{0,1},{1,0},{2,3},{3,2},{4,5},{5,4},{6,7},{7,6},{8,9},{9,8},{10,11... | collective-permute-start | bytes 430088 | tf_op jit(solution)/shard_map/ppermute | solution.py:734
  7.5 4.7 %collective-permute-start.1 = (f32[2,2,5,32,128]{4,3,2,1,0:T(8,128)S(1)}, f32[2,2,5,32,128]{4,3,2,1,0:T(8,128)S(1)}, u32[]{:S(2)}, u32[]{:S(2)}) collective-permute-start(f32[2,2,5,32,128]{4,3,2,1,0:T(8,128)S(1)} %get-tuple-element.37), channel_id=1, source_target_pairs={{0,30},{2,4},{4,2},{6,8},{8,6},{10,12},{12,10},{14,16},{16,14},{18... | collective-permute-start | bytes 983048 | tf_op jit(solution)/shard_map/ppermute | solution.py:775
  12.1 0.0 copy-start.3
  12.2 1.9 %shard_map.121.refs_5_.refs_1_ = f32[5,16,32,128]{3,2,1,0:T(8,128)S(1)} custom-call(f32[5,5]{1,0:T(8,128)S(1)} %copy-done.2, f32[5,16,32,128]{3,2,1,0:T(8,128)S(1)} %get-tuple-element.34.refs_1_, f32[16,32,128]{2,1,0:T(8,128)S(1)} %get-tuple-element.35.refs_2_.refs_3_), custom_call_target="tpu_custom_call" | custom-call | flops 2750000128 | bytes 2621440 | tf_op jit(solution)/shard_map/pallas_call | solution.py:689
  14.0 0.0 collective-permute-done.2.refs_1_.refs_4_.refs_2_.refs_5_
  14.1 0.1 shard_map.125
  14.2 0.1 collective-permute-start.3
  14.3 0.7 %shard_map.122.refs_1_ = f32[5,32,128]{2,1,0:T(8,128)S(1)} custom-call(f32[2,5,16,64]{3,2,1,0:T(8,128)S(1)} %bitcast.3, f32[5,56,128]{2,1,0:T(8,128)S(1)} %collective-permute-done.2.refs_1_.refs_4_.refs_2_.refs_5_, s32[2,16]{1,0:T(2,128)S(1)} %copy-done.3), custom_call_target="tpu_custom_call" | custom-call | flops 770000000 | bytes 163840 | tf_op jit(solution)/shard_map/pallas_call | solution.py:689
  15.0 0.9 %shard_map.123.refs_7_.refs_6_ = f32[5,16,32,128]{3,2,1,0:T(8,128)S(1)} custom-call(s32[1]{0:T(128)S(6)} %copy.21.refs_0_, f32[5,32,128]{2,1,0:T(8,128)S(1)} %shard_map.122.refs_1_), custom_call_target="tpu_custom_call" | custom-call | flops 770000000 | bytes 2621440 | tf_op jit(solution)/shard_map/pallas_call | solution.py:689
  15.9 2.0 %shard_map.124.refs_1_ = f32[5,16,32,128]{3,2,1,0:T(8,128)S(1)} custom-call(s32[1]{0:T(128)S(6)} %copy.21.refs_0_, f32[5,5]{1,0:T(8,128)S(1)} %copy-done.2, f32[5,16,32,128]{3,2,1,0:T(8,128)S(1)} %get-tuple-element.39.refs_2_, f32[5,16,32,128]{3,2,1,0:T(8,128)S(1)} %get-tuple-element.40.refs_3_, ...), custom_call_target="tpu_custom_call" | custom-call | flops 2750000128 | bytes 2621440 | tf_op jit(solution)/shard_map/pallas_call | solution.py:689
  17.9 0.0 collective-permute-done.refs_4_.refs_3_
  17.9 2.6 %shard_map.126 = (f32[5,16,32,128]{3,2,1,0:T(8,128)S(1)}, f32[5,16,32,128]{3,2,1,0:T(8,128)S(1)}, f32[2,2,5,32,128]{4,3,2,1,0:T(8,128)S(1)}, f32[2,2,5,32,128]{4...) custom-call(s32[1]{0:T(128)S(6)} %copy.21.refs_0_, ...), custom_call_target="tpu_custom_call" | custom-call | flops 3300000000 | bytes 7168000 | tf_op jit(solution)/shard_map/pallas_call | solution.py:689
  20.5 0.4 collective-permute-done.3.refs_2_
  20.9 1.2 %collective-permute-start.5 = (f32[11,32,128]{2,1,0:T(8,128)S(1)}, f32[11,32,128]{2,1,0:T(8,128)S(1)}, u32[]{:S(2)}, u32[]{:S(2)}) collective-permute-start(f32[11,32,128]{2,1,0:T(8,128)S(1)} %shard_map.127.refs_10_.refs_0_), channel_id=1, source_target_pairs={{0,4},{2,6},{4,0},{6,2},{8,12},{10,14},{12,8},{14,10},{16,20},{18,... | collective-permute-start | bytes 540680 | tf_op jit(solution)/shard_map/ppermute | solution.py:730
  22.1 1.6 %shard_map.128 = (f32[5,16,32,128]{3,2,1,0:T(8,128)S(1)}, f32[2,2,5,32,128]{4,3,2,1,0:T(8,128)S(1)}, f32[2,2,5,32,128]{4,3,2,1,0:T(8,128)S(1)}, f32[5,56,128]{2,1,0:T(8,128)S(1)}) custom-call(s32[1]{0:T(128)S(6)} %copy.21.refs_0_, f32[5,16,32,128]{3,2,1,0:T(8,128)S(1)} %shard_map.121.refs_5_.refs_1_, ...), custom_call_target="tpu_custom_call", output_to_operand_aliasing={{1}: (7, {}), {2}: (8, {}), {3}: (9, {})} | custom-call | flops 2750000128 | bytes 4218880 | tf_op jit(solution)/shard_map/pallas_call | solution.py:689
  23.7 0.7 %shard_map.129 = (f32[5,16,128]{2,1,0:T(8,128)S(1)}, f32[5,56,128]{2,1,0:T(8,128)S(1)}) custom-call(f32[5,32,128]{2,1,0:T(8,128)S(1)} %get-tuple-element.48.refs_0_, s32[2,16]{1,0:T(2,128)S(1)} %copy-done.3, f32[5,56,128]{2,1,0:T(8,128)S(1)} %get-tuple-element.49.refs_2_), custom_call_target="tpu_custom_call", output_to_operand_aliasing={{1}: (2, {})} | custom-call | flops 660000000 | bytes 368640 | tf_op jit(solution)/shard_map/pallas_call | solution.py:689
  24.4 1.6 %collective-permute-start.4 = (f32[5,56,128]{2,1,0:T(8,128)S(1)}, f32[5,56,128]{2,1,0:T(8,128)S(1)}, u32[]{:S(2)}, u32[]{:S(2)}) collective-permute-start(f32[5,56,128]{2,1,0:T(8,128)S(1)} %get-tuple-element.50), channel_id=1, source_target_pairs={{0,1},{1,0},{2,3},{3,2},{4,5},{5,4},{6,7},{7,6},{8,9},{9,8},{10,11... | collective-permute-start | bytes 430088 | tf_op jit(solution)/shard_map/ppermute | solution.py:734
  26.0 0.0 collective-permute-start.6
  26.0 3.8 %collective-permute-start.7 = (f32[2,2,5,32,128]{4,3,2,1,0:T(8,128)S(1)}, f32[2,2,5,32,128]{4,3,2,1,0:T(8,128)S(1)}, u32[]{:S(2)}, u32[]{:S(2)}) collective-permute-start(f32[2,2,5,32,128]{4,3,2,1,0:T(8,128)S(1)} %get-tuple-element.55), channel_id=1, source_target_pairs={{0,30},{2,4},{4,2},{6,8},{8,6},{10,12},{12,10},{14,16},{16,14},{18... | collective-permute-start | bytes 983048 | tf_op jit(solution)/shard_map/ppermute | solution.py:870
  29.9 0.1 collective-permute-start.8
  29.9 2.0 %shard_map.131.refs_4_.refs_0_ = f32[5,16,32,128]{3,2,1,0:T(8,128)S(1)} custom-call(s32[1]{0:T(128)S(6)} %copy.21.refs_0_, f32[5,5]{1,0:T(8,128)S(1)} %copy-done.2, f32[5,16,32,128]{3,2,1,0:T(8,128)S(1)} %get-tuple-element.51.refs_2_, f32[5,16,32,128]{3,2,1,0:T(8,128)S(1)} %get-tuple-element.52.refs_3_, ...), custom_call_target="tpu_custom_call" | custom-call | flops 2750000128 | bytes 2621440 | tf_op jit(solution)/shard_map/pallas_call | solution.py:689
  32.0 2.0 %shard_map.132.refs_2_ = f32[5,16,32,128]{3,2,1,0:T(8,128)S(1)} custom-call(f32[5,5]{1,0:T(8,128)S(1)} %copy-done.2, f32[5,16,32,128]{3,2,1,0:T(8,128)S(1)} %get-tuple-element.47.refs_1_, f32[16,32,128]{2,1,0:T(8,128)S(1)} %get-tuple-element.35.refs_2_.refs_3_, f32[5,56,128]{2,1,0:T(8,128)S(1)} %collective-permute-done.4.refs_4_.refs_3_, ...), custom_call_target="tpu_custom_call" | custom-call | flops 2750000128 | bytes 2621440 | tf_op jit(solution)/shard_map/pallas_call | solution.py:689
  34.0 2.7 %collective-permute-done.8.refs_1_ = f32[11,32,128]{2,1,0:T(8,128)S(1)} collective-permute-done((f32[11,32,128]{2,1,0:T(8,128)S(1)}, f32[11,32,128]{2,1,0:T(8,128)S(1)}, u32[]{:S(2)}, u32[]{:S(2)}) %collective-permute-start.8) | collective-permute-done | bytes 180256 | tf_op jit(solution)/shard_map/ppermute | solution.py:730
  36.7 0.1 collective-permute-start.9
  36.8 0.1 shard_map.136
  36.9 2.4 %collective-permute-start.10 = (f32[5,16,128]{2,1,0:T(8,128)S(1)}, f32[5,16,128]{2,1,0:T(8,128)S(1)}, u32[]{:S(2)}, u32[]{:S(2)}) collective-permute-start(f32[5,16,128]{2,1,0:T(8,128)S(1)} %shard_map.136), channel_id=1, source_target_pairs={{0,16},{2,18},{4,20},{6,22},{8,24},{10,26},{12,28},{14,30},{16,0},... | collective-permute-start | bytes 122888 | tf_op jit(solution)/shard_map/ppermute | solution.py:730
  39.3 2.9 %shard_map.134 = (f32[5,32,16,128]{3,2,1,0:T(8,128)}, f32[8,128]{1,0:T(8,128)S(1)}) custom-call(s32[1]{0:T(128)S(6)} %copy.21.refs_0_, f32[5,5]{1,0:T(8,128)S(1)} %copy-done.2, f32[5,16,32,128]{3,2,1,0:T(8,128)S(1)} %shard_map.132.refs_2_, f32[16,32,128]{2,1,0:T(8,128)S(1)} %get-tuple-element.35.refs_2_.refs_3_, ...), custom_call_target="tpu_custom_call" | custom-call | flops 3300000000 | bytes 2629632 | tf_op jit(solution)/shard_map/pallas_call | solution.py:689
  42.2 0.1 shard_map.135.refs_0_
  42.3 0.3 collective-permute-start.11
  42.6 1.9 %shard_map.138 = (f32[5,32,16,128]{3,2,1,0:T(8,128)}, f32[2,5,16,64]{3,2,1,0:T(8,128)}) custom-call(f32[5,16,32,128]{3,2,1,0:T(8,128)S(1)} %shard_map.131.refs_4_.refs_0_, f32[2,2,5,32,128]{4,3,2,1,0:T(8,128)S(1)} %collective-permute-done.6.refs_4_.refs_1_, f32[2,2,5,32,128]{4,3,2,1,0:T(8,128)S(1)} %collective-permute-done.7.refs_5_.refs_2_, ...), custom_call_target="tpu_custom_call" | custom-call | flops 2750000128 | bytes 2703360 | tf_op jit(solution)/shard_map/pallas_call | solution.py:689
  44.5 0.6 %shard_map.139 = f32[2,5,8,128]{3,2,1,0:T(8,128)} custom-call(f32[5,8,128]{2,1,0:T(8,128)S(1)} %get-tuple-element.60.refs_5_.refs_0_, f32[5,8,128]{2,1,0:T(8,128)S(1)} %collective-permute-done.11.refs_1_), custom_call_target="tpu_custom_call" | custom-call | flops 110000000 | bytes 81920 | tf_op jit(solution)/shard_map/pallas_call | solution.py:689
  (22 shorter events, 0.1 us)
Async XLA Ops:
  1.3 10.9 %copy-start.2 = (f32[5,5]{1,0:T(8,128)S(1)}, f32[5,5]{1,0:T(8,128)}, u32[]{:S(2)}) copy-start(f32[5,5]{1,0:T(8,128)} %refs_1_.13) | copy-start | bytes 304
  4.5 9.6 %collective-permute-start.2 = (f32[5,56,128]{2,1,0:T(8,128)S(1)}, f32[5,56,128]{2,1,0:T(8,128)S(1)}, u32[]{:S(2)}, u32[]{:S(2)}) collective-permute-start(f32[5,56,128]{2,1,0:T(8,128)S(1)} %get-tuple-element.38), channel_id=1, source_target_pairs={{0,1},{1,0},{2,3},{3,2},{4,5},{5,4},{6,7},{7,6},{8,9},{9,8},{10,11... | collective-permute-start | bytes 430088 | tf_op jit(solution)/shard_map/ppermute | solution.py:734
  7.5 10.4 %collective-permute-start = (f32[2,2,5,32,128]{4,3,2,1,0:T(8,128)S(1)}, f32[2,2,5,32,128]{4,3,2,1,0:T(8,128)S(1)}, u32[]{:S(2)}, u32[]{:S(2)}) collective-permute-start(f32[2,2,5,32,128]{4,3,2,1,0:T(8,128)S(1)} %get-tuple-element.36), channel_id=1, source_target_pairs={{0,2},{2,0},{4,6},{6,4},{8,10},{10,8},{12,14},{14,12},{16,18},{18,... | collective-permute-start | bytes 983048 | tf_op jit(solution)/shard_map/ppermute | solution.py:774
  7.5 10.5 %collective-permute-start.1 = (f32[2,2,5,32,128]{4,3,2,1,0:T(8,128)S(1)}, f32[2,2,5,32,128]{4,3,2,1,0:T(8,128)S(1)}, u32[]{:S(2)}, u32[]{:S(2)}) collective-permute-start(f32[2,2,5,32,128]{4,3,2,1,0:T(8,128)S(1)} %get-tuple-element.37), channel_id=1, source_target_pairs={{0,30},{2,4},{4,2},{6,8},{8,6},{10,12},{12,10},{14,16},{16,14},{18... | collective-permute-start | bytes 983048 | tf_op jit(solution)/shard_map/ppermute | solution.py:775
  12.1 1.9 %copy-start.1 = (f32[2,5,8,128]{3,2,1,0:T(8,128)S(1)}, f32[2,5,8,128]{3,2,1,0:T(8,128)}, u32[]{:S(2)}) copy-start(f32[2,5,8,128]{3,2,1,0:T(8,128)} %refs_0_.11) | copy-start | bytes 122884
  12.1 1.9 %copy-start.4 = (s32[2,128]{1,0:T(2,128)S(1)}, s32[2,128]{1,0:T(2,128)}, u32[]{:S(2)}) copy-start(s32[2,128]{1,0:T(2,128)} %refs_1_.15) | copy-start | bytes 3076
  12.1 2.2 %copy-start = (f32[2,5,64,16]{2,3,1,0:T(8,128)S(1)}, f32[2,5,64,16]{2,3,1,0:T(8,128)}, u32[]{:S(2)}) copy-start(f32[2,5,64,16]{2,3,1,0:T(8,128)} %param.14) | copy-start | bytes 122884
  12.1 2.2 %copy-start.3 = (s32[2,16]{1,0:T(2,128)S(1)}, s32[2,16]{1,0:T(2,128)}, u32[]{:S(2)}) copy-start(s32[2,16]{1,0:T(2,128)} %refs_1_.11) | copy-start | bytes 388
  14.2 6.7 %collective-permute-start.3 = (f32[6,32,128]{2,1,0:T(8,128)S(1)}, f32[6,32,128]{2,1,0:T(8,128)S(1)}, u32[]{:S(2)}, u32[]{:S(2)}) collective-permute-start(f32[6,32,128]{2,1,0:T(8,128)S(1)} %get-tuple-element.46), channel_id=1, source_target_pairs={{0,16},{2,18},{4,20},{6,22},{8,24},{10,26},{12,28},{14,30},{16,0},... | collective-permute-start | bytes 294920 | tf_op jit(solution)/shard_map/ppermute | solution.py:730
  20.9 8.9 %collective-permute-start.5 = (f32[11,32,128]{2,1,0:T(8,128)S(1)}, f32[11,32,128]{2,1,0:T(8,128)S(1)}, u32[]{:S(2)}, u32[]{:S(2)}) collective-permute-start(f32[11,32,128]{2,1,0:T(8,128)S(1)} %shard_map.127.refs_10_.refs_0_), channel_id=1, source_target_pairs={{0,4},{2,6},{4,0},{6,2},{8,12},{10,14},{12,8},{14,10},{16,20},{18,... | collective-permute-start | bytes 540680 | tf_op jit(solution)/shard_map/ppermute | solution.py:730
  24.4 5.5 %collective-permute-start.4 = (f32[5,56,128]{2,1,0:T(8,128)S(1)}, f32[5,56,128]{2,1,0:T(8,128)S(1)}, u32[]{:S(2)}, u32[]{:S(2)}) collective-permute-start(f32[5,56,128]{2,1,0:T(8,128)S(1)} %get-tuple-element.50), channel_id=1, source_target_pairs={{0,1},{1,0},{2,3},{3,2},{4,5},{5,4},{6,7},{7,6},{8,9},{9,8},{10,11... | collective-permute-start | bytes 430088 | tf_op jit(solution)/shard_map/ppermute | solution.py:734
  26.0 13.3 %collective-permute-start.6 = (f32[2,2,5,32,128]{4,3,2,1,0:T(8,128)S(1)}, f32[2,2,5,32,128]{4,3,2,1,0:T(8,128)S(1)}, u32[]{:S(2)}, u32[]{:S(2)}) collective-permute-start(f32[2,2,5,32,128]{4,3,2,1,0:T(8,128)S(1)} %get-tuple-element.54), channel_id=1, source_target_pairs={{0,2},{2,0},{4,6},{6,4},{8,10},{10,8},{12,14},{14,12},{16,18},{18,... | collective-permute-start | bytes 983048 | tf_op jit(solution)/shard_map/ppermute | solution.py:869
  26.0 13.3 %collective-permute-start.7 = (f32[2,2,5,32,128]{4,3,2,1,0:T(8,128)S(1)}, f32[2,2,5,32,128]{4,3,2,1,0:T(8,128)S(1)}, u32[]{:S(2)}, u32[]{:S(2)}) collective-permute-start(f32[2,2,5,32,128]{4,3,2,1,0:T(8,128)S(1)} %get-tuple-element.55), channel_id=1, source_target_pairs={{0,30},{2,4},{4,2},{6,8},{8,6},{10,12},{12,10},{14,16},{16,14},{18... | collective-permute-start | bytes 983048 | tf_op jit(solution)/shard_map/ppermute | solution.py:870
  29.9 6.9 %collective-permute-start.8 = (f32[11,32,128]{2,1,0:T(8,128)S(1)}, f32[11,32,128]{2,1,0:T(8,128)S(1)}, u32[]{:S(2)}, u32[]{:S(2)}) collective-permute-start(f32[11,32,128]{2,1,0:T(8,128)S(1)} %shard_map.130.refs_5_.refs_0_), channel_id=1, source_target_pairs={{0,8},{2,10},{4,12},{6,14},{8,0},{10,2},{12,4},{14,6},{16,24},{18,... | collective-permute-start | bytes 540680 | tf_op jit(solution)/shard_map/ppermute | solution.py:730
  36.7 2.6 %collective-permute-start.9 = (f32[6,32,128]{2,1,0:T(8,128)S(1)}, f32[6,32,128]{2,1,0:T(8,128)S(1)}, u32[]{:S(2)}, u32[]{:S(2)}) collective-permute-start(f32[6,32,128]{2,1,0:T(8,128)S(1)} %get-tuple-element.56.refs_7_), channel_id=1, source_target_pairs={{0,2},{2,0},{4,6},{6,4},{8,10},{10,8},{12,14},{14,12},{16,18},{18,... | collective-permute-start | bytes 294920 | tf_op jit(solution)/shard_map/ppermute | solution.py:730
  36.9 5.4 %collective-permute-start.10 = (f32[5,16,128]{2,1,0:T(8,128)S(1)}, f32[5,16,128]{2,1,0:T(8,128)S(1)}, u32[]{:S(2)}, u32[]{:S(2)}) collective-permute-start(f32[5,16,128]{2,1,0:T(8,128)S(1)} %shard_map.136), channel_id=1, source_target_pairs={{0,16},{2,18},{4,20},{6,22},{8,24},{10,26},{12,28},{14,30},{16,0},... | collective-permute-start | bytes 122888 | tf_op jit(solution)/shard_map/ppermute | solution.py:730
  42.3 2.1 %collective-permute-start.11 = (f32[5,8,128]{2,1,0:T(8,128)S(1)}, f32[5,8,128]{2,1,0:T(8,128)S(1)}, u32[]{:S(2)}, u32[]{:S(2)}) collective-permute-start(f32[5,8,128]{2,1,0:T(8,128)S(1)} %get-tuple-element.62), channel_id=1, source_target_pairs={{0,2},{2,0},{4,6},{6,4},{8,10},{10,8},{12,14},{14,12},{16,18},{18,... | collective-permute-start | bytes 61448 | tf_op jit(solution)/shard_map/ppermute | solution.py:730
